TPU v7x, 32 devices: a whole 2x2x4 slice. The times are simulated.
32 devices in a mesh: row: 4 (over y, core), col: 8 (over z, x).
Axes of the slice: x: 2, y: 2, z: 4, core: 2. Of those that a mesh axis runs over, the one named last changes fastest.
Arguments:
- traces: float32 [64, 4096], P(('row', 'col')), may hold values from -6 to 6
- offsets: int32 [64, 8], P(('row', 'col')), may hold values from 0 to 3072, as said below
- band_lo: int32 [64], P(('row', 'col')), may hold values from 0 to 63
- band_hi: int32 [64], P(('row', 'col')), may hold values from 192 to 256
- live: int32 [64], P(('row', 'col')), may hold values 0 or 1
Outputs:
- correlations: bfloat16 [64, 8, 4, 2, 512], P('row', 'col')
Inputs may be any that keep to these rules, and one draw needn't show every extreme that they name: `offsets`: every offset is a multiple of 256.
All inputs are finite; a program needn't handle non-finite values. No bound on the sum of `live` on one device may be relied on, other than what follows from the above.
Results may differ from a plain program's by a relative error of at most 0.0052.
Values may be sent and summed in bfloat16 or wider, within the bound.
No kernel may reach another device: no remote copies, remote signals or barrier semaphores. Data moves between devices by JAX's collectives and lax.ppermute only.
A program may use at most 64 MiB of HBM per device.

v0:
```python
import math

import jax
import jax.numpy as jnp
from jax import lax
from jax.sharding import PartitionSpec as P

SEG = 8
SAMPLES = 1024
BINS = 256
LAGS = 512
TRACE = 4096


def transform_table():
    times = jnp.arange(SAMPLES, dtype=jnp.int32)
    freqs = jnp.arange(BINS, dtype=jnp.int32) + 1
    phase = jnp.mod(times[:, None] * freqs[None, :], SAMPLES).astype(jnp.float32) * (
        2.0 * math.pi / SAMPLES
    )
    taper = 0.5 - 0.5 * jnp.cos(times.astype(jnp.float32) * (2.0 * math.pi / SAMPLES))
    return jnp.concatenate([jnp.cos(phase), -jnp.sin(phase)], axis=1) * taper[:, None]


def lag_table():
    freqs = jnp.arange(BINS, dtype=jnp.int32) + 1
    shifts = jnp.arange(LAGS, dtype=jnp.int32) - LAGS // 2
    phase = jnp.mod(freqs[:, None] * shifts[None, :], SAMPLES).astype(jnp.float32) * (
        2.0 * math.pi / SAMPLES
    )
    return jnp.concatenate([jnp.cos(phase), -jnp.sin(phase)], axis=0) * (
        1.0 / math.sqrt(SEG * BINS)
    )


def cut_segments(traces, offsets):
    count = traces.shape[0]
    quarter = SAMPLES // 4
    block_count = TRACE // quarter
    blocks = traces.reshape(count, 1, block_count, quarter)
    first_block = offsets // quarter
    segment = jnp.zeros((count, SEG, 4, quarter), jnp.float32)
    for place in range(block_count - 3):
        picked = (first_block == place)[:, :, None, None]
        segment = jnp.where(picked, blocks[:, :, place : place + 4, :], segment)
    return segment.reshape(count * SEG, SAMPLES)


def whiten(traces, offsets, band_lo, band_hi, live):
    count = traces.shape[0]
    flat = cut_segments(traces, offsets)
    spec = jnp.dot(flat, transform_table(), precision=lax.Precision.HIGHEST)
    spec_re = spec[:, :BINS]
    spec_im = spec[:, BINS:]
    amp = jnp.sqrt(spec_re * spec_re + spec_im * spec_im)
    padded = jnp.pad(amp, ((0, 0), (2, 2)))
    smooth = (
        padded[:, 0:BINS]
        + padded[:, 1 : BINS + 1]
        + padded[:, 2 : BINS + 2]
        + padded[:, 3 : BINS + 3]
        + padded[:, 4 : BINS + 4]
    ) / 5.0
    level = jnp.mean(amp, axis=1, keepdims=True)
    factor = 1.0 / (smooth + 0.1 * level + 1e-06)
    bins = jnp.arange(BINS, dtype=jnp.int32)
    inside = (
        (bins[None, :] >= band_lo[:, None])
        & (bins[None, :] < band_hi[:, None])
        & (live[:, None] == 1)
    )
    keep = inside.astype(jnp.float32)
    factor = factor.reshape(count, SEG, BINS) * keep[:, None, :]
    spec = spec.reshape(count, SEG, 2 * BINS)
    white = spec * jnp.concatenate([factor, factor], axis=2)
    return white.astype(jnp.bfloat16)


def correlate(first, second, table):
    first_re, first_im = (first[..., :BINS], first[..., BINS:])
    second_re, second_im = (second[..., :BINS], second[..., BINS:])
    count_i, count_j = (first.shape[0], second.shape[0])
    cross_re = jnp.zeros((count_i, count_j, BINS), jnp.float32)
    cross_im = jnp.zeros((count_i, count_j, BINS), jnp.float32)
    for seg_index in range(SEG):
        left_re = first_re[:, None, seg_index, :].astype(jnp.float32)
        left_im = first_im[:, None, seg_index, :].astype(jnp.float32)
        right_re = second_re[None, :, seg_index, :].astype(jnp.float32)
        right_im = second_im[None, :, seg_index, :].astype(jnp.float32)
        cross_re = cross_re + (left_re * right_re + left_im * right_im)
        cross_im = cross_im + (left_im * right_re - left_re * right_im)
    cross = jnp.concatenate([cross_re, cross_im], axis=2)
    corr = jnp.dot(
        cross.reshape(count_i * count_j, 2 * BINS), table, precision=lax.Precision.HIGHEST
    )
    return corr.astype(jnp.bfloat16).reshape(count_i, count_j, LAGS)


def body(traces, offsets, band_lo, band_hi, live):
    white = whiten(traces, offsets, band_lo, band_hi, live)
    table = lag_table()
    first_panel = lax.all_gather(white, "col", axis=0, tiled=True)
    stacked = correlate(first_panel, lax.all_gather(white, "row", axis=0, tiled=True), table)
    channel_count = white.shape[0]
    return stacked.reshape(stacked.shape[0], 1, lax.axis_size("row"), channel_count, LAGS)


def solution(mesh):
    in_specs = (
        P(("row", "col"), None),
        P(("row", "col"), None),
        P(("row", "col")),
        P(("row", "col")),
        P(("row", "col")),
    )
    out_specs = P("row", "col", None, None, None)
    return jax.shard_map(body, mesh=mesh, in_specs=in_specs, out_specs=out_specs, check_vma=False)
```

profile of v0, /device:TPU:0, one launch (start us, length us, event | category | flops | bytes accessed | tf_op | source)
XLA Modules:
  0.0 50.1 jit_solution(1294756092299155581)
XLA Ops:
  0.0 0.8 %copy.74 = f32[1,2,16,256]{3,2,1,0:T(8,128)S(1)} copy(f32[1,2,16,256]{3,1,2,0:T(2,128)} %bitcast.132) | data formatting | bytes 65536
  1.0 0.1 broadcast_in_dim.247
  1.1 0.1 broadcast_in_dim.252
  1.2 0.1 broadcast_in_dim.257
  1.3 0.1 broadcast_in_dim.262
  1.4 0.1 broadcast_in_dim.267
  1.5 0.1 broadcast_in_dim.272
  1.7 0.1 broadcast_in_dim.287
  1.8 0.1 broadcast_in_dim.292
  1.9 0.1 broadcast_in_dim.297
  2.1 4.1 %fusion.16 = (f32[1024,256]{1,0:T(8,128)S(1)}, f32[1024,256]{1,0:T(8,128)S(1)}) fusion(s32[256]{0:T(256)S(1)} %iota_add_fusion.1), kind=kLoop, calls=%fused_computation.29 | loop fusion | flops 3932160 | bytes 2098176 | tf_op jit(solution)/shard_map/cos | solution.py:22
  6.2 0.1 broadcast_in_dim.242
  6.4 1.3 %fusion = f32[16,512]{1,0:T(8,128)S(1)} fusion(f32[1024,256]{1,0:T(8,128)S(1)} %get-tuple-element.69, f32[1024,256]{1,0:T(8,128)S(1)} %get-tuple-element.68, f32[1024]{0:T(1024)S(1)} %multiply_subtract_fusion, f32[16,1024]{1,0:T(8,128)S(1)} %bitcast.119, f32[16,1024]{1,0:T(8,128)S(1)} %bitcast.128, f32[16,1024]{1,0:T(8,128)S(1)} %bitcast.129, ...), kind=kOutput, calls=%fused_computation.1 | convolution fusion | flops 101924864 | bytes 2986192 | tf_op jit(solution)/shard_map/dot_general | solution.py:52
  7.7 0.1 fusion.63
  7.9 0.1 bitcast_multiply_fusion
  8.0 32.3 %all_gather.6 = bf16[16,8,512]{2,1,0:T(8,128)(2,1)S(1)} all-gather(bf16[2,8,512]{2,1,0:T(8,128)(2,1)S(1)} %fusion.34), channel_id=1, replica_groups=mesh['row'=4,'col'=8] {'col'}, dimensions={0}, use_global_device_ids=true | all-gather | bytes 147456 | tf_op jit(solution)/shard_map/all_gather | solution.py:102
  40.3 0.2 slice_convert_fusion.15
  40.6 5.2 %all_gather.7 = bf16[8,8,512]{2,1,0:T(8,128)(2,1)S(1)} all-gather(bf16[2,8,512]{2,1,0:T(8,128)(2,1)S(1)} %fusion.34), channel_id=1, replica_groups=mesh['row'=4,'col'=8] {'row'}, dimensions={0}, use_global_device_ids=true | all-gather | bytes 81920 | tf_op jit(solution)/shard_map/all_gather | solution.py:103
  45.8 0.1 slice_convert_fusion.31
  46.1 0.2 add_bitcast_fusion.1
  46.3 0.2 add_bitcast_fusion
  46.5 2.1 %fusion.20 = (f32[256,512]{1,0:T(8,128)S(1)}, f32[256,512]{1,0:T(8,128)S(1)}) fusion(s32[512]{0:T(512)S(1)} %iota_add_fusion, s32[256]{0:T(256)S(1)} %iota_add_fusion.1), kind=kLoop, calls=%fused_computation.33 | loop fusion | flops 1966080 | bytes 1051648 | tf_op jit(solution)/shard_map/cos | solution.py:31
  48.6 0.7 %convolution_convert_fusion = bf16[128,512]{1,0:T(8,128)(2,1)S(1)} fusion(f32[256,512]{1,0:T(8,128)S(1)} %get-tuple-element.55, f32[256,512]{1,0:T(8,128)S(1)} %get-tuple-element.54, f32[128,256]{1,0:T(8,128)S(1)} %add_bitcast_fusion, f32[128,256]{1,0:T(8,128)S(1)} %add_bitcast_fusion.1), kind=kOutput, calls=%fused_computation.7 | convolution fusion | flops 403308544 | bytes 1441792 | tf_op jit(solution)/shard_map/dot_general | solution.py:93
  49.4 0.7 %reshape_reshape.3 = bf16[16,1,4,2,512]{4,3,2,0,1:T(2,128)(2,1)} reshape(bf16[128,512]{1,0:T(8,128)(2,1)S(1)} %convolution_convert_fusion) | data formatting | bytes 262144 | tf_op jit(solution)/shard_map/reshape;reshape | solution.py:105
  (50 shorter events, 0.6 us)
Async XLA Ops:
  0.0 1.0 %copy-start = (s32[2,8]{1,0:T(2,128)S(1)}, s32[2,8]{1,0:T(2,128)}, u32[]{:S(2)}) copy-start(s32[2,8]{1,0:T(2,128)} %param.6) | copy-start | bytes 196
  6.3 1.5 %copy-start.3 = (s32[2]{0:T(128)S(1)}, s32[2]{0:T(128)}, u32[]{:S(2)}) copy-start(s32[2]{0:T(128)} %param.9) | copy-start | bytes 28
  6.3 1.5 %copy-start.1 = (s32[2]{0:T(128)S(1)}, s32[2]{0:T(128)}, u32[]{:S(2)}) copy-start(s32[2]{0:T(128)} %param.8) | copy-start | bytes 28
  6.3 1.5 %copy-start.2 = (s32[2]{0:T(128)S(1)}, s32[2]{0:T(128)}, u32[]{:S(2)}) copy-start(s32[2]{0:T(128)} %param.7) | copy-start | bytes 28
where the time goes:
time: 50.3 us; the launch traced here: 50.1 us
  blocking collectives  37.6 us (75%)
  other arithmetic  7.31 us (15%)
  local copies, waits for them, and re-layouts  2.77 us (6%)
  matrix products  2.05 us (4%)
    all_gather x1, blocking collectives, body(): first_panel = lax.all_gather(white, 'col', axis=0, tiled=True)  32.3 us
    all_gather x1, blocking collectives, body(): lax.all_gather(white, 'row', axis=0, tiled=True)  5.25 us
    cos x1, other arithmetic, transform_table(): jnp.cos(phase)  4.13 us
    cos x1, other arithmetic, lag_table(): jnp.cos(phase)  2.13 us
    dot_general x1, matrix products, whiten(): spec = jnp.dot(flat, transform_table(), precision=lax.Precision.HIGHEST)  1.31 us
    broadcast_in_dim x27, local copies, waits for them, and re-layouts, cut_segments(): segment = jnp.where(picked, blocks[:, :, place:place + 4, :], segment)  1.2 us

commit v1 on v0

v1 whole, which is shorter than its diff:
```python
import functools
import math

import jax
import jax.numpy as jnp
import numpy as np
from jax import lax
from jax.experimental import pallas as pl
from jax.experimental.pallas import tpu as pltpu
from jax.sharding import PartitionSpec as P

SEG = 8
SAMPLES = 1024
BINS = 256
LAGS = 512
TRACE = 4096
QUARTER = SAMPLES // 4
BLOCKS = TRACE // QUARTER
LANES = 128
VMEM = pl.BlockSpec(memory_space=pltpu.VMEM)
SMEM = pl.BlockSpec(memory_space=pltpu.SMEM)


def split(values):
    high = values.astype(jnp.bfloat16)
    return high, (values - high.astype(jnp.float32)).astype(jnp.bfloat16)


def split_table(table):
    high = table.astype(jnp.bfloat16)
    return np.stack([high, (table - high.astype(np.float64)).astype(jnp.bfloat16)])


def quarter_table():
    times = np.arange(QUARTER)
    freqs = np.arange(BINS) + 1
    phase = (times[:, None] * freqs[None, :] % SAMPLES) * (2.0 * math.pi / SAMPLES)
    return split_table(np.concatenate([np.cos(phase), -np.sin(phase)], axis=1))


def wave_rows():
    turn = np.arange(QUARTER) * (2.0 * math.pi / SAMPLES)
    freqs = np.arange(BINS) + 1
    cos_turn = np.array([1.0, 0.0, -1.0, 0.0])[freqs % 4]
    sin_turn = np.array([0.0, 1.0, 0.0, -1.0])[freqs % 4]
    rows = np.zeros((8, QUARTER), np.float32)
    rows[0] = np.cos(turn)
    rows[1] = np.sin(turn)
    rows[2] = cos_turn
    rows[3] = sin_turn
    rows[4] = np.where(freqs % 2 == 0, 1.0, -1.0)
    return rows


def lag_table():
    freqs = np.arange(BINS) + 1
    shifts = np.arange(LAGS) - LAGS // 2
    phase = (freqs[:, None] * shifts[None, :] % SAMPLES) * (2.0 * math.pi / SAMPLES)
    table = np.concatenate([np.cos(phase), -np.sin(phase)], axis=0)
    return split_table(table / math.sqrt(SEG * BINS))


def dot(left, right):
    return jnp.dot(left, right, preferred_element_type=jnp.float32)


def dot_split(values, table_ref):
    high, low = split(values)
    return dot(high, table_ref[0]) + (dot(low, table_ref[0]) + dot(high, table_ref[1]))


def whiten_kernel(offsets, band_lo, band_hi, live, traces, table, waves, out, quarters, white):
    count = traces.shape[0]
    rows = count * BLOCKS
    for k in range(count):
        for block in range(BLOCKS):
            quarters[pl.ds(k * BLOCKS + block, 1), :] = traces[
                pl.ds(k, 1), pl.ds(block * QUARTER, QUARTER)
            ]
    plain = quarters[...] * 0.5
    spectra = dot_split(
        jnp.concatenate([plain, plain * waves[0:1, :], plain * waves[1:2, :]], axis=0), table
    )
    flat, with_cos, with_sin = (spectra[n * rows : (n + 1) * rows] for n in range(3))

    def later(values, steps):
        return pltpu.roll(values, rows - steps, 0)

    first = flat - with_cos
    second = later(flat + with_sin, 1)
    third = later(flat + with_cos, 2)
    fourth = later(flat - with_sin, 3)
    cos_turn, sin_turn, sign = waves[2:3, :], waves[3:4, :], waves[4:5, :]
    both = second + fourth
    diff = second - fourth
    re = (
        first[:, :BINS]
        + third[:, :BINS] * sign
        + (both[:, :BINS] * cos_turn + diff[:, BINS:] * sin_turn)
    )
    im = (
        first[:, BINS:]
        + third[:, BINS:] * sign
        + (both[:, BINS:] * cos_turn - diff[:, :BINS] * sin_turn)
    )
    amp = jnp.sqrt(re * re + im * im)
    bins = lax.broadcasted_iota(jnp.int32, (1, BINS), 1)
    total = amp
    for step in (1, 2):
        total = total + jnp.where(bins >= step, pltpu.roll(amp, step, 1), 0.0)
        total = total + jnp.where(bins < BINS - step, pltpu.roll(amp, BINS - step, 1), 0.0)
    level = jnp.sum(amp, axis=1, keepdims=True) * (1.0 / BINS)
    factor = 1.0 / (total / 5.0 + 0.1 * level + 1e-06)
    keep = jnp.concatenate(
        [
            jnp.broadcast_to(
                jnp.where(
                    (bins >= band_lo[k]) & (bins < jnp.where(live[k] == 1, band_hi[k], 0)), 1.0, 0.0
                ),
                (BLOCKS, BINS),
            )
            for k in range(count)
        ],
        axis=0,
    )
    factor = factor * keep
    re, im = re * factor, im * factor
    for t in range(BINS // LANES):
        white[t] = re[:, t * LANES : (t + 1) * LANES]
        white[t + BINS // LANES] = im[:, t * LANES : (t + 1) * LANES]
    for t in range(2 * BINS // LANES):
        picked = [
            white[t, pl.ds(k * BLOCKS + lax.div(offsets[k, s], QUARTER), 1), :]
            for k in range(count)
            for s in range(SEG)
        ]
        out[:, t * LANES : (t + 1) * LANES] = jnp.concatenate(picked, axis=0).astype(jnp.bfloat16)


def whiten(traces, offsets, band_lo, band_hi, live):
    count = traces.shape[0]
    rows = count * BLOCKS
    return pl.pallas_call(
        whiten_kernel,
        out_shape=jax.ShapeDtypeStruct((count * SEG, 2 * BINS), jnp.bfloat16),
        in_specs=[SMEM] * 4 + [VMEM] * 3,
        out_specs=VMEM,
        scratch_shapes=[
            pltpu.VMEM((rows, QUARTER), jnp.float32),
            pltpu.VMEM((2 * BINS // LANES, rows, LANES), jnp.float32),
        ],
        name="whiten",
    )(offsets, band_lo, band_hi, live, traces, jnp.asarray(quarter_table()), jnp.asarray(wave_rows()))


def correlate_kernel(count, first_masks, second_masks, *refs):
    n_first, n_second = len(first_masks), len(second_masks)
    first_refs, second_refs = refs[:n_first], refs[n_first : n_first + n_second]
    table, out, left, right, cross = refs[n_first + n_second :]
    wide = count * n_second
    for n, ref in enumerate(second_refs):
        for k in range(count):
            rows = ref[k * SEG : (k + 1) * SEG, :].astype(jnp.float32)
            for t in range(2 * BINS // LANES):
                right[t, pl.ds(n * count + k, SEG, stride=wide), :] = rows[
                    :, t * LANES : (t + 1) * LANES
                ]
    at = 0
    for ref in first_refs:
        left[at : at + ref.shape[0], :] = ref[...].astype(jnp.float32)
        at += ref.shape[0]
    channels = at // SEG

    @pl.loop(0, channels, unroll=4)
    def _(i):
        there = pl.ds(pl.multiple_of(i * wide, wide), wide)
        segments = pl.ds(pl.multiple_of(i * SEG, SEG), SEG)
        for t in range(BINS // LANES):
            re = pl.ds(t * LANES, LANES)
            im = pl.ds(BINS + t * LANES, LANES)
            cross_re = jnp.zeros((wide, LANES), jnp.float32)
            cross_im = jnp.zeros((wide, LANES), jnp.float32)
            rows_re, rows_im = left[segments, re], left[segments, im]
            for s in range(SEG):
                left_re, left_im = rows_re[s : s + 1, :], rows_im[s : s + 1, :]
                right_re = right[t, s * wide : (s + 1) * wide, :]
                right_im = right[t + BINS // LANES, s * wide : (s + 1) * wide, :]
                cross_re = cross_re + (left_re * right_re + left_im * right_im)
                cross_im = cross_im + (left_im * right_re - left_re * right_im)
            cross[there, re] = cross_re
            cross[there, im] = cross_im

    row_index, col_index = lax.axis_index("row"), lax.axis_index("col")
    at = 0
    for masks in first_masks:
        for mask in masks:
            size = count * wide
            corr = dot_split(cross[at : at + size, :], table).astype(jnp.bfloat16)
            at += size
            for k in range(count):
                for n, row_mask in enumerate(second_masks):
                    start = k * wide + n * count
                    out[(col_index ^ mask) * count + k, 0, row_index ^ row_mask] = corr[
                        start : start + count, :
                    ]


def correlate(count, n_row, n_col, first, second):
    first_masks = tuple(tuple(masks) for masks, _ in first)
    second_masks = tuple(mask for masks, _ in second for mask in masks)
    channels, wide = count * n_col, count * n_row
    return pl.pallas_call(
        functools.partial(correlate_kernel, count, first_masks, second_masks),
        out_shape=jax.ShapeDtypeStruct((channels, 1, n_row, count, LAGS), jnp.bfloat16),
        in_specs=[VMEM] * (len(first) + len(second) + 1),
        out_specs=VMEM,
        scratch_shapes=[
            pltpu.VMEM((channels * SEG, 2 * BINS), jnp.float32),
            pltpu.VMEM((2 * BINS // LANES, wide * SEG, LANES), jnp.float32),
            pltpu.VMEM((channels * wide, 2 * BINS), jnp.float32),
        ],
        name="correlate",
    )(*(a for _, a in first), *(a for _, a in second), jnp.asarray(lag_table()))


def swap(block, axis, mask):
    return lax.ppermute(block, axis, [(i, i ^ mask) for i in range(lax.axis_size(axis))])


def body(traces, offsets, band_lo, band_hi, live):
    count = traces.shape[0]
    n_row, n_col = lax.axis_size("row"), lax.axis_size("col")
    white = whiten(traces, offsets, band_lo, band_hi, live)
    second = [([0], white)]
    bit = n_row // 2
    while bit:
        second += [([masks[0] ^ bit], swap(block, "row", bit)) for masks, block in second]
        bit //= 2
    held, masks = white, [0]
    bit = n_col // 2
    while bit > 2:
        held = jnp.concatenate([held, swap(held, "col", bit)], axis=0)
        masks = masks + [mask ^ bit for mask in masks]
        bit //= 2
    first = [(masks, held)]
    for step in (3, 1, 2):
        if step < n_col:
            first.append(([mask ^ step for mask in masks], swap(held, "col", step)))
    return correlate(count, n_row, n_col, first, second)


def solution(mesh):
    in_specs = (
        P(("row", "col"), None),
        P(("row", "col"), None),
        P(("row", "col")),
        P(("row", "col")),
        P(("row", "col")),
    )
    out_specs = P("row", "col", None, None, None)
    return jax.shard_map(body, mesh=mesh, in_specs=in_specs, out_specs=out_specs, check_vma=False)
```

time: 50.3 us -> 22 us (0.44)
  blocking collectives: 37.6 us -> 0 us
  starting transfers between devices: 0 us -> 9.54 us
  other arithmetic: 7.31 us -> 0.72 us
  Pallas kernels: 0 us -> 6.25 us
  waiting for transfers between devices: 0 us -> 4.6 us
  local copies, waits for them, and re-layouts: 2.77 us -> 0.62 us
  matrix products: 2.05 us -> 0 us
    all_gather x2 -> x0, blocking collectives: 37.6 us -> none  [the longest x1 32.3 us: body(): first_panel = lax.all_gather(white, 'col', axis=0, tiled=True)]
    ppermute x0 -> x7, starting transfers between devices: none -> 9.54 us  [swap(): lax.ppermute(block, axis, [(i, i ^ mask) for i in range(lax.axis_size(axi...]
    cos x2 -> x0, other arithmetic: 6.27 us -> none  [the longest x1 4.13 us: transform_table(): jnp.cos(phase)]
    pallas_call x0 -> x2, Pallas kernels: none -> 6.25 us  [the longest x1 4.11 us: correlate(): pl.pallas_call(functools.partial(correlate_kernel, count, first_masks, se...]
    ppermute x0 -> x7, waiting for transfers between devices: none -> 4.6 us  [swap(): lax.ppermute(block, axis, [(i, i ^ mask) for i in range(lax.axis_size(axi...]
    dot_general x2 -> x0, matrix products: 2.05 us -> none  [the longest x1 1.31 us: whiten(): spec = jnp.dot(flat, transform_table(), precision=lax.Precision.HIGHEST)]
    broadcast_in_dim x27 -> x0, local copies, waits for them, and re-layouts: 1.2 us -> none  [cut_segments(): segment = jnp.where(picked, blocks[:, :, place:place + 4, :], segment)]
    concatenate x0 -> x1, other arithmetic: none -> 0.72 us  [body(): held = jnp.concatenate([held, swap(held, 'col', bit)], axis=0)]
  transfers between devices with their start and end apart: 0 -> 7, of which waited for: 0 -> 5; matrix products, arithmetic and copies ran while one was open for 0% -> 3% of each run, Pallas kernels for 0% -> 0%
where the time goes in v1:
time: 22 us; the launch traced here: 21.8 us
  starting transfers between devices  9.54 us (43%)
  Pallas kernels  6.25 us (28%)
  waiting for transfers between devices  4.6 us (21%)
  other arithmetic  0.72 us (3%)
  local copies, waits for them, and re-layouts  0.62 us (3%)
    ppermute x7, starting transfers between devices, swap(): lax.ppermute(block, axis, [(i, i ^ mask) for i in range(lax.axis_size(axi...  9.54 us
    ppermute x7, waiting for transfers between devices, swap(): lax.ppermute(block, axis, [(i, i ^ mask) for i in range(lax.axis_size(axi...  4.6 us
    pallas_call x1, Pallas kernels, correlate(): pl.pallas_call(functools.partial(correlate_kernel, count, first_masks, se...  4.11 us
    pallas_call x1, Pallas kernels, whiten(): pl.pallas_call(whiten_kernel, out_shape=jax.ShapeDtypeStruct((count * SEG...  2.14 us
    concatenate x1, other arithmetic, body(): held = jnp.concatenate([held, swap(held, 'col', bit)], axis=0)  0.72 us
    unnamed x16, local copies, waits for them, and re-layouts  0.62 us
  transfers between devices with their start and end apart: 7, of which 5 were waited for; matrix products, arithmetic and copies ran while one was open for 3% of the time, Pallas kernels for 0%

profile of v1, /device:TPU:0, one launch (start us, length us, event | category | flops | bytes accessed | tf_op | source)
XLA Modules:
  0.0 21.8 jit_solution(10647432445828884347)
XLA Ops:
  0.0 2.1 %whiten.1.refs_4_ = bf16[16,512]{1,0:T(8,128)(2,1)} custom-call(s32[2,8]{1,0:T(2,128)} %offsets.1, s32[2]{0:T(128)} %band_lo.1, s32[2]{0:T(128)} %band_hi.1, s32[2]{0:T(128)} %live.1, f32[2,4096]{1,0:T(2,128)} %traces.1, bf16[2,256,512]{2,1,0:T(8,128)(2,1)} %constant.6.clone.table, f32[8,256]{1,0:T(8,128)} %constant.7.clone.waves), custom_call_target="tpu_custom_call" | custom-call | tf_op jit(solution)/shard_map/whiten/pallas_call | solution.py:143
  2.1 4.0 %collective-permute-start = (bf16[16,512]{1,0:T(8,128)(2,1)}, bf16[16,512]{1,0:T(8,128)(2,1)S(1)}, u32[]{:S(2)}, u32[]{:S(2)}) collective-permute-start(bf16[16,512]{1,0:T(8,128)(2,1)} %whiten.1.refs_4_), channel_id=1, source_target_pairs={{0,4},{1,5},{2,6},{3,7},{4,0},{5,1},{6,2},{7,3},{8,12},{9,13},{10,... | collective-permute-start | bytes 49160 | tf_op jit(solution)/shard_map/ppermute | solution.py:227
  6.2 1.5 %collective-permute-start.4 = (bf16[16,512]{1,0:T(8,128)(2,1)}, bf16[16,512]{1,0:T(8,128)(2,1)S(1)}, u32[]{:S(2)}, u32[]{:S(2)}) collective-permute-start(bf16[16,512]{1,0:T(8,128)(2,1)} %whiten.1.refs_4_), channel_id=1, source_target_pairs={{0,16},{8,24},{16,0},{24,8},{1,17},{9,25},{17,1},{25,9},{2,18},{10... | collective-permute-start | bytes 49160 | tf_op jit(solution)/shard_map/ppermute | solution.py:227
  7.7 0.5 %collective-permute-done = bf16[16,512]{1,0:T(8,128)(2,1)S(1)} collective-permute-done((bf16[16,512]{1,0:T(8,128)(2,1)}, bf16[16,512]{1,0:T(8,128)(2,1)S(1)}, u32[]{:S(2)}, u32[]{:S(2)}) %collective-permute-start) | collective-permute-done | bytes 16416 | tf_op jit(solution)/shard_map/ppermute | solution.py:227
  8.2 0.7 %pad_maximum_fusion.refs_0_ = bf16[32,512]{1,0:T(8,128)(2,1)S(1)} fusion(bf16[16,512]{1,0:T(8,128)(2,1)S(1)} %collective-permute-done, bf16[16,512]{1,0:T(8,128)(2,1)} %whiten.1.refs_4_), kind=kLoop, calls=%fused_computation | loop fusion | flops 65536 | bytes 65536 | tf_op jit(solution)/shard_map/concatenate | solution.py:242
  8.9 1.8 %collective-permute-start.3 = (bf16[32,512]{1,0:T(8,128)(2,1)S(1)}, bf16[32,512]{1,0:T(8,128)(2,1)S(1)}, u32[]{:S(2)}, u32[]{:S(2)}) collective-permute-start(bf16[32,512]{1,0:T(8,128)(2,1)S(1)} %pad_maximum_fusion.refs_0_), channel_id=1, source_target_pairs={{0,2},{1,3},{2,0},{3,1},{4,6},{5,7},{6,4},{7,5},{8,10},{9,11},{10,... | collective-permute-start | bytes 98312 | tf_op jit(solution)/shard_map/ppermute | solution.py:227
  10.7 1.5 %collective-permute-start.2 = (bf16[32,512]{1,0:T(8,128)(2,1)S(1)}, bf16[32,512]{1,0:T(8,128)(2,1)S(1)}, u32[]{:S(2)}, u32[]{:S(2)}) collective-permute-start(bf16[32,512]{1,0:T(8,128)(2,1)S(1)} %pad_maximum_fusion.refs_0_), channel_id=1, source_target_pairs={{0,1},{1,0},{2,3},{3,2},{4,5},{5,4},{6,7},{7,6},{8,9},{9,8},{10,11... | collective-permute-start | bytes 98312 | tf_op jit(solution)/shard_map/ppermute | solution.py:227
  12.2 0.2 collective-permute-start.1
  12.4 0.0 copy-done
  12.4 0.0 collective-permute-start.5
  12.4 0.0 collective-permute-done.4.refs_5_
  12.4 0.0 copy-start.5
  12.4 0.5 %collective-permute-start.6 = (bf16[16,512]{1,0:T(8,128)(2,1)S(1)}, bf16[16,512]{1,0:T(8,128)(2,1)S(1)}, u32[]{:S(2)}, u32[]{:S(2)}) collective-permute-start(bf16[16,512]{1,0:T(8,128)(2,1)S(1)} %collective-permute-done.4.refs_5_), channel_id=1, source_target_pairs={{0,8},{8,0},{16,24},{24,16},{1,9},{9,1},{17,25},{25,17},{2,10},{10... | collective-permute-start | bytes 49160 | tf_op jit(solution)/shard_map/ppermute | solution.py:227
  12.9 0.7 %collective-permute-done.5.refs_6_ = bf16[16,512]{1,0:T(8,128)(2,1)S(1)} collective-permute-done((bf16[16,512]{1,0:T(8,128)(2,1)S(1)}, bf16[16,512]{1,0:T(8,128)(2,1)S(1)}, u32[]{:S(2)}, u32[]{:S(2)}) %collective-permute-start.5) | collective-permute-done | bytes 16416 | tf_op jit(solution)/shard_map/ppermute | solution.py:227
  13.6 0.2 collective-permute-done.6.refs_7_
  13.8 0.0 collective-permute-done.3.refs_3_
  13.8 1.0 %collective-permute-done.2.refs_2_ = bf16[32,512]{1,0:T(8,128)(2,1)S(1)} collective-permute-done((bf16[32,512]{1,0:T(8,128)(2,1)S(1)}, bf16[32,512]{1,0:T(8,128)(2,1)S(1)}, u32[]{:S(2)}, u32[]{:S(2)}) %collective-permute-start.2) | collective-permute-done | bytes 32800 | tf_op jit(solution)/shard_map/ppermute | solution.py:227
  14.8 2.3 %collective-permute-done.1.refs_1_ = bf16[32,512]{1,0:T(8,128)(2,1)S(1)} collective-permute-done((bf16[32,512]{1,0:T(8,128)(2,1)S(1)}, bf16[32,512]{1,0:T(8,128)(2,1)S(1)}, u32[]{:S(2)}, u32[]{:S(2)}) %collective-permute-start.1) | collective-permute-done | bytes 32800 | tf_op jit(solution)/shard_map/ppermute | solution.py:227
  17.0 0.0 copy-done.1
  17.0 0.0 copy-done.5
  17.0 0.0 copy-done.6
  17.1 0.0 copy-done.7
  17.1 0.6 %copy-done.4 = bf16[32,512]{1,0:T(8,128)(2,1)} copy-done((bf16[32,512]{1,0:T(8,128)(2,1)}, bf16[32,512]{1,0:T(8,128)(2,1)S(1)}, u32[]{:S(2)}) %copy-start.4) | copy-done | bytes 32792
  17.7 4.1 %correlate.1 = bf16[16,1,4,2,512]{4,3,2,1,0:T(2,128)(2,1)} custom-call(bf16[32,512]{1,0:T(8,128)(2,1)} %copy-done.1, bf16[32,512]{1,0:T(8,128)(2,1)} %copy-done.4, bf16[32,512]{1,0:T(8,128)(2,1)} %copy-done.3, bf16[32,512]{1,0:T(8,128)(2,1)} %copy-done.2, bf16[16,512]{1,0:T(8,128)(2,1)} %whiten.1.refs_4_, bf16[16,512]{1,0:T(8,128)(2,1)} %copy-done.5, ...), custom_call_target="tpu_custom_call" | custom-call | tf_op jit(solution)/shard_map/correlate/pallas_call | solution.py:212
  (9 shorter events, 0.0 us)
Async XLA Ops:
  2.1 10.3 %copy-start = (bf16[16,512]{1,0:T(8,128)(2,1)S(1)}, bf16[16,512]{1,0:T(8,128)(2,1)}, u32[]{:S(2)}) copy-start(bf16[16,512]{1,0:T(8,128)(2,1)} %whiten.1.refs_4_) | copy-start | bytes 49156
  2.1 6.0 %collective-permute-start = (bf16[16,512]{1,0:T(8,128)(2,1)}, bf16[16,512]{1,0:T(8,128)(2,1)S(1)}, u32[]{:S(2)}, u32[]{:S(2)}) collective-permute-start(bf16[16,512]{1,0:T(8,128)(2,1)} %whiten.1.refs_4_), channel_id=1, source_target_pairs={{0,4},{1,5},{2,6},{3,7},{4,0},{5,1},{6,2},{7,3},{8,12},{9,13},{10,... | collective-permute-start | bytes 49160 | tf_op jit(solution)/shard_map/ppermute | solution.py:227
  6.2 6.2 %collective-permute-start.4 = (bf16[16,512]{1,0:T(8,128)(2,1)}, bf16[16,512]{1,0:T(8,128)(2,1)S(1)}, u32[]{:S(2)}, u32[]{:S(2)}) collective-permute-start(bf16[16,512]{1,0:T(8,128)(2,1)} %whiten.1.refs_4_), channel_id=1, source_target_pairs={{0,16},{8,24},{16,0},{24,8},{1,17},{9,25},{17,1},{25,9},{2,18},{10... | collective-permute-start | bytes 49160 | tf_op jit(solution)/shard_map/ppermute | solution.py:227
  8.9 8.1 %copy-start.1 = (bf16[32,512]{1,0:T(8,128)(2,1)}, bf16[32,512]{1,0:T(8,128)(2,1)S(1)}, u32[]{:S(2)}) copy-start(bf16[32,512]{1,0:T(8,128)(2,1)S(1)} %pad_maximum_fusion.refs_0_) | copy-start | bytes 98308
  8.9 4.9 %collective-permute-start.3 = (bf16[32,512]{1,0:T(8,128)(2,1)S(1)}, bf16[32,512]{1,0:T(8,128)(2,1)S(1)}, u32[]{:S(2)}, u32[]{:S(2)}) collective-permute-start(bf16[32,512]{1,0:T(8,128)(2,1)S(1)} %pad_maximum_fusion.refs_0_), channel_id=1, source_target_pairs={{0,2},{1,3},{2,0},{3,1},{4,6},{5,7},{6,4},{7,5},{8,10},{9,11},{10,... | collective-permute-start | bytes 98312 | tf_op jit(solution)/shard_map/ppermute | solution.py:227
  10.7 4.0 %collective-permute-start.2 = (bf16[32,512]{1,0:T(8,128)(2,1)S(1)}, bf16[32,512]{1,0:T(8,128)(2,1)S(1)}, u32[]{:S(2)}, u32[]{:S(2)}) collective-permute-start(bf16[32,512]{1,0:T(8,128)(2,1)S(1)} %pad_maximum_fusion.refs_0_), channel_id=1, source_target_pairs={{0,1},{1,0},{2,3},{3,2},{4,5},{5,4},{6,7},{7,6},{8,9},{9,8},{10,11... | collective-permute-start | bytes 98312 | tf_op jit(solution)/shard_map/ppermute | solution.py:227
  12.2 4.8 %collective-permute-start.1 = (bf16[32,512]{1,0:T(8,128)(2,1)S(1)}, bf16[32,512]{1,0:T(8,128)(2,1)S(1)}, u32[]{:S(2)}, u32[]{:S(2)}) collective-permute-start(bf16[32,512]{1,0:T(8,128)(2,1)S(1)} %pad_maximum_fusion.refs_0_), channel_id=1, source_target_pairs={{0,3},{1,2},{2,1},{3,0},{4,7},{5,6},{6,5},{7,4},{8,11},{9,10},{10,... | collective-permute-start | bytes 98312 | tf_op jit(solution)/shard_map/ppermute | solution.py:227
  12.4 1.2 %collective-permute-start.5 = (bf16[16,512]{1,0:T(8,128)(2,1)S(1)}, bf16[16,512]{1,0:T(8,128)(2,1)S(1)}, u32[]{:S(2)}, u32[]{:S(2)}) collective-permute-start(bf16[16,512]{1,0:T(8,128)(2,1)S(1)} %copy-done), channel_id=1, source_target_pairs={{0,8},{8,0},{16,24},{24,16},{1,9},{9,1},{17,25},{25,17},{2,10},{10... | collective-permute-start | bytes 49160 | tf_op jit(solution)/shard_map/ppermute | solution.py:227
  12.4 4.6 %copy-start.5 = (bf16[16,512]{1,0:T(8,128)(2,1)}, bf16[16,512]{1,0:T(8,128)(2,1)S(1)}, u32[]{:S(2)}) copy-start(bf16[16,512]{1,0:T(8,128)(2,1)S(1)} %collective-permute-done.4.refs_5_) | copy-start | bytes 49156
  12.4 1.3 %collective-permute-start.6 = (bf16[16,512]{1,0:T(8,128)(2,1)S(1)}, bf16[16,512]{1,0:T(8,128)(2,1)S(1)}, u32[]{:S(2)}, u32[]{:S(2)}) collective-permute-start(bf16[16,512]{1,0:T(8,128)(2,1)S(1)} %collective-permute-done.4.refs_5_), channel_id=1, source_target_pairs={{0,8},{8,0},{16,24},{24,16},{1,9},{9,1},{17,25},{25,17},{2,10},{10... | collective-permute-start | bytes 49160 | tf_op jit(solution)/shard_map/ppermute | solution.py:227
  13.6 3.5 %copy-start.6 = (bf16[16,512]{1,0:T(8,128)(2,1)}, bf16[16,512]{1,0:T(8,128)(2,1)S(1)}, u32[]{:S(2)}) copy-start(bf16[16,512]{1,0:T(8,128)(2,1)S(1)} %collective-permute-done.5.refs_6_) | copy-start | bytes 49156
  13.8 3.3 %copy-start.7 = (bf16[16,512]{1,0:T(8,128)(2,1)}, bf16[16,512]{1,0:T(8,128)(2,1)S(1)}, u32[]{:S(2)}) copy-start(bf16[16,512]{1,0:T(8,128)(2,1)S(1)} %collective-permute-done.6.refs_7_) | copy-start | bytes 49156
  13.8 3.3 %copy-start.2 = (bf16[32,512]{1,0:T(8,128)(2,1)}, bf16[32,512]{1,0:T(8,128)(2,1)S(1)}, u32[]{:S(2)}) copy-start(bf16[32,512]{1,0:T(8,128)(2,1)S(1)} %collective-permute-done.3.refs_3_) | copy-start | bytes 98308
  14.8 2.3 %copy-start.3 = (bf16[32,512]{1,0:T(8,128)(2,1)}, bf16[32,512]{1,0:T(8,128)(2,1)S(1)}, u32[]{:S(2)}) copy-start(bf16[32,512]{1,0:T(8,128)(2,1)S(1)} %collective-permute-done.2.refs_2_) | copy-start | bytes 98308
  17.1 0.6 %copy-start.4 = (bf16[32,512]{1,0:T(8,128)(2,1)}, bf16[32,512]{1,0:T(8,128)(2,1)S(1)}, u32[]{:S(2)}) copy-start(bf16[32,512]{1,0:T(8,128)(2,1)S(1)} %collective-permute-done.1.refs_1_) | copy-start | bytes 98308

commit v2 on v1

--- a/solution.py
+++ b/solution.py
@@ -60,6 +60,10 @@
     return split_table(table / math.sqrt(SEG * BINS))
 
 
+def in_vmem(array):
+    return pltpu.with_memory_space_constraint(array, pltpu.VMEM)
+
+
 def dot(left, right):
     return jnp.dot(left, right, preferred_element_type=jnp.float32)
 
@@ -69,8 +73,21 @@
     return dot(high, table_ref[0]) + (dot(low, table_ref[0]) + dot(high, table_ref[1]))
 
 
-def whiten_kernel(offsets, band_lo, band_hi, live, traces, table, waves, out, quarters, white):
+def whiten_kernel(
+    offsets_in, band_lo_in, band_hi_in, live_in, traces_in, waves_in, table_in, lags_in,
+    out, lags_out,
+    offsets, band_lo, band_hi, live, traces, waves, table, quarters, white, arrived,
+):
+    sources = (traces_in, waves_in, table_in, offsets_in, band_lo_in, band_hi_in, live_in, lags_in)
+    targets = (traces, waves, table, offsets, band_lo, band_hi, live, lags_out)
+    copies = [
+        pltpu.make_async_copy(source, target, arrived.at[n])
+        for n, (source, target) in enumerate(zip(sources, targets, strict=True))
+    ]
+    for copy in copies:
+        copy.start()
     count = traces.shape[0]
+    copies[0].wait()
     rows = count * BLOCKS
     for k in range(count):
         for block in range(BLOCKS):
@@ -78,9 +95,10 @@
                 pl.ds(k, 1), pl.ds(block * QUARTER, QUARTER)
             ]
     plain = quarters[...] * 0.5
-    spectra = dot_split(
-        jnp.concatenate([plain, plain * waves[0:1, :], plain * waves[1:2, :]], axis=0), table
-    )
+    copies[1].wait()
+    parts = jnp.concatenate([plain, plain * waves[0:1, :], plain * waves[1:2, :]], axis=0)
+    copies[2].wait()
+    spectra = dot_split(parts, table)
     flat, with_cos, with_sin = (spectra[n * rows : (n + 1) * rows] for n in range(3))
 
     def later(values, steps):
@@ -110,6 +128,8 @@
         total = total + jnp.where(bins >= step, pltpu.roll(amp, step, 1), 0.0)
         total = total + jnp.where(bins < BINS - step, pltpu.roll(amp, BINS - step, 1), 0.0)
     level = jnp.sum(amp, axis=1, keepdims=True) * (1.0 / BINS)
+    for copy in copies[3:7]:
+        copy.wait()
     factor = 1.0 / (total / 5.0 + 0.1 * level + 1e-06)
     keep = jnp.concatenate(
         [
@@ -135,27 +155,40 @@
             for s in range(SEG)
         ]
         out[:, t * LANES : (t + 1) * LANES] = jnp.concatenate(picked, axis=0).astype(jnp.bfloat16)
+    copies[7].wait()
 
 
 def whiten(traces, offsets, band_lo, band_hi, live):
     count = traces.shape[0]
     rows = count * BLOCKS
+    tables = (wave_rows(), quarter_table(), lag_table())
     return pl.pallas_call(
         whiten_kernel,
-        out_shape=jax.ShapeDtypeStruct((count * SEG, 2 * BINS), jnp.bfloat16),
-        in_specs=[SMEM] * 4 + [VMEM] * 3,
-        out_specs=VMEM,
+        out_shape=(
+            pltpu.VMEM((count * SEG, 2 * BINS), jnp.bfloat16),
+            pltpu.VMEM(tables[2].shape, jnp.bfloat16),
+        ),
+        in_specs=[pl.BlockSpec(memory_space=pl.ANY)] * 8,
+        out_specs=(VMEM, VMEM),
         scratch_shapes=[
+            pltpu.SMEM(offsets.shape, jnp.int32),
+            pltpu.SMEM(band_lo.shape, jnp.int32),
+            pltpu.SMEM(band_hi.shape, jnp.int32),
+            pltpu.SMEM(live.shape, jnp.int32),
+            pltpu.VMEM(traces.shape, jnp.float32),
+            pltpu.VMEM(tables[0].shape, jnp.float32),
+            pltpu.VMEM(tables[1].shape, jnp.bfloat16),
             pltpu.VMEM((rows, QUARTER), jnp.float32),
             pltpu.VMEM((2 * BINS // LANES, rows, LANES), jnp.float32),
+            pltpu.SemaphoreType.DMA((8,)),
         ],
         name="whiten",
-    )(offsets, band_lo, band_hi, live, traces, jnp.asarray(quarter_table()), jnp.asarray(wave_rows()))
+    )(offsets, band_lo, band_hi, live, traces, *(jnp.asarray(table) for table in tables))
 
 
 def correlate_kernel(count, first_masks, second_masks, *refs):
     n_first, n_second = len(first_masks), len(second_masks)
-    first_refs, second_refs = refs[:n_first], refs[n_first : n_first + n_second]
+    second_refs, first_refs = refs[:n_second], refs[n_second : n_first + n_second]
     table, out, left, right, cross = refs[n_first + n_second :]
     wide = count * n_second
     for n, ref in enumerate(second_refs):
@@ -192,10 +225,11 @@
 
     row_index, col_index = lax.axis_index("row"), lax.axis_index("col")
     at = 0
+    whole = dot_split(cross[...], table).astype(jnp.bfloat16)
     for masks in first_masks:
         for mask in masks:
             size = count * wide
-            corr = dot_split(cross[at : at + size, :], table).astype(jnp.bfloat16)
+            corr = whole[at : at + size]
             at += size
             for k in range(count):
                 for n, row_mask in enumerate(second_masks):
@@ -205,7 +239,7 @@
                     ]
 
 
-def correlate(count, n_row, n_col, first, second):
+def correlate(count, n_row, n_col, first, second, lags):
     first_masks = tuple(tuple(masks) for masks, _ in first)
     second_masks = tuple(mask for masks, _ in second for mask in masks)
     channels, wide = count * n_col, count * n_row
@@ -220,7 +254,7 @@
             pltpu.VMEM((channels * wide, 2 * BINS), jnp.float32),
         ],
         name="correlate",
-    )(*(a for _, a in first), *(a for _, a in second), jnp.asarray(lag_table()))
+    )(*(in_vmem(a) for _, a in second + first), in_vmem(lags))
 
 
 def swap(block, axis, mask):
@@ -230,7 +264,7 @@
 def body(traces, offsets, band_lo, band_hi, live):
     count = traces.shape[0]
     n_row, n_col = lax.axis_size("row"), lax.axis_size("col")
-    white = whiten(traces, offsets, band_lo, band_hi, live)
+    white, lags = whiten(traces, offsets, band_lo, band_hi, live)
     second = [([0], white)]
     bit = n_row // 2
     while bit:
@@ -239,14 +273,15 @@
     held, masks = white, [0]
     bit = n_col // 2
     while bit > 2:
-        held = jnp.concatenate([held, swap(held, "col", bit)], axis=0)
-        masks = masks + [mask ^ bit for mask in masks]
+        across = bit + bit // 2
+        held = jnp.concatenate([held, swap(held, "col", across)], axis=0)
+        masks = masks + [mask ^ across for mask in masks]
         bit //= 2
     first = [(masks, held)]
-    for step in (3, 1, 2):
+    for step in (2, 1, 3):
         if step < n_col:
             first.append(([mask ^ step for mask in masks], swap(held, "col", step)))
-    return correlate(count, n_row, n_col, first, second)
+    return correlate(count, n_row, n_col, first, second, lags)
 
 
 def solution(mesh):

time: 22 us -> 16 us (0.73)
  the two profiles are of different devices: /device:TPU:0 before, /device:TPU:22 now
where the time goes in v2:
time: 16 us; the launch traced here: 15.8 us
  starting transfers between devices  6.54 us (41%)
  waiting for transfers between devices  6.18 us (39%)
  Pallas kernels  3.08 us (19%)
    ppermute x7, starting transfers between devices, swap(): lax.ppermute(block, axis, [(i, i ^ mask) for i in range(lax.axis_size(axi...  6.54 us
    ppermute x7, waiting for transfers between devices, swap(): lax.ppermute(block, axis, [(i, i ^ mask) for i in range(lax.axis_size(axi...  6.18 us
    pallas_call x1, Pallas kernels, whiten(): pl.pallas_call(whiten_kernel, out_shape=(pltpu.VMEM((count * SEG, 2 * BIN...  1.71 us
    pallas_call x1, Pallas kernels, correlate(): pl.pallas_call(functools.partial(correlate_kernel, count, first_masks, se...  1.37 us
  transfers between devices with their start and end apart: 7, of which 5 were waited for; matrix products, arithmetic and copies ran while one was open for 0% of the time, Pallas kernels for 0%

profile of v2, /device:TPU:22, one launch (start us, length us, event | category | flops | bytes accessed | tf_op | source)
XLA Modules:
  0.0 15.8 jit_solution(3035328138152467699)
XLA Ops:
  0.0 1.7 %whiten.1 = (bf16[16,512]{1,0:T(8,128)(2,1)S(1)}, bf16[2,512,512]{2,1,0:T(8,128)(2,1)S(1)}) custom-call(s32[2,8]{1,0:T(2,128)} %offsets_in.1, s32[2]{0:T(128)} %band_lo_in.1, s32[2]{0:T(128)} %band_hi_in.1, s32[2]{0:T(128)} %live_in.1, f32[2,4096]{1,0:T(2,128)} %traces_in.1, f32[8,256]{1,0:T(8,128)} %constant.6.clone.waves_in, ...), custom_call_target="tpu_custom_call" | custom-call | tf_op jit(solution)/shard_map/whiten/pallas_call | solution.py:165
  1.7 0.5 %collective-permute-start.3 = (bf16[16,512]{1,0:T(8,128)(2,1)S(1)}, bf16[16,512]{1,0:T(8,128)(2,1)S(1)}, u32[]{:S(2)}, u32[]{:S(2)}) collective-permute-start(bf16[16,512]{1,0:T(8,128)(2,1)S(1)} %get-tuple-element.7.refs_0_), channel_id=1, source_target_pairs={{0,6},{1,7},{2,4},{3,5},{4,2},{5,3},{6,0},{7,1},{8,14},{9,15},{10,... | collective-permute-start | bytes 49160 | tf_op jit(solution)/shard_map/ppermute | solution.py:261
  2.2 0.5 %collective-permute-start = (bf16[16,512]{1,0:T(8,128)(2,1)S(1)}, bf16[16,512]{1,0:T(8,128)(2,1)S(1)}, u32[]{:S(2)}, u32[]{:S(2)}) collective-permute-start(bf16[16,512]{1,0:T(8,128)(2,1)S(1)} %get-tuple-element.7.refs_0_), channel_id=1, source_target_pairs={{0,16},{8,24},{16,0},{24,8},{1,17},{9,25},{17,1},{25,9},{2,18},{10... | collective-permute-start | bytes 49160 | tf_op jit(solution)/shard_map/ppermute | solution.py:261
  2.7 2.8 %collective-permute-done.3 = bf16[16,512]{1,0:T(8,128)(2,1)S(1)} collective-permute-done((bf16[16,512]{1,0:T(8,128)(2,1)S(1)}, bf16[16,512]{1,0:T(8,128)(2,1)S(1)}, u32[]{:S(2)}, u32[]{:S(2)}) %collective-permute-start.3) | collective-permute-done | bytes 16416 | tf_op jit(solution)/shard_map/ppermute | solution.py:261
  5.5 3.3 %collective-permute-start.6 = (bf16[32,512]{1,0:T(8,128)(2,1)S(1)}, bf16[32,512]{1,0:T(8,128)(2,1)S(1)}, u32[]{:S(2)}, u32[]{:S(2)}) collective-permute-start(bf16[32,512]{1,0:T(8,128)(2,1)S(1)} %constant_dynamic-update-slice_fusion.refs_4_), channel_id=1, source_target_pairs={{0,3},{1,2},{2,1},{3,0},{4,7},{5,6},{6,5},{7,4},{8,11},{9,10},{10,... | collective-permute-start | bytes 98312 | tf_op jit(solution)/shard_map/ppermute | solution.py:261
  8.9 1.7 %collective-permute-start.5 = (bf16[32,512]{1,0:T(8,128)(2,1)S(1)}, bf16[32,512]{1,0:T(8,128)(2,1)S(1)}, u32[]{:S(2)}, u32[]{:S(2)}) collective-permute-start(bf16[32,512]{1,0:T(8,128)(2,1)S(1)} %constant_dynamic-update-slice_fusion.refs_4_), channel_id=1, source_target_pairs={{0,1},{1,0},{2,3},{3,2},{4,5},{5,4},{6,7},{7,6},{8,9},{9,8},{10,11... | collective-permute-start | bytes 98312 | tf_op jit(solution)/shard_map/ppermute | solution.py:261
  10.5 0.0 collective-permute-start.4
  10.5 0.0 collective-permute-start.1
  10.5 0.0 collective-permute-done.refs_1_
  10.6 0.5 %collective-permute-start.2 = (bf16[16,512]{1,0:T(8,128)(2,1)S(1)}, bf16[16,512]{1,0:T(8,128)(2,1)S(1)}, u32[]{:S(2)}, u32[]{:S(2)}) collective-permute-start(bf16[16,512]{1,0:T(8,128)(2,1)S(1)} %collective-permute-done.refs_1_), channel_id=1, source_target_pairs={{0,8},{8,0},{16,24},{24,16},{1,9},{9,1},{17,25},{25,17},{2,10},{10... | collective-permute-start | bytes 49160 | tf_op jit(solution)/shard_map/ppermute | solution.py:261
  11.1 0.7 %collective-permute-done.1.refs_2_ = bf16[16,512]{1,0:T(8,128)(2,1)S(1)} collective-permute-done((bf16[16,512]{1,0:T(8,128)(2,1)S(1)}, bf16[16,512]{1,0:T(8,128)(2,1)S(1)}, u32[]{:S(2)}, u32[]{:S(2)}) %collective-permute-start.1) | collective-permute-done | bytes 16416 | tf_op jit(solution)/shard_map/ppermute | solution.py:261
  11.7 0.2 %collective-permute-done.2.refs_3_ = bf16[16,512]{1,0:T(8,128)(2,1)S(1)} collective-permute-done((bf16[16,512]{1,0:T(8,128)(2,1)S(1)}, bf16[16,512]{1,0:T(8,128)(2,1)S(1)}, u32[]{:S(2)}, u32[]{:S(2)}) %collective-permute-start.2) | collective-permute-done | bytes 16416 | tf_op jit(solution)/shard_map/ppermute | solution.py:261
  11.9 0.0 collective-permute-done.6.refs_7_
  11.9 0.9 %collective-permute-done.5.refs_6_ = bf16[32,512]{1,0:T(8,128)(2,1)S(1)} collective-permute-done((bf16[32,512]{1,0:T(8,128)(2,1)S(1)}, bf16[32,512]{1,0:T(8,128)(2,1)S(1)}, u32[]{:S(2)}, u32[]{:S(2)}) %collective-permute-start.5) | collective-permute-done | bytes 32800 | tf_op jit(solution)/shard_map/ppermute | solution.py:261
  12.8 1.7 %collective-permute-done.4.refs_5_ = bf16[32,512]{1,0:T(8,128)(2,1)S(1)} collective-permute-done((bf16[32,512]{1,0:T(8,128)(2,1)S(1)}, bf16[32,512]{1,0:T(8,128)(2,1)S(1)}, u32[]{:S(2)}, u32[]{:S(2)}) %collective-permute-start.4) | collective-permute-done | bytes 32800 | tf_op jit(solution)/shard_map/ppermute | solution.py:261
  14.5 1.4 %correlate.1 = bf16[16,1,4,2,512]{4,3,2,1,0:T(2,128)(2,1)} custom-call(bf16[16,512]{1,0:T(8,128)(2,1)S(1)} %get-tuple-element.7.refs_0_, bf16[16,512]{1,0:T(8,128)(2,1)S(1)} %collective-permute-done.refs_1_, bf16[16,512]{1,0:T(8,128)(2,1)S(1)} %collective-permute-done.1.refs_2_, bf16[16,512]{1,0:T(8,128)(2,1)S(1)} %collective-permute-done.2.refs_3_, ...), custom_call_target="tpu_custom_call" | custom-call | tf_op jit(solution)/shard_map/correlate/pallas_call | solution.py:246
  (2 shorter events, 0.0 us)
Async XLA Ops:
  1.7 3.8 %collective-permute-start.3 = (bf16[16,512]{1,0:T(8,128)(2,1)S(1)}, bf16[16,512]{1,0:T(8,128)(2,1)S(1)}, u32[]{:S(2)}, u32[]{:S(2)}) collective-permute-start(bf16[16,512]{1,0:T(8,128)(2,1)S(1)} %get-tuple-element.7.refs_0_), channel_id=1, source_target_pairs={{0,6},{1,7},{2,4},{3,5},{4,2},{5,3},{6,0},{7,1},{8,14},{9,15},{10,... | collective-permute-start | bytes 49160 | tf_op jit(solution)/shard_map/ppermute | solution.py:261
  2.2 8.3 %collective-permute-start = (bf16[16,512]{1,0:T(8,128)(2,1)S(1)}, bf16[16,512]{1,0:T(8,128)(2,1)S(1)}, u32[]{:S(2)}, u32[]{:S(2)}) collective-permute-start(bf16[16,512]{1,0:T(8,128)(2,1)S(1)} %get-tuple-element.7.refs_0_), channel_id=1, source_target_pairs={{0,16},{8,24},{16,0},{24,8},{1,17},{9,25},{17,1},{25,9},{2,18},{10... | collective-permute-start | bytes 49160 | tf_op jit(solution)/shard_map/ppermute | solution.py:261
  5.5 6.4 %collective-permute-start.6 = (bf16[32,512]{1,0:T(8,128)(2,1)S(1)}, bf16[32,512]{1,0:T(8,128)(2,1)S(1)}, u32[]{:S(2)}, u32[]{:S(2)}) collective-permute-start(bf16[32,512]{1,0:T(8,128)(2,1)S(1)} %constant_dynamic-update-slice_fusion.refs_4_), channel_id=1, source_target_pairs={{0,3},{1,2},{2,1},{3,0},{4,7},{5,6},{6,5},{7,4},{8,11},{9,10},{10,... | collective-permute-start | bytes 98312 | tf_op jit(solution)/shard_map/ppermute | solution.py:261
  8.9 3.9 %collective-permute-start.5 = (bf16[32,512]{1,0:T(8,128)(2,1)S(1)}, bf16[32,512]{1,0:T(8,128)(2,1)S(1)}, u32[]{:S(2)}, u32[]{:S(2)}) collective-permute-start(bf16[32,512]{1,0:T(8,128)(2,1)S(1)} %constant_dynamic-update-slice_fusion.refs_4_), channel_id=1, source_target_pairs={{0,1},{1,0},{2,3},{3,2},{4,5},{5,4},{6,7},{7,6},{8,9},{9,8},{10,11... | collective-permute-start | bytes 98312 | tf_op jit(solution)/shard_map/ppermute | solution.py:261
  10.5 3.9 %collective-permute-start.4 = (bf16[32,512]{1,0:T(8,128)(2,1)S(1)}, bf16[32,512]{1,0:T(8,128)(2,1)S(1)}, u32[]{:S(2)}, u32[]{:S(2)}) collective-permute-start(bf16[32,512]{1,0:T(8,128)(2,1)S(1)} %constant_dynamic-update-slice_fusion.refs_4_), channel_id=1, source_target_pairs={{0,2},{1,3},{2,0},{3,1},{4,6},{5,7},{6,4},{7,5},{8,10},{9,11},{10,... | collective-permute-start | bytes 98312 | tf_op jit(solution)/shard_map/ppermute | solution.py:261
  10.5 1.2 %collective-permute-start.1 = (bf16[16,512]{1,0:T(8,128)(2,1)S(1)}, bf16[16,512]{1,0:T(8,128)(2,1)S(1)}, u32[]{:S(2)}, u32[]{:S(2)}) collective-permute-start(bf16[16,512]{1,0:T(8,128)(2,1)S(1)} %get-tuple-element.7.refs_0_), channel_id=1, source_target_pairs={{0,8},{8,0},{16,24},{24,16},{1,9},{9,1},{17,25},{25,17},{2,10},{10... | collective-permute-start | bytes 49160 | tf_op jit(solution)/shard_map/ppermute | solution.py:261
  10.6 1.3 %collective-permute-start.2 = (bf16[16,512]{1,0:T(8,128)(2,1)S(1)}, bf16[16,512]{1,0:T(8,128)(2,1)S(1)}, u32[]{:S(2)}, u32[]{:S(2)}) collective-permute-start(bf16[16,512]{1,0:T(8,128)(2,1)S(1)} %collective-permute-done.refs_1_), channel_id=1, source_target_pairs={{0,8},{8,0},{16,24},{24,16},{1,9},{9,1},{17,25},{25,17},{2,10},{10... | collective-permute-start | bytes 49160 | tf_op jit(solution)/shard_map/ppermute | solution.py:261

commit v3 on v1

v3 whole, which is shorter than its diff:
```python
import functools
import math

import jax
import jax.numpy as jnp
import numpy as np
from jax import lax
from jax.experimental import pallas as pl
from jax.experimental.pallas import tpu as pltpu
from jax.sharding import PartitionSpec as P

SEG = 8
SAMPLES = 1024
BINS = 256
LAGS = 512
QUARTER = SAMPLES // 4
EIGHTH = SAMPLES // 8
LANES = 128
VMEM = pl.BlockSpec(memory_space=pltpu.VMEM)
SMEM = pl.BlockSpec(memory_space=pltpu.SMEM)


def split(values):
    high = values.astype(jnp.bfloat16)
    return high, (values - high.astype(jnp.float32)).astype(jnp.bfloat16)


def split_table(table):
    high = table.astype(jnp.bfloat16)
    return np.stack([high, (table - high.astype(np.float64)).astype(jnp.bfloat16)])


def eighth_table():
    times = np.arange(EIGHTH)
    freqs = np.arange(BINS) + 1
    phase = (times[:, None] * freqs[None, :] % SAMPLES) * (2.0 * math.pi / SAMPLES)
    return split_table(np.concatenate([np.cos(phase), -np.sin(phase)], axis=1))


def wave_rows():
    times = np.arange(SAMPLES) * (2.0 * math.pi / SAMPLES)
    freqs = np.arange(BINS) + 1
    eighth = (freqs % 8) * (math.pi / 4.0)
    cos_turn = np.array([1.0, 0.0, -1.0, 0.0])[freqs % 4]
    sin_turn = np.array([0.0, 1.0, 0.0, -1.0])[freqs % 4]
    taper = (0.5 - 0.5 * np.cos(times)).reshape(4, QUARTER)
    return np.stack([*taper, cos_turn, sin_turn, np.cos(eighth), np.sin(eighth)]).astype(np.float32)


def lag_table():
    freqs = np.arange(BINS) + 1
    shifts = np.arange(LAGS) - LAGS // 2
    phase = (freqs[:, None] * shifts[None, :] % SAMPLES) * (2.0 * math.pi / SAMPLES)
    table = np.concatenate([np.cos(phase), -np.sin(phase)], axis=0)
    return (table / math.sqrt(SEG * BINS)).astype(jnp.bfloat16)


def in_vmem(array):
    return pltpu.with_memory_space_constraint(array, pltpu.VMEM)


def dot(left, right):
    return jnp.dot(left, right, preferred_element_type=jnp.float32)


def whiten_kernel(offsets, band_lo, band_hi, live, traces, waves, table, out, quarters):
    count = traces.shape[0]
    rows = count * SEG
    for k in range(count):
        for s in range(SEG):
            start = pl.multiple_of(offsets[k, s], QUARTER)
            segment = traces[pl.ds(k, 1), pl.ds(start, SAMPLES)]
            for q in range(4):
                quarters[pl.ds(q * rows + k * SEG + s, 1), :] = segment[
                    :, q * QUARTER : (q + 1) * QUARTER
                ]
    parts = jnp.concatenate(
        [quarters[q * rows : (q + 1) * rows, :] * waves[q : q + 1, :] for q in range(4)], axis=0
    )
    high, low = split(jnp.concatenate([parts[:, :EIGHTH], parts[:, EIGHTH:]], axis=0))
    spectra = dot(
        jnp.concatenate([high, low, high], axis=1),
        jnp.concatenate([table[0], table[0], table[1]], axis=0),
    )
    cos_turn, sin_turn = waves[4:5, :], waves[5:6, :]
    sign = cos_turn * cos_turn - sin_turn * sin_turn

    def turned(n):
        quarter = [spectra[(n + q) * rows : (n + q + 1) * rows] for q in range(4)]
        re, im = [x[:, :BINS] for x in quarter], [x[:, BINS:] for x in quarter]
        return (
            (re[0] + re[2] * sign) + ((re[1] + re[3]) * cos_turn + (im[1] - im[3]) * sin_turn),
            (im[0] + im[2] * sign) + ((im[1] + im[3]) * cos_turn + (re[3] - re[1]) * sin_turn),
        )

    early_re, early_im = turned(0)
    late_re, late_im = turned(4)
    cos_eighth, sin_eighth = waves[6:7, :], waves[7:8, :]
    re = early_re + (late_re * cos_eighth + late_im * sin_eighth)
    im = early_im + (late_im * cos_eighth - late_re * sin_eighth)
    amp = jnp.sqrt(re * re + im * im)
    bins = lax.broadcasted_iota(jnp.int32, (1, BINS), 1)
    total = amp
    for step in (1, 2):
        total = total + jnp.where(bins >= step, pltpu.roll(amp, step, 1), 0.0)
        total = total + jnp.where(bins < BINS - step, pltpu.roll(amp, BINS - step, 1), 0.0)
    level = jnp.sum(amp, axis=1, keepdims=True) * (1.0 / BINS)
    factor = 1.0 / (total / 5.0 + 0.1 * level + 1e-06)
    keep = jnp.concatenate(
        [
            jnp.broadcast_to(
                jnp.where(
                    (bins >= band_lo[k]) & (bins < jnp.where(live[k] == 1, band_hi[k], 0)), 1.0, 0.0
                ),
                (SEG, BINS),
            )
            for k in range(count)
        ],
        axis=0,
    )
    factor = factor * keep
    out[:, :BINS] = (re * factor).astype(jnp.bfloat16)
    out[:, BINS:] = (im * factor).astype(jnp.bfloat16)


def whiten(traces, offsets, band_lo, band_hi, live):
    count = traces.shape[0]
    tables = (wave_rows(), eighth_table())
    return pl.pallas_call(
        whiten_kernel,
        out_shape=pltpu.VMEM((count * SEG, 2 * BINS), jnp.bfloat16),
        in_specs=[SMEM] * 4 + [VMEM] * 3,
        out_specs=VMEM,
        scratch_shapes=[pltpu.VMEM((4 * count * SEG, QUARTER), jnp.float32)],
        name="whiten",
    )(offsets, band_lo, band_hi, live, traces, *(jnp.asarray(table) for table in tables))


def cross_spectra(first_refs, left, right, cross, wide):
    at = 0
    for ref in first_refs:
        left[at : at + ref.shape[0], :] = ref[...].astype(jnp.float32)
        at += ref.shape[0]

    @pl.loop(0, left.shape[0] // SEG, unroll=4)
    def _(i):
        there = pl.ds(pl.multiple_of(i * wide, wide), wide)
        segments = pl.ds(pl.multiple_of(i * SEG, SEG), SEG)
        for t in range(BINS // LANES):
            re = pl.ds(t * LANES, LANES)
            im = pl.ds(BINS + t * LANES, LANES)
            cross_re = jnp.zeros((wide, LANES), jnp.float32)
            cross_im = jnp.zeros((wide, LANES), jnp.float32)
            rows_re, rows_im = left[segments, re], left[segments, im]
            for s in range(SEG):
                left_re, left_im = rows_re[s : s + 1, :], rows_im[s : s + 1, :]
                right_re = right[t, s * wide : (s + 1) * wide, :]
                right_im = right[t + BINS // LANES, s * wide : (s + 1) * wide, :]
                cross_re = cross_re + (left_re * right_re + left_im * right_im)
                cross_im = cross_im + (left_im * right_re - left_re * right_im)
            cross[there, re] = cross_re
            cross[there, im] = cross_im


def load_kernel(table, after, out, arrived):
    copy = pltpu.make_async_copy(table, out, arrived)
    copy.start()
    copy.wait()


def load_lags(after):
    table = lag_table()
    return pl.pallas_call(
        load_kernel,
        out_shape=pltpu.VMEM(table.shape, table.dtype),
        in_specs=[pl.BlockSpec(memory_space=pl.ANY), VMEM],
        out_specs=VMEM,
        scratch_shapes=[pltpu.SemaphoreType.DMA(())],
        name="load_lags",
    )(jnp.asarray(table), in_vmem(after))


def prepare_kernel(count, n_second, *refs):
    second_refs = refs[:n_second]
    *first_refs, right, cross, left = refs[n_second:]
    wide = count * n_second
    for n, ref in enumerate(second_refs):
        for k in range(count):
            rows = ref[k * SEG : (k + 1) * SEG, :].astype(jnp.float32)
            for t in range(2 * BINS // LANES):
                right[t, pl.ds(n * count + k, SEG, stride=wide), :] = rows[
                    :, t * LANES : (t + 1) * LANES
                ]
    cross_spectra(first_refs, left, right, cross, wide)


def prepare(count, second, first):
    wide = count * len(second)
    rows = sum(block.shape[0] for block in first)
    return pl.pallas_call(
        functools.partial(prepare_kernel, count, len(second)),
        out_shape=(
            pltpu.VMEM((2 * BINS // LANES, wide * SEG, LANES), jnp.float32),
            pltpu.VMEM((rows // SEG * wide, 2 * BINS), jnp.float32),
        ),
        in_specs=[VMEM] * (len(second) + len(first)),
        out_specs=(VMEM, VMEM),
        scratch_shapes=[pltpu.VMEM((rows, 2 * BINS), jnp.float32)],
        name="prepare",
    )(*(in_vmem(block) for block in (*second, *first)))


def correlate_kernel(count, bits, steps, row_masks, *refs):
    right, ready, table, *first_refs, out, left, cross = refs
    wide = count * len(row_masks)
    cross_spectra(first_refs, left, right, cross, wide)
    high, low = split(jnp.concatenate([ready[...], cross[...]], axis=0))
    corr = dot(
        jnp.concatenate([high, low], axis=1), jnp.concatenate([table[...], table[...]], axis=0)
    ).astype(jnp.bfloat16)
    row_index, col_index = lax.axis_index("row"), lax.axis_index("col")
    held = [col_index]
    for bit in bits:
        across = jnp.where(col_index & bit == 0, far(bit), bit)
        held += [col ^ across for col in held]
    at = 0
    for col in (col ^ step for step in steps for col in held):
        for k in range(count):
            for row_mask in row_masks:
                out[col * count + k, 0, row_index ^ row_mask] = corr[at : at + count, :]
                at += count


def correlate(count, n_row, n_col, bits, steps, row_masks, prepared, lags, first):
    channels, wide = count * n_col, count * n_row
    rows = sum(block.shape[0] for block in first)
    return pl.pallas_call(
        functools.partial(correlate_kernel, count, bits, steps, row_masks),
        out_shape=jax.ShapeDtypeStruct((channels, 1, n_row, count, LAGS), jnp.bfloat16),
        in_specs=[VMEM] * (3 + len(first)),
        out_specs=VMEM,
        scratch_shapes=[
            pltpu.VMEM((rows, 2 * BINS), jnp.float32),
            pltpu.VMEM((rows // SEG * wide, 2 * BINS), jnp.float32),
        ],
        name="correlate",
    )(*(in_vmem(block) for block in (*prepared, lags, *first)))


def swap(block, axis, mask):
    return lax.ppermute(block, axis, [(i, i ^ mask) for i in range(lax.axis_size(axis))])


def far(bit):
    return bit + bit // 2


def cross_over(block, bit):
    pairs = [(i, i ^ (far(bit) if i & bit else bit)) for i in range(lax.axis_size("col"))]
    return lax.ppermute(block, "col", pairs)


def body(traces, offsets, band_lo, band_hi, live):
    count = traces.shape[0]
    n_row, n_col = lax.axis_size("row"), lax.axis_size("col")
    white = whiten(traces, offsets, band_lo, band_hi, live)
    second, row_masks = [white], [0]
    bit = n_row // 2
    while bit:
        second += [swap(block, "row", bit) for block in second]
        row_masks += [mask ^ bit for mask in row_masks]
        bit //= 2
    held, bits = white, []
    bit = n_col // 2
    while bit > 2:
        held = jnp.concatenate([held, cross_over(held, bit)], axis=0)
        bits.append(bit)
        bit //= 2
    steps = [step for step in (3, 1, 2) if step < n_col]
    near = [swap(held, "col", step) for step in steps]
    prepared = prepare(count, second, [held, *near[:1]])
    lags = load_lags(second[1])
    return correlate(
        count, n_row, n_col, bits, [0, *steps[:1], *steps[:0:-1]], row_masks, prepared, lags, near[:0:-1]
    )


def solution(mesh):
    in_specs = (
        P(("row", "col"), None),
        P(("row", "col"), None),
        P(("row", "col")),
        P(("row", "col")),
        P(("row", "col")),
    )
    out_specs = P("row", "col", None, None, None)
    return jax.shard_map(body, mesh=mesh, in_specs=in_specs, out_specs=out_specs, check_vma=False)
```

time: 22 us -> 15.2 us (0.69)
  waiting for transfers between devices: 4.6 us -> 1.68 us
  Pallas kernels: 6.25 us -> 3.73 us
  other arithmetic: 0.72 us -> 0.01 us
  local copies, waits for them, and re-layouts: 0.62 us -> 0 us
    ppermute x7 -> x6, waiting for transfers between devices: 4.6 us -> 0.47 us  [swap(): lax.ppermute(block, axis, [(i, i ^ mask) for i in range(lax.axis_size(axi...]
    ppermute x0 -> x1, starting transfers between devices: none -> 4.08 us  [cross_over(): return lax.ppermute(block, 'col', pairs)]
    ppermute x7 -> x6, starting transfers between devices: 9.54 us -> 5.52 us  [swap(): lax.ppermute(block, axis, [(i, i ^ mask) for i in range(lax.axis_size(axi...]
    pallas_call x2 -> x4, Pallas kernels: 6.25 us -> 3.73 us  [the longest x1 1.37 us: whiten(): pl.pallas_call(whiten_kernel, out_shape=pltpu.VMEM((count * SEG, 2 * BINS...]
    ppermute x0 -> x1, waiting for transfers between devices: none -> 1.21 us  [cross_over(): return lax.ppermute(block, 'col', pairs)]
    concatenate x1, other arithmetic: 0.72 us -> 0.01 us  [body(): held = jnp.concatenate([held, cross_over(held, bit)], axis=0)]
    unnamed x16 -> x0, local copies, waits for them, and re-layouts: 0.62 us -> none
  transfers between devices with their start and end apart: 7 -> 7, of which waited for: 5 -> 2; matrix products, arithmetic and copies ran while one was open for 3% -> 0% of each run, Pallas kernels for 0% -> 8%
where the time goes in v3:
time: 15.2 us; the launch traced here: 15.1 us
  starting transfers between devices  9.6 us (63%)
  Pallas kernels  3.73 us (25%)
  waiting for transfers between devices  1.68 us (11%)
    ppermute x6, starting transfers between devices, swap(): lax.ppermute(block, axis, [(i, i ^ mask) for i in range(lax.axis_size(axi...  5.52 us
    ppermute x1, starting transfers between devices, cross_over(): return lax.ppermute(block, 'col', pairs)  4.08 us
    pallas_call x1, Pallas kernels, whiten(): pl.pallas_call(whiten_kernel, out_shape=pltpu.VMEM((count * SEG, 2 * BINS...  1.37 us
    ppermute x1, waiting for transfers between devices, cross_over(): return lax.ppermute(block, 'col', pairs)  1.21 us
    pallas_call x1, Pallas kernels, correlate(): pl.pallas_call(functools.partial(correlate_kernel, count, bits, steps, ro...  1.13 us
    pallas_call x1, Pallas kernels, load_lags(): pl.pallas_call(load_kernel, out_shape=pltpu.VMEM(table.shape, table.dtype...  1.05 us
    ppermute x6, waiting for transfers between devices, swap(): lax.ppermute(block, axis, [(i, i ^ mask) for i in range(lax.axis_size(axi...  0.47 us
  transfers between devices with their start and end apart: 7, of which 2 were waited for; matrix products, arithmetic and copies ran while one was open for 0% of the time, Pallas kernels for 8%

profile of v3, /device:TPU:0, one launch (start us, length us, event | category | flops | bytes accessed | tf_op | source)
XLA Modules:
  0.0 15.1 jit_solution(10523793028310630012)
XLA Ops:
  0.0 1.4 %whiten.1.refs_0_ = bf16[16,512]{1,0:T(8,128)(2,1)S(1)} custom-call(s32[2,8]{1,0:T(2,128)} %offsets.1, s32[2]{0:T(128)} %band_lo.1, s32[2]{0:T(128)} %band_hi.1, s32[2]{0:T(128)} %live.1, f32[2,4096]{1,0:T(2,128)} %traces.1, f32[8,256]{1,0:T(8,128)} %constant.6.clone.waves, bf16[2,128,512]{2,1,0:T(8,128)(2,1)} %constant.7.clone.table), custom_call_target="tpu_custom_call" | custom-call | tf_op jit(solution)/shard_map/whiten/pallas_call | solution.py:129
  1.4 4.1 %collective-permute-start.3 = (bf16[16,512]{1,0:T(8,128)(2,1)S(1)}, bf16[16,512]{1,0:T(8,128)(2,1)S(1)}, u32[]{:S(2)}, u32[]{:S(2)}) collective-permute-start(bf16[16,512]{1,0:T(8,128)(2,1)S(1)} %whiten.1.refs_0_), channel_id=1, source_target_pairs={{0,4},{1,5},{2,6},{3,7},{4,2},{5,3},{6,0},{7,1},{8,12},{9,13},{10,... | collective-permute-start | bytes 49160 | tf_op jit(solution)/shard_map/ppermute | solution.py:260
  5.5 1.5 %collective-permute-start = (bf16[16,512]{1,0:T(8,128)(2,1)S(1)}, bf16[16,512]{1,0:T(8,128)(2,1)S(1)}, u32[]{:S(2)}, u32[]{:S(2)}) collective-permute-start(bf16[16,512]{1,0:T(8,128)(2,1)S(1)} %whiten.1.refs_0_), channel_id=1, source_target_pairs={{0,16},{8,24},{16,0},{24,8},{1,17},{9,25},{17,1},{25,9},{2,18},{10... | collective-permute-start | bytes 49160 | tf_op jit(solution)/shard_map/ppermute | solution.py:251
  7.0 1.2 %collective-permute-done.3 = bf16[16,512]{1,0:T(8,128)(2,1)S(1)} collective-permute-done((bf16[16,512]{1,0:T(8,128)(2,1)S(1)}, bf16[16,512]{1,0:T(8,128)(2,1)S(1)}, u32[]{:S(2)}, u32[]{:S(2)}) %collective-permute-start.3) | collective-permute-done | bytes 16416 | tf_op jit(solution)/shard_map/ppermute | solution.py:260
  8.2 1.3 %collective-permute-start.4 = (bf16[32,512]{1,0:T(8,128)(2,1)S(1)}, bf16[32,512]{1,0:T(8,128)(2,1)S(1)}, u32[]{:S(2)}, u32[]{:S(2)}) collective-permute-start(bf16[32,512]{1,0:T(8,128)(2,1)S(1)} %pad_maximum_fusion.refs_4_), channel_id=1, source_target_pairs={{0,3},{1,2},{2,1},{3,0},{4,7},{5,6},{6,5},{7,4},{8,11},{9,10},{10,... | collective-permute-start | bytes 98312 | tf_op jit(solution)/shard_map/ppermute | solution.py:251
  9.5 0.5 %collective-permute-start.6 = (bf16[32,512]{1,0:T(8,128)(2,1)S(1)}, bf16[32,512]{1,0:T(8,128)(2,1)S(1)}, u32[]{:S(2)}, u32[]{:S(2)}) collective-permute-start(bf16[32,512]{1,0:T(8,128)(2,1)S(1)} %pad_maximum_fusion.refs_4_), channel_id=1, source_target_pairs={{0,1},{1,0},{2,3},{3,2},{4,5},{5,4},{6,7},{7,6},{8,9},{9,8},{10,11... | collective-permute-start | bytes 98312 | tf_op jit(solution)/shard_map/ppermute | solution.py:251
  10.0 1.7 %collective-permute-start.5 = (bf16[32,512]{1,0:T(8,128)(2,1)S(1)}, bf16[32,512]{1,0:T(8,128)(2,1)S(1)}, u32[]{:S(2)}, u32[]{:S(2)}) collective-permute-start(bf16[32,512]{1,0:T(8,128)(2,1)S(1)} %pad_maximum_fusion.refs_4_), channel_id=1, source_target_pairs={{0,2},{1,3},{2,0},{3,1},{4,6},{5,7},{6,4},{7,5},{8,10},{9,11},{10,... | collective-permute-start | bytes 98312 | tf_op jit(solution)/shard_map/ppermute | solution.py:251
  11.7 0.0 collective-permute-start.1
  11.7 0.0 collective-permute-done.refs_1_.after
  11.7 0.5 %collective-permute-start.2 = (bf16[16,512]{1,0:T(8,128)(2,1)S(1)}, bf16[16,512]{1,0:T(8,128)(2,1)S(1)}, u32[]{:S(2)}, u32[]{:S(2)}) collective-permute-start(bf16[16,512]{1,0:T(8,128)(2,1)S(1)} %collective-permute-done.refs_1_.after), channel_id=1, source_target_pairs={{0,8},{8,0},{16,24},{24,16},{1,9},{9,1},{17,25},{25,17},{2,10},{10... | collective-permute-start | bytes 49160 | tf_op jit(solution)/shard_map/ppermute | solution.py:251
  12.2 1.0 %load_lags.1.refs_2_ = bf16[512,512]{1,0:T(8,128)(2,1)S(1)} custom-call(bf16[512,512]{1,0:T(8,128)(2,1)} %constant.8.clone.table, bf16[16,512]{1,0:T(8,128)(2,1)S(1)} %collective-permute-done.refs_1_.after), custom_call_target="tpu_custom_call" | custom-call | tf_op jit(solution)/shard_map/load_lags/pallas_call | solution.py:173
  13.3 0.0 collective-permute-done.1.refs_2_
  13.3 0.0 collective-permute-done.2.refs_3_
  13.3 0.0 collective-permute-done.4.refs_5_
  13.3 0.2 %prepare.1 = (f32[4,64,128]{2,1,0:T(8,128)S(1)}, f32[64,512]{1,0:T(8,128)S(1)}) custom-call(bf16[16,512]{1,0:T(8,128)(2,1)S(1)} %whiten.1.refs_0_, bf16[16,512]{1,0:T(8,128)(2,1)S(1)} %collective-permute-done.refs_1_.after, bf16[16,512]{1,0:T(8,128)(2,1)S(1)} %collective-permute-done.1.refs_2_, bf16[16,512]{1,0:T(8,128)(2,1)S(1)} %collective-permute-done.2.refs_3_, ...), custom_call_target="tpu_custom_call" | custom-call | tf_op jit(solution)/shard_map/prepare/pallas_call | solution.py:200
  13.5 0.0 collective-permute-done.6.refs_4_
  13.5 0.5 %collective-permute-done.5.refs_3_ = bf16[32,512]{1,0:T(8,128)(2,1)S(1)} collective-permute-done((bf16[32,512]{1,0:T(8,128)(2,1)S(1)}, bf16[32,512]{1,0:T(8,128)(2,1)S(1)}, u32[]{:S(2)}, u32[]{:S(2)}) %collective-permute-start.5) | collective-permute-done | bytes 32800 | tf_op jit(solution)/shard_map/ppermute | solution.py:251
  13.9 1.1 %correlate.1 = bf16[16,1,4,2,512]{4,3,2,1,0:T(2,128)(2,1)} custom-call(f32[4,64,128]{2,1,0:T(8,128)S(1)} %get-tuple-element.7.refs_0_, f32[64,512]{1,0:T(8,128)S(1)} %get-tuple-element.8.refs_1_, bf16[512,512]{1,0:T(8,128)(2,1)S(1)} %load_lags.1.refs_2_, bf16[32,512]{1,0:T(8,128)(2,1)S(1)} %collective-permute-done.5.refs_3_, ...), custom_call_target="tpu_custom_call" | custom-call | tf_op jit(solution)/shard_map/correlate/pallas_call | solution.py:237
  (1 shorter events, 0.0 us)
Async XLA Ops:
  1.4 6.8 %collective-permute-start.3 = (bf16[16,512]{1,0:T(8,128)(2,1)S(1)}, bf16[16,512]{1,0:T(8,128)(2,1)S(1)}, u32[]{:S(2)}, u32[]{:S(2)}) collective-permute-start(bf16[16,512]{1,0:T(8,128)(2,1)S(1)} %whiten.1.refs_0_), channel_id=1, source_target_pairs={{0,4},{1,5},{2,6},{3,7},{4,2},{5,3},{6,0},{7,1},{8,12},{9,13},{10,... | collective-permute-start | bytes 49160 | tf_op jit(solution)/shard_map/ppermute | solution.py:260
  5.5 6.2 %collective-permute-start = (bf16[16,512]{1,0:T(8,128)(2,1)S(1)}, bf16[16,512]{1,0:T(8,128)(2,1)S(1)}, u32[]{:S(2)}, u32[]{:S(2)}) collective-permute-start(bf16[16,512]{1,0:T(8,128)(2,1)S(1)} %whiten.1.refs_0_), channel_id=1, source_target_pairs={{0,16},{8,24},{16,0},{24,8},{1,17},{9,25},{17,1},{25,9},{2,18},{10... | collective-permute-start | bytes 49160 | tf_op jit(solution)/shard_map/ppermute | solution.py:251
  8.2 5.1 %collective-permute-start.4 = (bf16[32,512]{1,0:T(8,128)(2,1)S(1)}, bf16[32,512]{1,0:T(8,128)(2,1)S(1)}, u32[]{:S(2)}, u32[]{:S(2)}) collective-permute-start(bf16[32,512]{1,0:T(8,128)(2,1)S(1)} %pad_maximum_fusion.refs_4_), channel_id=1, source_target_pairs={{0,3},{1,2},{2,1},{3,0},{4,7},{5,6},{6,5},{7,4},{8,11},{9,10},{10,... | collective-permute-start | bytes 98312 | tf_op jit(solution)/shard_map/ppermute | solution.py:251
  9.5 4.0 %collective-permute-start.6 = (bf16[32,512]{1,0:T(8,128)(2,1)S(1)}, bf16[32,512]{1,0:T(8,128)(2,1)S(1)}, u32[]{:S(2)}, u32[]{:S(2)}) collective-permute-start(bf16[32,512]{1,0:T(8,128)(2,1)S(1)} %pad_maximum_fusion.refs_4_), channel_id=1, source_target_pairs={{0,1},{1,0},{2,3},{3,2},{4,5},{5,4},{6,7},{7,6},{8,9},{9,8},{10,11... | collective-permute-start | bytes 98312 | tf_op jit(solution)/shard_map/ppermute | solution.py:251
  10.0 3.9 %collective-permute-start.5 = (bf16[32,512]{1,0:T(8,128)(2,1)S(1)}, bf16[32,512]{1,0:T(8,128)(2,1)S(1)}, u32[]{:S(2)}, u32[]{:S(2)}) collective-permute-start(bf16[32,512]{1,0:T(8,128)(2,1)S(1)} %pad_maximum_fusion.refs_4_), channel_id=1, source_target_pairs={{0,2},{1,3},{2,0},{3,1},{4,6},{5,7},{6,4},{7,5},{8,10},{9,11},{10,... | collective-permute-start | bytes 98312 | tf_op jit(solution)/shard_map/ppermute | solution.py:251
  11.7 1.6 %collective-permute-start.1 = (bf16[16,512]{1,0:T(8,128)(2,1)S(1)}, bf16[16,512]{1,0:T(8,128)(2,1)S(1)}, u32[]{:S(2)}, u32[]{:S(2)}) collective-permute-start(bf16[16,512]{1,0:T(8,128)(2,1)S(1)} %whiten.1.refs_0_), channel_id=1, source_target_pairs={{0,8},{8,0},{16,24},{24,16},{1,9},{9,1},{17,25},{25,17},{2,10},{10... | collective-permute-start | bytes 49160 | tf_op jit(solution)/shard_map/ppermute | solution.py:251
  11.7 1.6 %collective-permute-start.2 = (bf16[16,512]{1,0:T(8,128)(2,1)S(1)}, bf16[16,512]{1,0:T(8,128)(2,1)S(1)}, u32[]{:S(2)}, u32[]{:S(2)}) collective-permute-start(bf16[16,512]{1,0:T(8,128)(2,1)S(1)} %collective-permute-done.refs_1_.after), channel_id=1, source_target_pairs={{0,8},{8,0},{16,24},{24,16},{1,9},{9,1},{17,25},{25,17},{2,10},{10... | collective-permute-start | bytes 49160 | tf_op jit(solution)/shard_map/ppermute | solution.py:251

commit v4 on v3

--- a/solution.py
+++ b/solution.py
@@ -177,12 +177,27 @@
         out_specs=VMEM,
         scratch_shapes=[pltpu.SemaphoreType.DMA(())],
         name="load_lags",
+        cost_estimate=pl.CostEstimate(flops=1000000000, bytes_accessed=10000000, transcendentals=0),
     )(jnp.asarray(table), in_vmem(after))
 
 
-def prepare_kernel(count, n_second, *refs):
+def correlations(cross, table, out, row_masks):
+    count = out.shape[3]
+    high, low = split(cross[...])
+    both = dot(jnp.concatenate([high, low], axis=0), table[...])
+    corr = (both[: high.shape[0]] + both[high.shape[0] :]).astype(jnp.bfloat16)
+    row_index = lax.axis_index("row")
+    at = 0
+    for i in range(out.shape[0]):
+        for row_mask in row_masks:
+            out[i, 0, row_index ^ row_mask] = corr[at : at + count, :]
+            at += count
+
+
+def prepare_kernel(count, row_masks, *refs):
+    n_second = len(row_masks)
     second_refs = refs[:n_second]
-    *first_refs, right, cross, left = refs[n_second:]
+    table, *first_refs, right, ready, left, cross = refs[n_second:]
     wide = count * n_second
     for n, ref in enumerate(second_refs):
         for k in range(count):
@@ -192,59 +207,93 @@
                     :, t * LANES : (t + 1) * LANES
                 ]
     cross_spectra(first_refs, left, right, cross, wide)
-
-
-def prepare(count, second, first):
-    wide = count * len(second)
+    correlations(cross, table, ready, row_masks)
+
+
+def prepare(count, row_masks, second, lags, first):
+    n_row = len(second)
     rows = sum(block.shape[0] for block in first)
     return pl.pallas_call(
-        functools.partial(prepare_kernel, count, len(second)),
+        functools.partial(prepare_kernel, count, row_masks),
         out_shape=(
-            pltpu.VMEM((2 * BINS // LANES, wide * SEG, LANES), jnp.float32),
-            pltpu.VMEM((rows // SEG * wide, 2 * BINS), jnp.float32),
+            pltpu.VMEM((2 * BINS // LANES, count * n_row * SEG, LANES), jnp.float32),
+            pltpu.VMEM((rows // SEG, 1, n_row, count, LAGS), jnp.bfloat16),
         ),
-        in_specs=[VMEM] * (len(second) + len(first)),
+        in_specs=[VMEM] * (len(second) + 1 + len(first)),
         out_specs=(VMEM, VMEM),
-        scratch_shapes=[pltpu.VMEM((rows, 2 * BINS), jnp.float32)],
+        scratch_shapes=[
+            pltpu.VMEM((rows, 2 * BINS), jnp.float32),
+            pltpu.VMEM((rows // SEG * count * n_row, 2 * BINS), jnp.float32),
+        ],
         name="prepare",
-    )(*(in_vmem(block) for block in (*second, *first)))
-
-
-def correlate_kernel(count, bits, steps, row_masks, *refs):
-    right, ready, table, *first_refs, out, left, cross = refs
-    wide = count * len(row_masks)
-    cross_spectra(first_refs, left, right, cross, wide)
-    high, low = split(jnp.concatenate([ready[...], cross[...]], axis=0))
-    corr = dot(
-        jnp.concatenate([high, low], axis=1), jnp.concatenate([table[...], table[...]], axis=0)
-    ).astype(jnp.bfloat16)
-    row_index, col_index = lax.axis_index("row"), lax.axis_index("col")
+    )(*(in_vmem(block) for block in (*second, lags, *first)))
+
+
+def stage_kernel(row_masks, right, table, *refs):
+    *first_refs, ready, left, cross = refs
+    cross_spectra(first_refs, left, right, cross, right.shape[1] // SEG)
+    correlations(cross, table, ready, row_masks)
+
+
+def stage(count, row_masks, right, lags, first):
+    n_row = len(row_masks)
+    rows = sum(block.shape[0] for block in first)
+    return pl.pallas_call(
+        functools.partial(stage_kernel, row_masks),
+        out_shape=pltpu.VMEM((rows // SEG, 1, n_row, count, LAGS), jnp.bfloat16),
+        in_specs=[VMEM] * (2 + len(first)),
+        out_specs=VMEM,
+        scratch_shapes=[
+            pltpu.VMEM((rows, 2 * BINS), jnp.float32),
+            pltpu.VMEM((rows // SEG * count * n_row, 2 * BINS), jnp.float32),
+        ],
+        name="stage",
+    )(*(in_vmem(block) for block in (right, lags, *first)))
+
+
+def correlate_kernel(count, n_ready, bits, steps, row_masks, *refs):
+    ready = refs[:n_ready]
+    right, table, *first_refs, out, left, cross, last, sent = refs[n_ready:]
+    col_index = lax.axis_index("col")
     held = [col_index]
     for bit in bits:
         across = jnp.where(col_index & bit == 0, far(bit), bit)
         held += [col ^ across for col in held]
-    at = 0
-    for col in (col ^ step for step in steps for col in held):
-        for k in range(count):
-            for row_mask in row_masks:
-                out[col * count + k, 0, row_index ^ row_mask] = corr[at : at + count, :]
-                at += count
-
-
-def correlate(count, n_row, n_col, bits, steps, row_masks, prepared, lags, first):
+    cols = [col ^ step for step in steps for col in held]
+    blocks = [
+        ref.at[pl.ds(at, count)] for ref in (*ready, last) for at in range(0, ref.shape[0], count)
+    ]
+    copies = [
+        pltpu.make_async_copy(block, out.at[pl.ds(col * count, count)], sent.at[n])
+        for n, (block, col) in enumerate(zip(blocks, cols, strict=True))
+    ]
+    early = len(blocks) - last.shape[0] // count
+    for copy in copies[:early]:
+        copy.start()
+    cross_spectra(first_refs, left, right, cross, count * len(row_masks))
+    correlations(cross, table, last, row_masks)
+    for copy in copies[early:]:
+        copy.start()
+    for copy in copies:
+        copy.wait()
+
+
+def correlate(count, n_row, n_col, bits, steps, row_masks, ready, right, lags, first):
     channels, wide = count * n_col, count * n_row
     rows = sum(block.shape[0] for block in first)
     return pl.pallas_call(
-        functools.partial(correlate_kernel, count, bits, steps, row_masks),
+        functools.partial(correlate_kernel, count, len(ready), bits, steps, row_masks),
         out_shape=jax.ShapeDtypeStruct((channels, 1, n_row, count, LAGS), jnp.bfloat16),
-        in_specs=[VMEM] * (3 + len(first)),
-        out_specs=VMEM,
+        in_specs=[VMEM] * (len(ready) + 2 + len(first)),
+        out_specs=pl.BlockSpec(memory_space=pl.ANY),
         scratch_shapes=[
             pltpu.VMEM((rows, 2 * BINS), jnp.float32),
             pltpu.VMEM((rows // SEG * wide, 2 * BINS), jnp.float32),
+            pltpu.VMEM((rows // SEG, 1, n_row, count, LAGS), jnp.bfloat16),
+            pltpu.SemaphoreType.DMA((n_col,)),
         ],
         name="correlate",
-    )(*(in_vmem(block) for block in (*prepared, lags, *first)))
+    )(*(in_vmem(block) for block in (*ready, right, lags, *first)))
 
 
 def swap(block, axis, mask):
@@ -278,10 +327,11 @@
         bit //= 2
     steps = [step for step in (3, 1, 2) if step < n_col]
     near = [swap(held, "col", step) for step in steps]
-    prepared = prepare(count, second, [held, *near[:1]])
-    lags = load_lags(second[1])
+    lags = load_lags(second[2])
+    right, *ready = prepare(count, row_masks, second, lags, [held, *near[:-2]])
+    ready += [stage(count, row_masks, right, lags, [block]) for block in near[-2:-1]]
     return correlate(
-        count, n_row, n_col, bits, [0, *steps[:1], *steps[:0:-1]], row_masks, prepared, lags, near[:0:-1]
+        count, n_row, n_col, bits, [0, *steps], row_masks, ready, right, lags, near[-1:]
     )
 
 

time: 15.2 us -> 15.1 us (level)
  starting transfers between devices: 9.6 us -> 9.1 us
  Pallas kernels: 3.73 us -> 4.06 us
    ppermute x6, starting transfers between devices: 5.52 us -> 5.01 us  [swap(): lax.ppermute(block, axis, [(i, i ^ mask) for i in range(lax.axis_size(axi...]
    pallas_call x2 -> x3, Pallas kernels: 1.31 us -> 1.64 us  [the longest x1 0.95 us: correlate(): pl.pallas_call(functools.partial(correlate_kernel, count, len(ready), bit...]
  transfers between devices with their start and end apart: 7 -> 7, of which waited for: 2 -> 4; matrix products, arithmetic and copies ran while one was open for 0% -> 0% of each run, Pallas kernels for 8% -> 12%
where the time goes in v4:
time: 15.1 us; the launch traced here: 14.9 us
  starting transfers between devices  9.1 us (60%)
  Pallas kernels  4.06 us (27%)
  waiting for transfers between devices  1.69 us (11%)
    ppermute x6, starting transfers between devices, swap(): lax.ppermute(block, axis, [(i, i ^ mask) for i in range(lax.axis_size(axi...  5.01 us
    ppermute x1, starting transfers between devices, cross_over(): return lax.ppermute(block, 'col', pairs)  4.08 us
    pallas_call x1, Pallas kernels, whiten(): pl.pallas_call(whiten_kernel, out_shape=pltpu.VMEM((count * SEG, 2 * BINS...  1.37 us
    ppermute x1, waiting for transfers between devices, cross_over(): return lax.ppermute(block, 'col', pairs)  1.21 us
    pallas_call x1, Pallas kernels, load_lags(): pl.pallas_call(load_kernel, out_shape=pltpu.VMEM(table.shape, table.dtype...  1.05 us
    pallas_call x1, Pallas kernels, correlate(): pl.pallas_call(functools.partial(correlate_kernel, count, len(ready), bit...  0.95 us
    ppermute x6, waiting for transfers between devices, swap(): lax.ppermute(block, axis, [(i, i ^ mask) for i in range(lax.axis_size(axi...  0.48 us
    pallas_call x1, Pallas kernels, prepare(): pl.pallas_call(functools.partial(prepare_kernel, count, row_masks), out_s...  0.41 us
  transfers between devices with their start and end apart: 7, of which 4 were waited for; matrix products, arithmetic and copies ran while one was open for 0% of the time, Pallas kernels for 12%

profile of v4, /device:TPU:0, one launch (start us, length us, event | category | flops | bytes accessed | tf_op | source)
XLA Modules:
  0.0 14.9 jit_solution(12684249839547331772)
XLA Ops:
  0.0 1.4 %whiten.1.refs_0_ = bf16[16,512]{1,0:T(8,128)(2,1)S(1)} custom-call(s32[2,8]{1,0:T(2,128)} %offsets.1, s32[2]{0:T(128)} %band_lo.1, s32[2]{0:T(128)} %band_hi.1, s32[2]{0:T(128)} %live.1, f32[2,4096]{1,0:T(2,128)} %traces.1, f32[8,256]{1,0:T(8,128)} %constant.6.clone.waves, bf16[2,128,512]{2,1,0:T(8,128)(2,1)} %constant.7.clone.table), custom_call_target="tpu_custom_call" | custom-call | tf_op jit(solution)/shard_map/whiten/pallas_call | solution.py:129
  1.4 4.1 %collective-permute-start.3 = (bf16[16,512]{1,0:T(8,128)(2,1)S(1)}, bf16[16,512]{1,0:T(8,128)(2,1)S(1)}, u32[]{:S(2)}, u32[]{:S(2)}) collective-permute-start(bf16[16,512]{1,0:T(8,128)(2,1)S(1)} %whiten.1.refs_0_), channel_id=1, source_target_pairs={{0,4},{1,5},{2,6},{3,7},{4,2},{5,3},{6,0},{7,1},{8,12},{9,13},{10,... | collective-permute-start | bytes 49160 | tf_op jit(solution)/shard_map/ppermute | solution.py:309
  5.5 0.0 collective-permute-start.1
  5.5 1.5 %collective-permute-start = (bf16[16,512]{1,0:T(8,128)(2,1)S(1)}, bf16[16,512]{1,0:T(8,128)(2,1)S(1)}, u32[]{:S(2)}, u32[]{:S(2)}) collective-permute-start(bf16[16,512]{1,0:T(8,128)(2,1)S(1)} %whiten.1.refs_0_), channel_id=1, source_target_pairs={{0,16},{8,24},{16,0},{24,8},{1,17},{9,25},{17,1},{25,9},{2,18},{10... | collective-permute-start | bytes 49160 | tf_op jit(solution)/shard_map/ppermute | solution.py:300
  7.0 1.2 %collective-permute-done.3 = bf16[16,512]{1,0:T(8,128)(2,1)S(1)} collective-permute-done((bf16[16,512]{1,0:T(8,128)(2,1)S(1)}, bf16[16,512]{1,0:T(8,128)(2,1)S(1)}, u32[]{:S(2)}, u32[]{:S(2)}) %collective-permute-start.3) | collective-permute-done | bytes 16416 | tf_op jit(solution)/shard_map/ppermute | solution.py:309
  8.2 1.3 %collective-permute-start.4 = (bf16[32,512]{1,0:T(8,128)(2,1)S(1)}, bf16[32,512]{1,0:T(8,128)(2,1)S(1)}, u32[]{:S(2)}, u32[]{:S(2)}) collective-permute-start(bf16[32,512]{1,0:T(8,128)(2,1)S(1)} %pad_maximum_fusion.refs_5_), channel_id=1, source_target_pairs={{0,3},{1,2},{2,1},{3,0},{4,7},{5,6},{6,5},{7,4},{8,11},{9,10},{10,... | collective-permute-start | bytes 98312 | tf_op jit(solution)/shard_map/ppermute | solution.py:300
  9.5 0.5 %collective-permute-start.5 = (bf16[32,512]{1,0:T(8,128)(2,1)S(1)}, bf16[32,512]{1,0:T(8,128)(2,1)S(1)}, u32[]{:S(2)}, u32[]{:S(2)}) collective-permute-start(bf16[32,512]{1,0:T(8,128)(2,1)S(1)} %pad_maximum_fusion.refs_5_), channel_id=1, source_target_pairs={{0,1},{1,0},{2,3},{3,2},{4,5},{5,4},{6,7},{7,6},{8,9},{9,8},{10,11... | collective-permute-start | bytes 98312 | tf_op jit(solution)/shard_map/ppermute | solution.py:300
  10.0 1.7 %collective-permute-start.6 = (bf16[32,512]{1,0:T(8,128)(2,1)S(1)}, bf16[32,512]{1,0:T(8,128)(2,1)S(1)}, u32[]{:S(2)}, u32[]{:S(2)}) collective-permute-start(bf16[32,512]{1,0:T(8,128)(2,1)S(1)} %pad_maximum_fusion.refs_5_), channel_id=1, source_target_pairs={{0,2},{1,3},{2,0},{3,1},{4,6},{5,7},{6,4},{7,5},{8,10},{9,11},{10,... | collective-permute-start | bytes 98312 | tf_op jit(solution)/shard_map/ppermute | solution.py:300
  11.7 0.0 collective-permute-done.refs_1_
  11.7 0.0 collective-permute-start.2
  11.7 0.0 collective-permute-done.1.after.refs_2_
  11.7 1.1 %load_lags.1.refs_4_.table.refs_3_ = bf16[512,512]{1,0:T(8,128)(2,1)S(1)} custom-call(bf16[512,512]{1,0:T(8,128)(2,1)} %constant.8.clone.table, bf16[16,512]{1,0:T(8,128)(2,1)S(1)} %collective-permute-done.1.after.refs_2_), custom_call_target="tpu_custom_call" | custom-call | flops 1000000000 | bytes 10000000 | tf_op jit(solution)/shard_map/load_lags/pallas_call | solution.py:173
  12.8 0.1 collective-permute-done.2.refs_3_
  12.9 0.1 collective-permute-done.4.refs_6_
  13.0 0.4 %prepare.1 = (f32[4,64,128]{2,1,0:T(8,128)S(1)}, bf16[8,1,4,2,512]{4,3,2,1,0:T(2,128)(2,1)S(1)}) custom-call(bf16[16,512]{1,0:T(8,128)(2,1)S(1)} %whiten.1.refs_0_, bf16[16,512]{1,0:T(8,128)(2,1)S(1)} %collective-permute-done.refs_1_, bf16[16,512]{1,0:T(8,128)(2,1)S(1)} %collective-permute-done.1.after.refs_2_, ...), custom_call_target="tpu_custom_call" | custom-call | tf_op jit(solution)/shard_map/prepare/pallas_call | solution.py:216
  13.4 0.0 collective-permute-done.5.refs_0_
  13.4 0.3 %stage.1.refs_1_ = bf16[4,1,4,2,512]{4,3,2,1,0:T(2,128)(2,1)S(1)} custom-call(f32[4,64,128]{2,1,0:T(8,128)S(1)} %get-tuple-element.8.right.refs_2_, bf16[512,512]{1,0:T(8,128)(2,1)S(1)} %load_lags.1.refs_4_.table.refs_3_, bf16[32,512]{1,0:T(8,128)(2,1)S(1)} %collective-permute-done.5.refs_0_), custom_call_target="tpu_custom_call" | custom-call | tf_op jit(solution)/shard_map/stage/pallas_call | solution.py:241
  13.7 0.2 %collective-permute-done.6.refs_4_ = bf16[32,512]{1,0:T(8,128)(2,1)S(1)} collective-permute-done((bf16[32,512]{1,0:T(8,128)(2,1)S(1)}, bf16[32,512]{1,0:T(8,128)(2,1)S(1)}, u32[]{:S(2)}, u32[]{:S(2)}) %collective-permute-start.6) | collective-permute-done | bytes 32800 | tf_op jit(solution)/shard_map/ppermute | solution.py:300
  13.9 1.0 %correlate.1 = bf16[16,1,4,2,512]{4,3,2,1,0:T(2,128)(2,1)} custom-call(bf16[8,1,4,2,512]{4,3,2,1,0:T(2,128)(2,1)S(1)} %get-tuple-element.7.refs_0_, bf16[4,1,4,2,512]{4,3,2,1,0:T(2,128)(2,1)S(1)} %stage.1.refs_1_, f32[4,64,128]{2,1,0:T(8,128)S(1)} %get-tuple-element.8.right.refs_2_, bf16[512,512]{1,0:T(8,128)(2,1)S(1)} %load_lags.1.refs_4_.table.refs_3_, ...), custom_call_target="tpu_custom_call" | custom-call | tf_op jit(solution)/shard_map/correlate/pallas_call | solution.py:284
  (1 shorter events, 0.0 us)
Async XLA Ops:
  1.4 6.8 %collective-permute-start.3 = (bf16[16,512]{1,0:T(8,128)(2,1)S(1)}, bf16[16,512]{1,0:T(8,128)(2,1)S(1)}, u32[]{:S(2)}, u32[]{:S(2)}) collective-permute-start(bf16[16,512]{1,0:T(8,128)(2,1)S(1)} %whiten.1.refs_0_), channel_id=1, source_target_pairs={{0,4},{1,5},{2,6},{3,7},{4,2},{5,3},{6,0},{7,1},{8,12},{9,13},{10,... | collective-permute-start | bytes 49160 | tf_op jit(solution)/shard_map/ppermute | solution.py:309
  5.5 6.2 %collective-permute-start.1 = (bf16[16,512]{1,0:T(8,128)(2,1)S(1)}, bf16[16,512]{1,0:T(8,128)(2,1)S(1)}, u32[]{:S(2)}, u32[]{:S(2)}) collective-permute-start(bf16[16,512]{1,0:T(8,128)(2,1)S(1)} %whiten.1.refs_0_), channel_id=1, source_target_pairs={{0,8},{8,0},{16,24},{24,16},{1,9},{9,1},{17,25},{25,17},{2,10},{10... | collective-permute-start | bytes 49160 | tf_op jit(solution)/shard_map/ppermute | solution.py:300
  5.5 6.2 %collective-permute-start = (bf16[16,512]{1,0:T(8,128)(2,1)S(1)}, bf16[16,512]{1,0:T(8,128)(2,1)S(1)}, u32[]{:S(2)}, u32[]{:S(2)}) collective-permute-start(bf16[16,512]{1,0:T(8,128)(2,1)S(1)} %whiten.1.refs_0_), channel_id=1, source_target_pairs={{0,16},{8,24},{16,0},{24,8},{1,17},{9,25},{17,1},{25,9},{2,18},{10... | collective-permute-start | bytes 49160 | tf_op jit(solution)/shard_map/ppermute | solution.py:300
  8.2 4.8 %collective-permute-start.4 = (bf16[32,512]{1,0:T(8,128)(2,1)S(1)}, bf16[32,512]{1,0:T(8,128)(2,1)S(1)}, u32[]{:S(2)}, u32[]{:S(2)}) collective-permute-start(bf16[32,512]{1,0:T(8,128)(2,1)S(1)} %pad_maximum_fusion.refs_5_), channel_id=1, source_target_pairs={{0,3},{1,2},{2,1},{3,0},{4,7},{5,6},{6,5},{7,4},{8,11},{9,10},{10,... | collective-permute-start | bytes 98312 | tf_op jit(solution)/shard_map/ppermute | solution.py:300
  9.5 3.9 %collective-permute-start.5 = (bf16[32,512]{1,0:T(8,128)(2,1)S(1)}, bf16[32,512]{1,0:T(8,128)(2,1)S(1)}, u32[]{:S(2)}, u32[]{:S(2)}) collective-permute-start(bf16[32,512]{1,0:T(8,128)(2,1)S(1)} %pad_maximum_fusion.refs_5_), channel_id=1, source_target_pairs={{0,1},{1,0},{2,3},{3,2},{4,5},{5,4},{6,7},{7,6},{8,9},{9,8},{10,11... | collective-permute-start | bytes 98312 | tf_op jit(solution)/shard_map/ppermute | solution.py:300
  10.0 3.9 %collective-permute-start.6 = (bf16[32,512]{1,0:T(8,128)(2,1)S(1)}, bf16[32,512]{1,0:T(8,128)(2,1)S(1)}, u32[]{:S(2)}, u32[]{:S(2)}) collective-permute-start(bf16[32,512]{1,0:T(8,128)(2,1)S(1)} %pad_maximum_fusion.refs_5_), channel_id=1, source_target_pairs={{0,2},{1,3},{2,0},{3,1},{4,6},{5,7},{6,4},{7,5},{8,10},{9,11},{10,... | collective-permute-start | bytes 98312 | tf_op jit(solution)/shard_map/ppermute | solution.py:300
  11.7 1.2 %collective-permute-start.2 = (bf16[16,512]{1,0:T(8,128)(2,1)S(1)}, bf16[16,512]{1,0:T(8,128)(2,1)S(1)}, u32[]{:S(2)}, u32[]{:S(2)}) collective-permute-start(bf16[16,512]{1,0:T(8,128)(2,1)S(1)} %collective-permute-done.refs_1_), channel_id=1, source_target_pairs={{0,8},{8,0},{16,24},{24,16},{1,9},{9,1},{17,25},{25,17},{2,10},{10... | collective-permute-start | bytes 49160 | tf_op jit(solution)/shard_map/ppermute | solution.py:300

commit v5 on v4

--- a/solution.py
+++ b/solution.py
@@ -162,23 +162,20 @@
             cross[there, im] = cross_im
 
 
-def load_kernel(table, after, out, arrived):
-    copy = pltpu.make_async_copy(table, out, arrived)
-    copy.start()
-    copy.wait()
-
-
-def load_lags(after):
-    table = lag_table()
-    return pl.pallas_call(
-        load_kernel,
-        out_shape=pltpu.VMEM(table.shape, table.dtype),
-        in_specs=[pl.BlockSpec(memory_space=pl.ANY), VMEM],
+def join_kernel(own, other, out):
+    out[: own.shape[0], :] = own[...]
+    out[own.shape[0] :, :] = other[...]
+
+
+def join(own, other, cost=10**6):
+    return pl.pallas_call(
+        join_kernel,
+        out_shape=pltpu.VMEM((own.shape[0] + other.shape[0], own.shape[1]), own.dtype),
+        in_specs=[VMEM] * 2,
         out_specs=VMEM,
-        scratch_shapes=[pltpu.SemaphoreType.DMA(())],
-        name="load_lags",
-        cost_estimate=pl.CostEstimate(flops=1000000000, bytes_accessed=10000000, transcendentals=0),
-    )(jnp.asarray(table), in_vmem(after))
+        cost_estimate=pl.CostEstimate(flops=cost, bytes_accessed=cost // 100, transcendentals=0),
+        name="join",
+    )(in_vmem(own), in_vmem(other))
 
 
 def correlations(cross, table, out, row_masks):
@@ -194,27 +191,26 @@
             at += count
 
 
-def prepare_kernel(count, row_masks, *refs):
-    n_second = len(row_masks)
+def prepare_kernel(count, n_second, row_masks, *refs):
     second_refs = refs[:n_second]
     table, *first_refs, right, ready, left, cross = refs[n_second:]
-    wide = count * n_second
-    for n, ref in enumerate(second_refs):
-        for k in range(count):
-            rows = ref[k * SEG : (k + 1) * SEG, :].astype(jnp.float32)
+    wide = count * len(row_masks)
+    n = 0
+    for ref in second_refs:
+        for at in range(0, ref.shape[0], SEG):
+            rows = ref[at : at + SEG, :].astype(jnp.float32)
             for t in range(2 * BINS // LANES):
-                right[t, pl.ds(n * count + k, SEG, stride=wide), :] = rows[
-                    :, t * LANES : (t + 1) * LANES
-                ]
+                right[t, pl.ds(n, SEG, stride=wide), :] = rows[:, t * LANES : (t + 1) * LANES]
+            n += 1
     cross_spectra(first_refs, left, right, cross, wide)
     correlations(cross, table, ready, row_masks)
 
 
 def prepare(count, row_masks, second, lags, first):
-    n_row = len(second)
+    n_row = len(row_masks)
     rows = sum(block.shape[0] for block in first)
     return pl.pallas_call(
-        functools.partial(prepare_kernel, count, row_masks),
+        functools.partial(prepare_kernel, count, len(second), row_masks),
         out_shape=(
             pltpu.VMEM((2 * BINS // LANES, count * n_row * SEG, LANES), jnp.float32),
             pltpu.VMEM((rows // SEG, 1, n_row, count, LAGS), jnp.bfloat16),
@@ -251,15 +247,11 @@
     )(*(in_vmem(block) for block in (right, lags, *first)))
 
 
-def correlate_kernel(count, n_ready, bits, steps, row_masks, *refs):
+def correlate_kernel(count, n_ready, moves, bits, row_masks, *refs):
     ready = refs[:n_ready]
     right, table, *first_refs, out, left, cross, last, sent = refs[n_ready:]
     col_index = lax.axis_index("col")
-    held = [col_index]
-    for bit in bits:
-        across = jnp.where(col_index & bit == 0, far(bit), bit)
-        held += [col ^ across for col in held]
-    cols = [col ^ step for step in steps for col in held]
+    cols = [at for source in sources(col_index, moves) for at in held_at(source, moves, bits)]
     blocks = [
         ref.at[pl.ds(at, count)] for ref in (*ready, last) for at in range(0, ref.shape[0], count)
     ]
@@ -278,11 +270,11 @@
         copy.wait()
 
 
-def correlate(count, n_row, n_col, bits, steps, row_masks, ready, right, lags, first):
+def correlate(count, n_row, n_col, moves, bits, row_masks, ready, right, lags, first):
     channels, wide = count * n_col, count * n_row
     rows = sum(block.shape[0] for block in first)
     return pl.pallas_call(
-        functools.partial(correlate_kernel, count, len(ready), bits, steps, row_masks),
+        functools.partial(correlate_kernel, count, len(ready), moves, bits, row_masks),
         out_shape=jax.ShapeDtypeStruct((channels, 1, n_row, count, LAGS), jnp.bfloat16),
         in_specs=[VMEM] * (len(ready) + 2 + len(first)),
         out_specs=pl.BlockSpec(memory_space=pl.ANY),
@@ -300,13 +292,37 @@
     return lax.ppermute(block, axis, [(i, i ^ mask) for i in range(lax.axis_size(axis))])
 
 
-def far(bit):
-    return bit + bit // 2
-
-
-def cross_over(block, bit):
-    pairs = [(i, i ^ (far(bit) if i & bit else bit)) for i in range(lax.axis_size("col"))]
+def moves_of(n_col):
+    if n_col >= 8:
+        return ((4, 1), (3, 6), (1, 4), (2, 2))
+    return ((0, 0), *((step, step) for step in (3, 1, 2) if step < n_col))
+
+
+def move(block, masks):
+    pairs = [(i, i ^ masks[i // 2 % 2]) for i in range(lax.axis_size("col"))]
     return lax.ppermute(block, "col", pairs)
+
+
+def sent_from(col, masks):
+    clear, set_ = masks if clear_stays(masks) else masks[::-1]
+    return col ^ jnp.where(col & 2 == 0, clear, set_)
+
+
+def clear_stays(masks):
+    return masks[0] & 2 == 0
+
+
+def sources(col, moves):
+    return [col] + [sent_from(col, masks) for masks in moves[1:]]
+
+
+def held_at(col, moves, bits):
+    held = [col]
+    for bit in bits:
+        held += [at ^ bit for at in held]
+    if moves[0] != (0, 0):
+        held += [at ^ sent_from(col, moves[0]) ^ col for at in held]
+    return held
 
 
 def body(traces, offsets, band_lo, band_hi, live):
@@ -314,25 +330,28 @@
     n_row, n_col = lax.axis_size("row"), lax.axis_size("col")
     white = whiten(traces, offsets, band_lo, band_hi, live)
     second, row_masks = [white], [0]
-    bit = n_row // 2
-    while bit:
-        second += [swap(block, "row", bit) for block in second]
+    bit = 1
+    while bit < n_row:
+        mine = second[0] if len(second) == 1 else join(*second)
+        second = [mine, swap(mine, "row", bit)]
         row_masks += [mask ^ bit for mask in row_masks]
-        bit //= 2
+        bit *= 2
     held, bits = white, []
     bit = n_col // 2
-    while bit > 2:
-        held = jnp.concatenate([held, cross_over(held, bit)], axis=0)
+    while bit > 4:
+        held = join(held, swap(held, "col", bit))
         bits.append(bit)
         bit //= 2
-    steps = [step for step in (3, 1, 2) if step < n_col]
-    near = [swap(held, "col", step) for step in steps]
-    lags = load_lags(second[2])
-    right, *ready = prepare(count, row_masks, second, lags, [held, *near[:-2]])
-    ready += [stage(count, row_masks, right, lags, [block]) for block in near[-2:-1]]
-    return correlate(
-        count, n_row, n_col, bits, [0, *steps], row_masks, ready, right, lags, near[-1:]
-    )
+    moves = moves_of(n_col)
+    if moves[0] != (0, 0):
+        held = join(held, move(held, moves[0]), 10**9)
+    near = [move(held, masks) for masks in moves[1:]]
+    lags = jnp.asarray(lag_table())
+    right, *ready = prepare(count, row_masks, second, lags, [held])
+    if len(near) > 1:
+        ready += [stage(count, row_masks, right, lags, near[-2::-1])]
+    order = (moves[0], *moves[-2:0:-1], moves[-1])
+    return correlate(count, n_row, n_col, order, bits, row_masks, ready, right, lags, near[-1:])
 
 
 def solution(mesh):

time: 15.1 us -> 14.8 us (0.980)
  starting transfers between devices: 9.1 us -> 10.2 us
  Pallas kernels: 4.06 us -> 3.01 us
  waiting for transfers between devices: 1.69 us -> 1.44 us
    ppermute x1 -> x4, starting transfers between devices: 4.08 us -> 8.05 us  [move(): return lax.ppermute(block, 'col', pairs)]
    ppermute x6 -> x2, starting transfers between devices: 5.01 us -> 2.1 us  [swap(): lax.ppermute(block, axis, [(i, i ^ mask) for i in range(lax.axis_size(axi...]
    pallas_call x3 -> x4, Pallas kernels: 2.42 us -> 1.24 us  [the longest x1 0.96 us: correlate(): pl.pallas_call(functools.partial(correlate_kernel, count, len(ready), mov...]
    ppermute x6 -> x2, waiting for transfers between devices: 0.48 us -> 0.01 us  [swap(): lax.ppermute(block, axis, [(i, i ^ mask) for i in range(lax.axis_size(axi...]
    ppermute x1 -> x4, waiting for transfers between devices: 1.21 us -> 1.44 us  [move(): return lax.ppermute(block, 'col', pairs)]
  transfers between devices with their start and end apart: 7 -> 6, of which waited for: 4 -> 2; matrix products, arithmetic and copies ran while one was open for 0% -> 0% of each run, Pallas kernels for 12% -> 5%
where the time goes in v5:
time: 14.8 us; the launch traced here: 14.6 us
  starting transfers between devices  10.2 us (69%)
  Pallas kernels  3.01 us (20%)
  waiting for transfers between devices  1.44 us (10%)
    ppermute x4, starting transfers between devices, move(): return lax.ppermute(block, 'col', pairs)  8.05 us
    ppermute x2, starting transfers between devices, swap(): lax.ppermute(block, axis, [(i, i ^ mask) for i in range(lax.axis_size(axi...  2.1 us
    ppermute x4, waiting for transfers between devices, move(): return lax.ppermute(block, 'col', pairs)  1.44 us
    pallas_call x1, Pallas kernels, whiten(): pl.pallas_call(whiten_kernel, out_shape=pltpu.VMEM((count * SEG, 2 * BINS...  1.37 us
    pallas_call x1, Pallas kernels, correlate(): pl.pallas_call(functools.partial(correlate_kernel, count, len(ready), mov...  0.96 us
    pallas_call x1, Pallas kernels, stage(): pl.pallas_call(functools.partial(stage_kernel, row_masks), out_shape=pltp...  0.4 us
  transfers between devices with their start and end apart: 6, of which 2 were waited for; matrix products, arithmetic and copies ran while one was open for 0% of the time, Pallas kernels for 5%

profile of v5, /device:TPU:0, one launch (start us, length us, event | category | flops | bytes accessed | tf_op | source)
XLA Modules:
  0.0 14.6 jit_solution(15445855995440448507)
XLA Ops:
  0.0 1.4 %whiten.1.own = bf16[16,512]{1,0:T(8,128)(2,1)S(1)} custom-call(s32[2,8]{1,0:T(2,128)} %offsets.1, s32[2]{0:T(128)} %band_lo.1, s32[2]{0:T(128)} %band_hi.1, s32[2]{0:T(128)} %live.1, f32[2,4096]{1,0:T(2,128)} %traces.1, f32[8,256]{1,0:T(8,128)} %constant.6.clone.waves, bf16[2,128,512]{2,1,0:T(8,128)(2,1)} %constant.7.clone.table), custom_call_target="tpu_custom_call" | custom-call | tf_op jit(solution)/shard_map/whiten/pallas_call | solution.py:129
  1.4 0.5 %collective-permute-start = (bf16[16,512]{1,0:T(8,128)(2,1)S(1)}, bf16[16,512]{1,0:T(8,128)(2,1)S(1)}, u32[]{:S(2)}, u32[]{:S(2)}) collective-permute-start(bf16[16,512]{1,0:T(8,128)(2,1)S(1)} %whiten.1.own), channel_id=1, source_target_pairs={{0,8},{8,0},{16,24},{24,16},{1,9},{9,1},{17,25},{25,17},{2,10},{10... | collective-permute-start | bytes 49160 | tf_op jit(solution)/shard_map/ppermute | solution.py:292
  1.9 3.7 %collective-permute-start.2 = (bf16[16,512]{1,0:T(8,128)(2,1)S(1)}, bf16[16,512]{1,0:T(8,128)(2,1)S(1)}, u32[]{:S(2)}, u32[]{:S(2)}) collective-permute-start(bf16[16,512]{1,0:T(8,128)(2,1)S(1)} %whiten.1.own), channel_id=1, source_target_pairs={{0,4},{1,5},{2,3},{3,2},{4,0},{5,1},{6,7},{7,6},{8,12},{9,13},{10,... | collective-permute-start | bytes 49160 | tf_op jit(solution)/shard_map/ppermute | solution.py:303
  5.6 0.0 collective-permute-done.other
  5.6 0.0 copy-start
  5.6 1.6 %collective-permute-start.1 = (bf16[32,512]{1,0:T(8,128)(2,1)S(1)}, bf16[32,512]{1,0:T(8,128)(2,1)S(1)}, u32[]{:S(2)}, u32[]{:S(2)}) collective-permute-start(bf16[32,512]{1,0:T(8,128)(2,1)S(1)} %join.2.refs_0_), channel_id=1, source_target_pairs={{0,16},{8,24},{16,0},{24,8},{1,17},{9,25},{17,1},{25,9},{2,18},{10... | collective-permute-start | bytes 98312 | tf_op jit(solution)/shard_map/ppermute | solution.py:292
  7.2 0.1 collective-permute-done.2.other
  7.3 1.9 %collective-permute-start.4 = (bf16[32,512]{1,0:T(8,128)(2,1)S(1)}, bf16[32,512]{1,0:T(8,128)(2,1)S(1)}, u32[]{:S(2)}, u32[]{:S(2)}) collective-permute-start(bf16[32,512]{1,0:T(8,128)(2,1)S(1)} %join.3.refs_3_), channel_id=1, source_target_pairs={{0,3},{1,2},{2,4},{3,5},{4,7},{5,6},{6,0},{7,1},{8,11},{9,10},{10,... | collective-permute-start | bytes 98312 | tf_op jit(solution)/shard_map/ppermute | solution.py:303
  9.2 0.5 %collective-permute-start.3 = (bf16[32,512]{1,0:T(8,128)(2,1)S(1)}, bf16[32,512]{1,0:T(8,128)(2,1)S(1)}, u32[]{:S(2)}, u32[]{:S(2)}) collective-permute-start(bf16[32,512]{1,0:T(8,128)(2,1)S(1)} %join.3.refs_3_), channel_id=1, source_target_pairs={{0,1},{1,0},{2,6},{3,7},{4,5},{5,4},{6,2},{7,3},{8,9},{9,8},{10,14... | collective-permute-start | bytes 98312 | tf_op jit(solution)/shard_map/ppermute | solution.py:303
  9.7 1.9 %collective-permute-start.5 = (bf16[32,512]{1,0:T(8,128)(2,1)S(1)}, bf16[32,512]{1,0:T(8,128)(2,1)S(1)}, u32[]{:S(2)}, u32[]{:S(2)}) collective-permute-start(bf16[32,512]{1,0:T(8,128)(2,1)S(1)} %join.3.refs_3_), channel_id=1, source_target_pairs={{0,2},{1,3},{2,0},{3,1},{4,6},{5,7},{6,4},{7,5},{8,10},{9,11},{10,... | collective-permute-start | bytes 98312 | tf_op jit(solution)/shard_map/ppermute | solution.py:303
  11.7 0.0 collective-permute-done.1.refs_1_
  11.7 0.0 copy-done
  11.7 0.3 %prepare.1 = (f32[4,64,128]{2,1,0:T(8,128)S(1)}, bf16[4,1,4,2,512]{4,3,2,1,0:T(2,128)(2,1)S(1)}) custom-call(bf16[32,512]{1,0:T(8,128)(2,1)S(1)} %join.2.refs_0_, bf16[32,512]{1,0:T(8,128)(2,1)S(1)} %collective-permute-done.1.refs_1_, bf16[512,512]{1,0:T(8,128)(2,1)S(1)} %copy-done, bf16[32,512]{1,0:T(8,128)(2,1)S(1)} %join.3.refs_3_), custom_call_target="tpu_custom_call" | custom-call | tf_op jit(solution)/shard_map/prepare/pallas_call | solution.py:212
  12.0 1.3 %collective-permute-done.4.refs_1_ = bf16[32,512]{1,0:T(8,128)(2,1)S(1)} collective-permute-done((bf16[32,512]{1,0:T(8,128)(2,1)S(1)}, bf16[32,512]{1,0:T(8,128)(2,1)S(1)}, u32[]{:S(2)}, u32[]{:S(2)}) %collective-permute-start.4) | collective-permute-done | bytes 32800 | tf_op jit(solution)/shard_map/ppermute | solution.py:303
  13.3 0.0 collective-permute-done.3.refs_0_
  13.3 0.4 %stage.1.refs_1_ = bf16[8,1,4,2,512]{4,3,2,1,0:T(2,128)(2,1)S(1)} custom-call(f32[4,64,128]{2,1,0:T(8,128)S(1)} %get-tuple-element.8.right.refs_2_, bf16[512,512]{1,0:T(8,128)(2,1)S(1)} %copy-done, bf16[32,512]{1,0:T(8,128)(2,1)S(1)} %collective-permute-done.3.refs_0_, bf16[32,512]{1,0:T(8,128)(2,1)S(1)} %collective-permute-done.4.refs_1_), custom_call_target="tpu_custom_call" | custom-call | tf_op jit(solution)/shard_map/stage/pallas_call | solution.py:237
  13.7 0.0 collective-permute-done.5.refs_4_
  13.7 1.0 %correlate.1 = bf16[16,1,4,2,512]{4,3,2,1,0:T(2,128)(2,1)} custom-call(bf16[4,1,4,2,512]{4,3,2,1,0:T(2,128)(2,1)S(1)} %get-tuple-element.7.refs_0_, bf16[8,1,4,2,512]{4,3,2,1,0:T(2,128)(2,1)S(1)} %stage.1.refs_1_, f32[4,64,128]{2,1,0:T(8,128)S(1)} %get-tuple-element.8.right.refs_2_, bf16[512,512]{1,0:T(8,128)(2,1)S(1)} %copy-done, ...), custom_call_target="tpu_custom_call" | custom-call | tf_op jit(solution)/shard_map/correlate/pallas_call | solution.py:276
  (2 shorter events, 0.0 us)
Async XLA Ops:
  1.4 4.2 %collective-permute-start = (bf16[16,512]{1,0:T(8,128)(2,1)S(1)}, bf16[16,512]{1,0:T(8,128)(2,1)S(1)}, u32[]{:S(2)}, u32[]{:S(2)}) collective-permute-start(bf16[16,512]{1,0:T(8,128)(2,1)S(1)} %whiten.1.own), channel_id=1, source_target_pairs={{0,8},{8,0},{16,24},{24,16},{1,9},{9,1},{17,25},{25,17},{2,10},{10... | collective-permute-start | bytes 49160 | tf_op jit(solution)/shard_map/ppermute | solution.py:292
  1.9 5.4 %collective-permute-start.2 = (bf16[16,512]{1,0:T(8,128)(2,1)S(1)}, bf16[16,512]{1,0:T(8,128)(2,1)S(1)}, u32[]{:S(2)}, u32[]{:S(2)}) collective-permute-start(bf16[16,512]{1,0:T(8,128)(2,1)S(1)} %whiten.1.own), channel_id=1, source_target_pairs={{0,4},{1,5},{2,3},{3,2},{4,0},{5,1},{6,7},{7,6},{8,12},{9,13},{10,... | collective-permute-start | bytes 49160 | tf_op jit(solution)/shard_map/ppermute | solution.py:303
  5.6 6.1 %copy-start = (bf16[512,512]{1,0:T(8,128)(2,1)S(1)}, bf16[512,512]{1,0:T(8,128)(2,1)}, u32[]{:S(2)}) copy-start(bf16[512,512]{1,0:T(8,128)(2,1)} %constant.8.clone.refs_2_.table.refs_3_) | copy-start | bytes 1572868
  5.6 6.1 %collective-permute-start.1 = (bf16[32,512]{1,0:T(8,128)(2,1)S(1)}, bf16[32,512]{1,0:T(8,128)(2,1)S(1)}, u32[]{:S(2)}, u32[]{:S(2)}) collective-permute-start(bf16[32,512]{1,0:T(8,128)(2,1)S(1)} %join.2.refs_0_), channel_id=1, source_target_pairs={{0,16},{8,24},{16,0},{24,8},{1,17},{9,25},{17,1},{25,9},{2,18},{10... | collective-permute-start | bytes 98312 | tf_op jit(solution)/shard_map/ppermute | solution.py:292
  7.3 6.0 %collective-permute-start.4 = (bf16[32,512]{1,0:T(8,128)(2,1)S(1)}, bf16[32,512]{1,0:T(8,128)(2,1)S(1)}, u32[]{:S(2)}, u32[]{:S(2)}) collective-permute-start(bf16[32,512]{1,0:T(8,128)(2,1)S(1)} %join.3.refs_3_), channel_id=1, source_target_pairs={{0,3},{1,2},{2,4},{3,5},{4,7},{5,6},{6,0},{7,1},{8,11},{9,10},{10,... | collective-permute-start | bytes 98312 | tf_op jit(solution)/shard_map/ppermute | solution.py:303
  9.2 4.1 %collective-permute-start.3 = (bf16[32,512]{1,0:T(8,128)(2,1)S(1)}, bf16[32,512]{1,0:T(8,128)(2,1)S(1)}, u32[]{:S(2)}, u32[]{:S(2)}) collective-permute-start(bf16[32,512]{1,0:T(8,128)(2,1)S(1)} %join.3.refs_3_), channel_id=1, source_target_pairs={{0,1},{1,0},{2,6},{3,7},{4,5},{5,4},{6,2},{7,3},{8,9},{9,8},{10,14... | collective-permute-start | bytes 98312 | tf_op jit(solution)/shard_map/ppermute | solution.py:303
  9.7 3.9 %collective-permute-start.5 = (bf16[32,512]{1,0:T(8,128)(2,1)S(1)}, bf16[32,512]{1,0:T(8,128)(2,1)S(1)}, u32[]{:S(2)}, u32[]{:S(2)}) collective-permute-start(bf16[32,512]{1,0:T(8,128)(2,1)S(1)} %join.3.refs_3_), channel_id=1, source_target_pairs={{0,2},{1,3},{2,0},{3,1},{4,6},{5,7},{6,4},{7,5},{8,10},{9,11},{10,... | collective-permute-start | bytes 98312 | tf_op jit(solution)/shard_map/ppermute | solution.py:303

commit v6 on v5

--- a/solution.py
+++ b/solution.py
@@ -16,6 +16,9 @@
 QUARTER = SAMPLES // 4
 EIGHTH = SAMPLES // 8
 LANES = 128
+GROUP = 8
+FAR = 6
+STEPS = (3, 1, 2)
 VMEM = pl.BlockSpec(memory_space=pltpu.VMEM)
 SMEM = pl.BlockSpec(memory_space=pltpu.SMEM)
 
@@ -191,9 +194,11 @@
             at += count
 
 
-def prepare_kernel(count, n_second, row_masks, *refs):
-    second_refs = refs[:n_second]
+def prepare_kernel(count, second_parts, first_parts, row_masks, *refs):
+    n_second = len(second_parts)
+    second_refs = [ref.at[part, :] for ref, part in zip(refs[:n_second], second_parts, strict=True)]
     table, *first_refs, right, ready, left, cross = refs[n_second:]
+    first_refs = [ref.at[part, :] for ref, part in zip(first_refs, first_parts, strict=True)]
     wide = count * len(row_masks)
     n = 0
     for ref in second_refs:
@@ -208,9 +213,10 @@
 
 def prepare(count, row_masks, second, lags, first):
     n_row = len(row_masks)
-    rows = sum(block.shape[0] for block in first)
-    return pl.pallas_call(
-        functools.partial(prepare_kernel, count, len(second), row_masks),
+    parts = [tuple(part for _, part in blocks) for blocks in (second, first)]
+    rows = sum(part.size for part in parts[1])
+    return pl.pallas_call(
+        functools.partial(prepare_kernel, count, *parts, row_masks),
         out_shape=(
             pltpu.VMEM((2 * BINS // LANES, count * n_row * SEG, LANES), jnp.float32),
             pltpu.VMEM((rows // SEG, 1, n_row, count, LAGS), jnp.bfloat16),
@@ -222,7 +228,7 @@
             pltpu.VMEM((rows // SEG * count * n_row, 2 * BINS), jnp.float32),
         ],
         name="prepare",
-    )(*(in_vmem(block) for block in (*second, lags, *first)))
+    )(*(in_vmem(block) for block, _ in second), in_vmem(lags), *(in_vmem(block) for block, _ in first))
 
 
 def stage_kernel(row_masks, right, table, *refs):
@@ -247,11 +253,11 @@
     )(*(in_vmem(block) for block in (right, lags, *first)))
 
 
-def correlate_kernel(count, n_ready, moves, bits, row_masks, *refs):
+def correlate_kernel(count, n_ready, masks, bits, row_masks, *refs):
     ready = refs[:n_ready]
     right, table, *first_refs, out, left, cross, last, sent = refs[n_ready:]
     col_index = lax.axis_index("col")
-    cols = [at for source in sources(col_index, moves) for at in held_at(source, moves, bits)]
+    cols = [at for mask in masks for at in spread(col_index ^ mask, bits)]
     blocks = [
         ref.at[pl.ds(at, count)] for ref in (*ready, last) for at in range(0, ref.shape[0], count)
     ]
@@ -270,11 +276,11 @@
         copy.wait()
 
 
-def correlate(count, n_row, n_col, moves, bits, row_masks, ready, right, lags, first):
+def correlate(count, n_row, n_col, masks, bits, row_masks, ready, right, lags, first):
     channels, wide = count * n_col, count * n_row
     rows = sum(block.shape[0] for block in first)
     return pl.pallas_call(
-        functools.partial(correlate_kernel, count, len(ready), moves, bits, row_masks),
+        functools.partial(correlate_kernel, count, len(ready), masks, bits, row_masks),
         out_shape=jax.ShapeDtypeStruct((channels, 1, n_row, count, LAGS), jnp.bfloat16),
         in_specs=[VMEM] * (len(ready) + 2 + len(first)),
         out_specs=pl.BlockSpec(memory_space=pl.ANY),
@@ -288,70 +294,58 @@
     )(*(in_vmem(block) for block in (*ready, right, lags, *first)))
 
 
-def swap(block, axis, mask):
-    return lax.ppermute(block, axis, [(i, i ^ mask) for i in range(lax.axis_size(axis))])
-
-
-def moves_of(n_col):
-    if n_col >= 8:
-        return ((4, 1), (3, 6), (1, 4), (2, 2))
-    return ((0, 0), *((step, step) for step in (3, 1, 2) if step < n_col))
-
-
-def move(block, masks):
-    pairs = [(i, i ^ masks[i // 2 % 2]) for i in range(lax.axis_size("col"))]
-    return lax.ppermute(block, "col", pairs)
-
-
-def sent_from(col, masks):
-    clear, set_ = masks if clear_stays(masks) else masks[::-1]
-    return col ^ jnp.where(col & 2 == 0, clear, set_)
-
-
-def clear_stays(masks):
-    return masks[0] & 2 == 0
-
-
-def sources(col, moves):
-    return [col] + [sent_from(col, masks) for masks in moves[1:]]
-
-
-def held_at(col, moves, bits):
-    held = [col]
+def swap(block, row_mask, col_mask):
+    n_row, n_col = lax.axis_size("row"), lax.axis_size("col")
+    pairs = [
+        (row * n_col + col, (row ^ row_mask) * n_col + (col ^ col_mask))
+        for row in range(n_row)
+        for col in range(n_col)
+    ]
+    return lax.ppermute(block, ("row", "col"), pairs)
+
+
+def spread(col, bits):
+    cols = [col]
     for bit in bits:
-        held += [at ^ bit for at in held]
-    if moves[0] != (0, 0):
-        held += [at ^ sent_from(col, moves[0]) ^ col for at in held]
-    return held
+        cols += [at ^ bit for at in cols]
+    return cols
 
 
 def body(traces, offsets, band_lo, band_hi, live):
     count = traces.shape[0]
     n_row, n_col = lax.axis_size("row"), lax.axis_size("col")
     white = whiten(traces, offsets, band_lo, band_hi, live)
-    second, row_masks = [white], [0]
-    bit = 1
-    while bit < n_row:
-        mine = second[0] if len(second) == 1 else join(*second)
-        second = [mine, swap(mine, "row", bit)]
-        row_masks += [mask ^ bit for mask in row_masks]
-        bit *= 2
-    held, bits = white, []
+    own, bits = white, []
     bit = n_col // 2
-    while bit > 4:
-        held = join(held, swap(held, "col", bit))
+    while bit >= GROUP:
+        own = join(own, swap(own, 0, bit))
         bits.append(bit)
         bit //= 2
-    moves = moves_of(n_col)
-    if moves[0] != (0, 0):
-        held = join(held, move(held, moves[0]), 10**9)
-    near = [move(held, masks) for masks in moves[1:]]
+    far = swap(own, 1, FAR)
+    sibling = swap(own, 1, 0)
+    across = swap(white, 2, 0)
+    pair = join(far, sibling, 10**9)
+    near = [swap(pair, 1, step) for step in STEPS]
+    other, diagonal = swap(far, 1, 0), swap(across, 1, 0)
+    rows, held = white.shape[0], own.shape[0]
+    second = [(block, pl.ds(0, rows)) for block in (white, sibling, across, diagonal)]
+    row_masks = [0, 1, 2, 3]
+    if n_row > len(row_masks):
+        stacked = jnp.concatenate([block[part.start : part.start + rows] for block, part in second])
+        second = [(stacked, pl.ds(0, stacked.shape[0]))]
+        bit = len(row_masks)
+        while bit < n_row:
+            second += [
+                (swap(block, bit, 0), pl.ds(0, block.shape[0])) for block, _ in second
+            ]
+            row_masks += [mask ^ bit for mask in row_masks]
+            bit *= 2
     lags = jnp.asarray(lag_table())
-    right, *ready = prepare(count, row_masks, second, lags, [held])
-    if len(near) > 1:
-        ready += [stage(count, row_masks, right, lags, near[-2::-1])]
-    order = (moves[0], *moves[-2:0:-1], moves[-1])
-    return correlate(count, n_row, n_col, order, bits, row_masks, ready, right, lags, near[-1:])
+    first = [(own, pl.ds(0, held)), (other, pl.ds(0, held))]
+    right, *ready = prepare(count, row_masks, second, lags, first)
+    ready += [stage(count, row_masks, right, lags, near[-2::-1])]
+    masks = [0, FAR, *(mask for step in (*STEPS[-2::-1], STEPS[-1]) for mask in (step ^ FAR, step))]
+    return correlate(count, n_row, n_col, masks, bits, row_masks, ready, right, lags, near[-1:])
 
 
 def solution(mesh):

time: 14.8 us -> 14.6 us (0.986)
  waiting for transfers between devices: 1.44 us -> 1.2 us
    ppermute x6 -> x8, waiting for transfers between devices: 1.44 us -> 1.2 us  [swap(): return lax.ppermute(block, ('row', 'col'), pairs)]
    ppermute x6 -> x8, starting transfers between devices: 10.2 us -> 10.1 us  [swap(): return lax.ppermute(block, ('row', 'col'), pairs)]
  transfers between devices with their start and end apart: 6 -> 8, of which waited for: 2 -> 2; matrix products, arithmetic and copies ran while one was open for 0% -> 0% of each run, Pallas kernels for 5% -> 5%
where the time goes in v6:
time: 14.6 us; the launch traced here: 14.4 us
  starting transfers between devices  10.1 us (69%)
  Pallas kernels  3 us (21%)
  waiting for transfers between devices  1.2 us (8%)
    ppermute x8, starting transfers between devices, swap(): return lax.ppermute(block, ('row', 'col'), pairs)  10.1 us
    pallas_call x1, Pallas kernels, whiten(): pl.pallas_call(whiten_kernel, out_shape=pltpu.VMEM((count * SEG, 2 * BINS...  1.37 us
    ppermute x8, waiting for transfers between devices, swap(): return lax.ppermute(block, ('row', 'col'), pairs)  1.2 us
    pallas_call x1, Pallas kernels, correlate(): pl.pallas_call(functools.partial(correlate_kernel, count, len(ready), mas...  0.96 us
    pallas_call x1, Pallas kernels, stage(): pl.pallas_call(functools.partial(stage_kernel, row_masks), out_shape=pltp...  0.4 us
  transfers between devices with their start and end apart: 8, of which 2 were waited for; matrix products, arithmetic and copies ran while one was open for 0% of the time, Pallas kernels for 5%

profile of v6, /device:TPU:0, one launch (start us, length us, event | category | flops | bytes accessed | tf_op | source)
XLA Modules:
  0.0 14.4 jit_solution(10056953259401463689)
XLA Ops:
  0.0 1.4 %whiten.1.refs_0_.refs_5_ = bf16[16,512]{1,0:T(8,128)(2,1)S(1)} custom-call(s32[2,8]{1,0:T(2,128)} %offsets.1, s32[2]{0:T(128)} %band_lo.1, s32[2]{0:T(128)} %band_hi.1, s32[2]{0:T(128)} %live.1, f32[2,4096]{1,0:T(2,128)} %traces.1, f32[8,256]{1,0:T(8,128)} %constant.6.clone.waves, bf16[2,128,512]{2,1,0:T(8,128)(2,1)} %constant.7.clone.table), custom_call_target="tpu_custom_call" | custom-call | tf_op jit(solution)/shard_map/whiten/pallas_call | solution.py:132
  1.4 0.0 copy-start
  1.4 4.6 %collective-permute-start.3 = (bf16[16,512]{1,0:T(8,128)(2,1)S(1)}, bf16[16,512]{1,0:T(8,128)(2,1)S(1)}, u32[]{:S(2)}, u32[]{:S(2)}) collective-permute-start(bf16[16,512]{1,0:T(8,128)(2,1)S(1)} %whiten.1.refs_0_.refs_5_), channel_id=1, source_target_pairs={{0,14},{1,15},{2,12},{3,13},{4,10},{5,11},{6,8},{7,9},{8,6},{9,7},... | collective-permute-start | bytes 49160 | tf_op jit(solution)/shard_map/ppermute | solution.py:304
  5.9 0.7 %collective-permute-start = (bf16[16,512]{1,0:T(8,128)(2,1)S(1)}, bf16[16,512]{1,0:T(8,128)(2,1)S(1)}, u32[]{:S(2)}, u32[]{:S(2)}) collective-permute-start(bf16[16,512]{1,0:T(8,128)(2,1)S(1)} %whiten.1.refs_0_.refs_5_), channel_id=1, source_target_pairs={{0,8},{1,9},{2,10},{3,11},{4,12},{5,13},{6,14},{7,15},{8,0},{9,1},... | collective-permute-start | bytes 49160 | tf_op jit(solution)/shard_map/ppermute | solution.py:304
  6.6 1.5 %collective-permute-start.1 = (bf16[16,512]{1,0:T(8,128)(2,1)S(1)}, bf16[16,512]{1,0:T(8,128)(2,1)S(1)}, u32[]{:S(2)}, u32[]{:S(2)}) collective-permute-start(bf16[16,512]{1,0:T(8,128)(2,1)S(1)} %whiten.1.refs_0_.refs_5_), channel_id=1, source_target_pairs={{0,16},{1,17},{2,18},{3,19},{4,20},{5,21},{6,22},{7,23},{8,24},{9,... | collective-permute-start | bytes 49160 | tf_op jit(solution)/shard_map/ppermute | solution.py:304
  8.1 0.0 collective-permute-done.3.own
  8.1 0.0 collective-permute-done.refs_1_.other
  8.1 0.2 %collective-permute-start.6 = (bf16[32,512]{1,0:T(8,128)(2,1)S(1)}, bf16[32,512]{1,0:T(8,128)(2,1)S(1)}, u32[]{:S(2)}, u32[]{:S(2)}) collective-permute-start(bf16[32,512]{1,0:T(8,128)(2,1)S(1)} %join.1), channel_id=1, source_target_pairs={{0,11},{1,10},{2,9},{3,8},{4,15},{5,14},{6,13},{7,12},{8,3},{9,2},... | collective-permute-start | bytes 98312 | tf_op jit(solution)/shard_map/ppermute | solution.py:304
  8.3 0.9 %collective-permute-start.5 = (bf16[32,512]{1,0:T(8,128)(2,1)S(1)}, bf16[32,512]{1,0:T(8,128)(2,1)S(1)}, u32[]{:S(2)}, u32[]{:S(2)}) collective-permute-start(bf16[32,512]{1,0:T(8,128)(2,1)S(1)} %join.1), channel_id=1, source_target_pairs={{0,9},{1,8},{2,11},{3,10},{4,13},{5,12},{6,15},{7,14},{8,1},{9,0},... | collective-permute-start | bytes 98312 | tf_op jit(solution)/shard_map/ppermute | solution.py:304
  9.2 1.7 %collective-permute-start.7 = (bf16[32,512]{1,0:T(8,128)(2,1)S(1)}, bf16[32,512]{1,0:T(8,128)(2,1)S(1)}, u32[]{:S(2)}, u32[]{:S(2)}) collective-permute-start(bf16[32,512]{1,0:T(8,128)(2,1)S(1)} %join.1), channel_id=1, source_target_pairs={{0,10},{1,11},{2,8},{3,9},{4,14},{5,15},{6,12},{7,13},{8,2},{9,3},... | collective-permute-start | bytes 98312 | tf_op jit(solution)/shard_map/ppermute | solution.py:304
  10.9 0.6 %collective-permute-start.4 = (bf16[16,512]{1,0:T(8,128)(2,1)S(1)}, bf16[16,512]{1,0:T(8,128)(2,1)S(1)}, u32[]{:S(2)}, u32[]{:S(2)}) collective-permute-start(bf16[16,512]{1,0:T(8,128)(2,1)S(1)} %collective-permute-done.3.own), channel_id=1, source_target_pairs={{0,8},{1,9},{2,10},{3,11},{4,12},{5,13},{6,14},{7,15},{8,0},{9,1},... | collective-permute-start | bytes 49160 | tf_op jit(solution)/shard_map/ppermute | solution.py:304
  11.5 0.0 collective-permute-done.1.refs_2_
  11.5 0.0 collective-permute-start.2
  11.5 0.8 %collective-permute-done.4.refs_6_ = bf16[16,512]{1,0:T(8,128)(2,1)S(1)} collective-permute-done((bf16[16,512]{1,0:T(8,128)(2,1)S(1)}, bf16[16,512]{1,0:T(8,128)(2,1)S(1)}, u32[]{:S(2)}, u32[]{:S(2)}) %collective-permute-start.4) | collective-permute-done | bytes 16416 | tf_op jit(solution)/shard_map/ppermute | solution.py:304
  12.4 0.3 %collective-permute-done.2.refs_3_ = bf16[16,512]{1,0:T(8,128)(2,1)S(1)} collective-permute-done((bf16[16,512]{1,0:T(8,128)(2,1)S(1)}, bf16[16,512]{1,0:T(8,128)(2,1)S(1)}, u32[]{:S(2)}, u32[]{:S(2)}) %collective-permute-start.2) | collective-permute-done | bytes 16416 | tf_op jit(solution)/shard_map/ppermute | solution.py:304
  12.7 0.0 copy-done
  12.7 0.3 %prepare.1 = (f32[4,64,128]{2,1,0:T(8,128)S(1)}, bf16[4,1,4,2,512]{4,3,2,1,0:T(2,128)(2,1)S(1)}) custom-call(bf16[16,512]{1,0:T(8,128)(2,1)S(1)} %whiten.1.refs_0_.refs_5_, bf16[16,512]{1,0:T(8,128)(2,1)S(1)} %collective-permute-done.refs_1_.other, bf16[16,512]{1,0:T(8,128)(2,1)S(1)} %collective-permute-done.1.refs_2_, ...), custom_call_target="tpu_custom_call" | custom-call | tf_op jit(solution)/shard_map/prepare/pallas_call | solution.py:218
  13.0 0.0 collective-permute-done.6.refs_1_
  13.0 0.0 collective-permute-done.5.refs_0_
  13.0 0.4 %stage.1.refs_1_ = bf16[8,1,4,2,512]{4,3,2,1,0:T(2,128)(2,1)S(1)} custom-call(f32[4,64,128]{2,1,0:T(8,128)S(1)} %get-tuple-element.8.right.refs_2_, bf16[512,512]{1,0:T(8,128)(2,1)S(1)} %copy-done, bf16[32,512]{1,0:T(8,128)(2,1)S(1)} %collective-permute-done.5.refs_0_, bf16[32,512]{1,0:T(8,128)(2,1)S(1)} %collective-permute-done.6.refs_1_), custom_call_target="tpu_custom_call" | custom-call | tf_op jit(solution)/shard_map/stage/pallas_call | solution.py:243
  13.4 0.0 collective-permute-done.7.refs_4_
  13.5 1.0 %correlate.1 = bf16[16,1,4,2,512]{4,3,2,1,0:T(2,128)(2,1)} custom-call(bf16[4,1,4,2,512]{4,3,2,1,0:T(2,128)(2,1)S(1)} %get-tuple-element.7.refs_0_, bf16[8,1,4,2,512]{4,3,2,1,0:T(2,128)(2,1)S(1)} %stage.1.refs_1_, f32[4,64,128]{2,1,0:T(8,128)S(1)} %get-tuple-element.8.right.refs_2_, bf16[512,512]{1,0:T(8,128)(2,1)S(1)} %copy-done, ...), custom_call_target="tpu_custom_call" | custom-call | tf_op jit(solution)/shard_map/correlate/pallas_call | solution.py:282
  (1 shorter events, 0.0 us)
Async XLA Ops:
  1.4 11.4 %copy-start = (bf16[512,512]{1,0:T(8,128)(2,1)S(1)}, bf16[512,512]{1,0:T(8,128)(2,1)}, u32[]{:S(2)}) copy-start(bf16[512,512]{1,0:T(8,128)(2,1)} %constant.8.clone.refs_4_.table.refs_3_) | copy-start | bytes 1572868
  1.4 6.7 %collective-permute-start.3 = (bf16[16,512]{1,0:T(8,128)(2,1)S(1)}, bf16[16,512]{1,0:T(8,128)(2,1)S(1)}, u32[]{:S(2)}, u32[]{:S(2)}) collective-permute-start(bf16[16,512]{1,0:T(8,128)(2,1)S(1)} %whiten.1.refs_0_.refs_5_), channel_id=1, source_target_pairs={{0,14},{1,15},{2,12},{3,13},{4,10},{5,11},{6,8},{7,9},{8,6},{9,7},... | collective-permute-start | bytes 49160 | tf_op jit(solution)/shard_map/ppermute | solution.py:304
  5.9 2.2 %collective-permute-start = (bf16[16,512]{1,0:T(8,128)(2,1)S(1)}, bf16[16,512]{1,0:T(8,128)(2,1)S(1)}, u32[]{:S(2)}, u32[]{:S(2)}) collective-permute-start(bf16[16,512]{1,0:T(8,128)(2,1)S(1)} %whiten.1.refs_0_.refs_5_), channel_id=1, source_target_pairs={{0,8},{1,9},{2,10},{3,11},{4,12},{5,13},{6,14},{7,15},{8,0},{9,1},... | collective-permute-start | bytes 49160 | tf_op jit(solution)/shard_map/ppermute | solution.py:304
  6.6 4.9 %collective-permute-start.1 = (bf16[16,512]{1,0:T(8,128)(2,1)S(1)}, bf16[16,512]{1,0:T(8,128)(2,1)S(1)}, u32[]{:S(2)}, u32[]{:S(2)}) collective-permute-start(bf16[16,512]{1,0:T(8,128)(2,1)S(1)} %whiten.1.refs_0_.refs_5_), channel_id=1, source_target_pairs={{0,16},{1,17},{2,18},{3,19},{4,20},{5,21},{6,22},{7,23},{8,24},{9,... | collective-permute-start | bytes 49160 | tf_op jit(solution)/shard_map/ppermute | solution.py:304
  8.1 4.9 %collective-permute-start.6 = (bf16[32,512]{1,0:T(8,128)(2,1)S(1)}, bf16[32,512]{1,0:T(8,128)(2,1)S(1)}, u32[]{:S(2)}, u32[]{:S(2)}) collective-permute-start(bf16[32,512]{1,0:T(8,128)(2,1)S(1)} %join.1), channel_id=1, source_target_pairs={{0,11},{1,10},{2,9},{3,8},{4,15},{5,14},{6,13},{7,12},{8,3},{9,2},... | collective-permute-start | bytes 98312 | tf_op jit(solution)/shard_map/ppermute | solution.py:304
  8.3 4.7 %collective-permute-start.5 = (bf16[32,512]{1,0:T(8,128)(2,1)S(1)}, bf16[32,512]{1,0:T(8,128)(2,1)S(1)}, u32[]{:S(2)}, u32[]{:S(2)}) collective-permute-start(bf16[32,512]{1,0:T(8,128)(2,1)S(1)} %join.1), channel_id=1, source_target_pairs={{0,9},{1,8},{2,11},{3,10},{4,13},{5,12},{6,15},{7,14},{8,1},{9,0},... | collective-permute-start | bytes 98312 | tf_op jit(solution)/shard_map/ppermute | solution.py:304
  9.2 4.2 %collective-permute-start.7 = (bf16[32,512]{1,0:T(8,128)(2,1)S(1)}, bf16[32,512]{1,0:T(8,128)(2,1)S(1)}, u32[]{:S(2)}, u32[]{:S(2)}) collective-permute-start(bf16[32,512]{1,0:T(8,128)(2,1)S(1)} %join.1), channel_id=1, source_target_pairs={{0,10},{1,11},{2,8},{3,9},{4,14},{5,15},{6,12},{7,13},{8,2},{9,3},... | collective-permute-start | bytes 98312 | tf_op jit(solution)/shard_map/ppermute | solution.py:304
  10.9 1.5 %collective-permute-start.4 = (bf16[16,512]{1,0:T(8,128)(2,1)S(1)}, bf16[16,512]{1,0:T(8,128)(2,1)S(1)}, u32[]{:S(2)}, u32[]{:S(2)}) collective-permute-start(bf16[16,512]{1,0:T(8,128)(2,1)S(1)} %collective-permute-done.3.own), channel_id=1, source_target_pairs={{0,8},{1,9},{2,10},{3,11},{4,12},{5,13},{6,14},{7,15},{8,0},{9,1},... | collective-permute-start | bytes 49160 | tf_op jit(solution)/shard_map/ppermute | solution.py:304
  11.5 1.2 %collective-permute-start.2 = (bf16[16,512]{1,0:T(8,128)(2,1)S(1)}, bf16[16,512]{1,0:T(8,128)(2,1)S(1)}, u32[]{:S(2)}, u32[]{:S(2)}) collective-permute-start(bf16[16,512]{1,0:T(8,128)(2,1)S(1)} %collective-permute-done.1.refs_2_), channel_id=1, source_target_pairs={{0,8},{1,9},{2,10},{3,11},{4,12},{5,13},{6,14},{7,15},{8,0},{9,1},... | collective-permute-start | bytes 49160 | tf_op jit(solution)/shard_map/ppermute | solution.py:304

commit v7 on v6

--- a/solution.py
+++ b/solution.py
@@ -323,13 +323,13 @@
         bit //= 2
     far = swap(own, 1, FAR)
     sibling = swap(own, 1, 0)
-    across = swap(white, 2, 0)
+    across = swap(white, 3, 0)
     pair = join(far, sibling, 10**9)
     near = [swap(pair, 1, step) for step in STEPS]
     other, diagonal = swap(far, 1, 0), swap(across, 1, 0)
     rows, held = white.shape[0], own.shape[0]
     second = [(block, pl.ds(0, rows)) for block in (white, sibling, across, diagonal)]
-    row_masks = [0, 1, 2, 3]
+    row_masks = [0, 1, 3, 2]
     if n_row > len(row_masks):
         stacked = jnp.concatenate([block[part.start : part.start + rows] for block, part in second])
         second = [(stacked, pl.ds(0, stacked.shape[0]))]
@@ -341,11 +341,13 @@
             row_masks += [mask ^ bit for mask in row_masks]
             bit *= 2
     lags = jnp.asarray(lag_table())
-    first = [(own, pl.ds(0, held)), (other, pl.ds(0, held))]
-    right, *ready = prepare(count, row_masks, second, lags, first)
-    ready += [stage(count, row_masks, right, lags, near[-2::-1])]
-    masks = [0, FAR, *(mask for step in (*STEPS[-2::-1], STEPS[-1]) for mask in (step ^ FAR, step))]
-    return correlate(count, n_row, n_col, masks, bits, row_masks, ready, right, lags, near[-1:])
+    right, *ready = prepare(count, row_masks, second, lags, [(own, pl.ds(0, held))])
+    ready += [stage(count, row_masks, right, lags, [other, near[0]])]
+    masks = [0, FAR]
+    for step in (STEPS[0], *STEPS[:0:-1]):
+        masks += [step ^ FAR, step]
+    last = near[:0:-1]
+    return correlate(count, n_row, n_col, masks, bits, row_masks, ready, right, lags, last)
 
 
 def solution(mesh):

time: 14.6 us -> 14.4 us (0.986)
  waiting for transfers between devices: 1.2 us -> 0.91 us
    ppermute x8, waiting for transfers between devices: 1.2 us -> 0.91 us  [swap(): return lax.ppermute(block, ('row', 'col'), pairs)]
  transfers between devices with their start and end apart: 8 -> 8, of which waited for: 2 -> 2; matrix products, arithmetic and copies ran while one was open for 0% -> 0% of each run, Pallas kernels for 5% -> 4%
where the time goes in v7:
time: 14.4 us; the launch traced here: 14.3 us
  starting transfers between devices  10.2 us (71%)
  Pallas kernels  3.08 us (21%)
  waiting for transfers between devices  0.91 us (6%)
    ppermute x8, starting transfers between devices, swap(): return lax.ppermute(block, ('row', 'col'), pairs)  10.2 us
    pallas_call x1, Pallas kernels, whiten(): pl.pallas_call(whiten_kernel, out_shape=pltpu.VMEM((count * SEG, 2 * BINS...  1.37 us
    pallas_call x1, Pallas kernels, correlate(): pl.pallas_call(functools.partial(correlate_kernel, count, len(ready), mas...  1.09 us
    ppermute x8, waiting for transfers between devices, swap(): return lax.ppermute(block, ('row', 'col'), pairs)  0.91 us
    pallas_call x1, Pallas kernels, stage(): pl.pallas_call(functools.partial(stage_kernel, row_masks), out_shape=pltp...  0.36 us
  transfers between devices with their start and end apart: 8, of which 2 were waited for; matrix products, arithmetic and copies ran while one was open for 0% of the time, Pallas kernels for 4%

profile of v7, /device:TPU:0, one launch (start us, length us, event | category | flops | bytes accessed | tf_op | source)
XLA Modules:
  0.0 14.3 jit_solution(5223564750930382116)
XLA Ops:
  0.0 1.4 %whiten.1.refs_0_.refs_5_ = bf16[16,512]{1,0:T(8,128)(2,1)S(1)} custom-call(s32[2,8]{1,0:T(2,128)} %offsets.1, s32[2]{0:T(128)} %band_lo.1, s32[2]{0:T(128)} %band_hi.1, s32[2]{0:T(128)} %live.1, f32[2,4096]{1,0:T(2,128)} %traces.1, f32[8,256]{1,0:T(8,128)} %constant.6.clone.waves, bf16[2,128,512]{2,1,0:T(8,128)(2,1)} %constant.7.clone.table), custom_call_target="tpu_custom_call" | custom-call | tf_op jit(solution)/shard_map/whiten/pallas_call | solution.py:132
  1.4 0.0 copy-start
  1.4 4.6 %collective-permute-start.3 = (bf16[16,512]{1,0:T(8,128)(2,1)S(1)}, bf16[16,512]{1,0:T(8,128)(2,1)S(1)}, u32[]{:S(2)}, u32[]{:S(2)}) collective-permute-start(bf16[16,512]{1,0:T(8,128)(2,1)S(1)} %whiten.1.refs_0_.refs_5_), channel_id=1, source_target_pairs={{0,14},{1,15},{2,12},{3,13},{4,10},{5,11},{6,8},{7,9},{8,6},{9,7},... | collective-permute-start | bytes 49160 | tf_op jit(solution)/shard_map/ppermute | solution.py:304
  5.9 0.7 %collective-permute-start = (bf16[16,512]{1,0:T(8,128)(2,1)S(1)}, bf16[16,512]{1,0:T(8,128)(2,1)S(1)}, u32[]{:S(2)}, u32[]{:S(2)}) collective-permute-start(bf16[16,512]{1,0:T(8,128)(2,1)S(1)} %whiten.1.refs_0_.refs_5_), channel_id=1, source_target_pairs={{0,8},{1,9},{2,10},{3,11},{4,12},{5,13},{6,14},{7,15},{8,0},{9,1},... | collective-permute-start | bytes 49160 | tf_op jit(solution)/shard_map/ppermute | solution.py:304
  6.6 1.1 %collective-permute-start.1 = (bf16[16,512]{1,0:T(8,128)(2,1)S(1)}, bf16[16,512]{1,0:T(8,128)(2,1)S(1)}, u32[]{:S(2)}, u32[]{:S(2)}) collective-permute-start(bf16[16,512]{1,0:T(8,128)(2,1)S(1)} %whiten.1.refs_0_.refs_5_), channel_id=1, source_target_pairs={{0,24},{1,25},{2,26},{3,27},{4,28},{5,29},{6,30},{7,31},{8,16},{9,... | collective-permute-start | bytes 49160 | tf_op jit(solution)/shard_map/ppermute | solution.py:304
  7.7 0.0 collective-permute-done.3.own
  7.7 0.0 collective-permute-done.refs_1_.other
  7.8 0.7 %collective-permute-start.5 = (bf16[32,512]{1,0:T(8,128)(2,1)S(1)}, bf16[32,512]{1,0:T(8,128)(2,1)S(1)}, u32[]{:S(2)}, u32[]{:S(2)}) collective-permute-start(bf16[32,512]{1,0:T(8,128)(2,1)S(1)} %join.1), channel_id=1, source_target_pairs={{0,11},{1,10},{2,9},{3,8},{4,15},{5,14},{6,13},{7,12},{8,3},{9,2},... | collective-permute-start | bytes 98312 | tf_op jit(solution)/shard_map/ppermute | solution.py:304
  8.4 1.1 %collective-permute-start.7 = (bf16[32,512]{1,0:T(8,128)(2,1)S(1)}, bf16[32,512]{1,0:T(8,128)(2,1)S(1)}, u32[]{:S(2)}, u32[]{:S(2)}) collective-permute-start(bf16[32,512]{1,0:T(8,128)(2,1)S(1)} %join.1), channel_id=1, source_target_pairs={{0,9},{1,8},{2,11},{3,10},{4,13},{5,12},{6,15},{7,14},{8,1},{9,0},... | collective-permute-start | bytes 98312 | tf_op jit(solution)/shard_map/ppermute | solution.py:304
  9.5 1.6 %collective-permute-start.6 = (bf16[32,512]{1,0:T(8,128)(2,1)S(1)}, bf16[32,512]{1,0:T(8,128)(2,1)S(1)}, u32[]{:S(2)}, u32[]{:S(2)}) collective-permute-start(bf16[32,512]{1,0:T(8,128)(2,1)S(1)} %join.1), channel_id=1, source_target_pairs={{0,10},{1,11},{2,8},{3,9},{4,14},{5,15},{6,12},{7,13},{8,2},{9,3},... | collective-permute-start | bytes 98312 | tf_op jit(solution)/shard_map/ppermute | solution.py:304
  11.1 0.0 collective-permute-done.1.refs_2_
  11.1 0.0 collective-permute-start.2
  11.2 0.5 %collective-permute-start.4 = (bf16[16,512]{1,0:T(8,128)(2,1)S(1)}, bf16[16,512]{1,0:T(8,128)(2,1)S(1)}, u32[]{:S(2)}, u32[]{:S(2)}) collective-permute-start(bf16[16,512]{1,0:T(8,128)(2,1)S(1)} %collective-permute-done.3.own), channel_id=1, source_target_pairs={{0,8},{1,9},{2,10},{3,11},{4,12},{5,13},{6,14},{7,15},{8,0},{9,1},... | collective-permute-start | bytes 49160 | tf_op jit(solution)/shard_map/ppermute | solution.py:304
  11.7 0.7 %collective-permute-done.2.refs_3_ = bf16[16,512]{1,0:T(8,128)(2,1)S(1)} collective-permute-done((bf16[16,512]{1,0:T(8,128)(2,1)S(1)}, bf16[16,512]{1,0:T(8,128)(2,1)S(1)}, u32[]{:S(2)}, u32[]{:S(2)}) %collective-permute-start.2) | collective-permute-done | bytes 16416 | tf_op jit(solution)/shard_map/ppermute | solution.py:304
  12.3 0.0 copy-done
  12.3 0.3 %prepare.1 = (f32[4,64,128]{2,1,0:T(8,128)S(1)}, bf16[2,1,4,2,512]{4,3,2,1,0:T(2,128)(2,1)S(1)}) custom-call(bf16[16,512]{1,0:T(8,128)(2,1)S(1)} %whiten.1.refs_0_.refs_5_, bf16[16,512]{1,0:T(8,128)(2,1)S(1)} %collective-permute-done.refs_1_.other, bf16[16,512]{1,0:T(8,128)(2,1)S(1)} %collective-permute-done.1.refs_2_, ...), custom_call_target="tpu_custom_call" | custom-call | tf_op jit(solution)/shard_map/prepare/pallas_call | solution.py:218
  12.6 0.0 collective-permute-done.4.refs_0_
  12.6 0.0 collective-permute-done.5.refs_1_
  12.6 0.4 %stage.1.refs_1_ = bf16[6,1,4,2,512]{4,3,2,1,0:T(2,128)(2,1)S(1)} custom-call(f32[4,64,128]{2,1,0:T(8,128)S(1)} %get-tuple-element.8.right.refs_2_, bf16[512,512]{1,0:T(8,128)(2,1)S(1)} %copy-done, bf16[16,512]{1,0:T(8,128)(2,1)S(1)} %collective-permute-done.4.refs_0_, bf16[32,512]{1,0:T(8,128)(2,1)S(1)} %collective-permute-done.5.refs_1_), custom_call_target="tpu_custom_call" | custom-call | tf_op jit(solution)/shard_map/stage/pallas_call | solution.py:243
  13.0 0.0 collective-permute-done.7.refs_5_
  13.0 0.2 %collective-permute-done.6.refs_4_ = bf16[32,512]{1,0:T(8,128)(2,1)S(1)} collective-permute-done((bf16[32,512]{1,0:T(8,128)(2,1)S(1)}, bf16[32,512]{1,0:T(8,128)(2,1)S(1)}, u32[]{:S(2)}, u32[]{:S(2)}) %collective-permute-start.6) | collective-permute-done | bytes 32800 | tf_op jit(solution)/shard_map/ppermute | solution.py:304
  13.2 1.1 %correlate.1 = bf16[16,1,4,2,512]{4,3,2,1,0:T(2,128)(2,1)} custom-call(bf16[2,1,4,2,512]{4,3,2,1,0:T(2,128)(2,1)S(1)} %get-tuple-element.7.refs_0_, bf16[6,1,4,2,512]{4,3,2,1,0:T(2,128)(2,1)S(1)} %stage.1.refs_1_, f32[4,64,128]{2,1,0:T(8,128)S(1)} %get-tuple-element.8.right.refs_2_, bf16[512,512]{1,0:T(8,128)(2,1)S(1)} %copy-done, ...), custom_call_target="tpu_custom_call" | custom-call | tf_op jit(solution)/shard_map/correlate/pallas_call | solution.py:282
  (1 shorter events, 0.0 us)
Async XLA Ops:
  1.4 11.0 %copy-start = (bf16[512,512]{1,0:T(8,128)(2,1)S(1)}, bf16[512,512]{1,0:T(8,128)(2,1)}, u32[]{:S(2)}) copy-start(bf16[512,512]{1,0:T(8,128)(2,1)} %constant.8.clone.refs_4_.table.refs_3_) | copy-start | bytes 1572868
  1.4 6.4 %collective-permute-start.3 = (bf16[16,512]{1,0:T(8,128)(2,1)S(1)}, bf16[16,512]{1,0:T(8,128)(2,1)S(1)}, u32[]{:S(2)}, u32[]{:S(2)}) collective-permute-start(bf16[16,512]{1,0:T(8,128)(2,1)S(1)} %whiten.1.refs_0_.refs_5_), channel_id=1, source_target_pairs={{0,14},{1,15},{2,12},{3,13},{4,10},{5,11},{6,8},{7,9},{8,6},{9,7},... | collective-permute-start | bytes 49160 | tf_op jit(solution)/shard_map/ppermute | solution.py:304
  5.9 1.8 %collective-permute-start = (bf16[16,512]{1,0:T(8,128)(2,1)S(1)}, bf16[16,512]{1,0:T(8,128)(2,1)S(1)}, u32[]{:S(2)}, u32[]{:S(2)}) collective-permute-start(bf16[16,512]{1,0:T(8,128)(2,1)S(1)} %whiten.1.refs_0_.refs_5_), channel_id=1, source_target_pairs={{0,8},{1,9},{2,10},{3,11},{4,12},{5,13},{6,14},{7,15},{8,0},{9,1},... | collective-permute-start | bytes 49160 | tf_op jit(solution)/shard_map/ppermute | solution.py:304
  6.6 4.5 %collective-permute-start.1 = (bf16[16,512]{1,0:T(8,128)(2,1)S(1)}, bf16[16,512]{1,0:T(8,128)(2,1)S(1)}, u32[]{:S(2)}, u32[]{:S(2)}) collective-permute-start(bf16[16,512]{1,0:T(8,128)(2,1)S(1)} %whiten.1.refs_0_.refs_5_), channel_id=1, source_target_pairs={{0,24},{1,25},{2,26},{3,27},{4,28},{5,29},{6,30},{7,31},{8,16},{9,... | collective-permute-start | bytes 49160 | tf_op jit(solution)/shard_map/ppermute | solution.py:304
  7.8 4.9 %collective-permute-start.5 = (bf16[32,512]{1,0:T(8,128)(2,1)S(1)}, bf16[32,512]{1,0:T(8,128)(2,1)S(1)}, u32[]{:S(2)}, u32[]{:S(2)}) collective-permute-start(bf16[32,512]{1,0:T(8,128)(2,1)S(1)} %join.1), channel_id=1, source_target_pairs={{0,11},{1,10},{2,9},{3,8},{4,15},{5,14},{6,13},{7,12},{8,3},{9,2},... | collective-permute-start | bytes 98312 | tf_op jit(solution)/shard_map/ppermute | solution.py:304
  8.4 4.6 %collective-permute-start.7 = (bf16[32,512]{1,0:T(8,128)(2,1)S(1)}, bf16[32,512]{1,0:T(8,128)(2,1)S(1)}, u32[]{:S(2)}, u32[]{:S(2)}) collective-permute-start(bf16[32,512]{1,0:T(8,128)(2,1)S(1)} %join.1), channel_id=1, source_target_pairs={{0,9},{1,8},{2,11},{3,10},{4,13},{5,12},{6,15},{7,14},{8,1},{9,0},... | collective-permute-start | bytes 98312 | tf_op jit(solution)/shard_map/ppermute | solution.py:304
  9.5 3.7 %collective-permute-start.6 = (bf16[32,512]{1,0:T(8,128)(2,1)S(1)}, bf16[32,512]{1,0:T(8,128)(2,1)S(1)}, u32[]{:S(2)}, u32[]{:S(2)}) collective-permute-start(bf16[32,512]{1,0:T(8,128)(2,1)S(1)} %join.1), channel_id=1, source_target_pairs={{0,10},{1,11},{2,8},{3,9},{4,14},{5,15},{6,12},{7,13},{8,2},{9,3},... | collective-permute-start | bytes 98312 | tf_op jit(solution)/shard_map/ppermute | solution.py:304
  11.1 1.2 %collective-permute-start.2 = (bf16[16,512]{1,0:T(8,128)(2,1)S(1)}, bf16[16,512]{1,0:T(8,128)(2,1)S(1)}, u32[]{:S(2)}, u32[]{:S(2)}) collective-permute-start(bf16[16,512]{1,0:T(8,128)(2,1)S(1)} %collective-permute-done.1.refs_2_), channel_id=1, source_target_pairs={{0,8},{1,9},{2,10},{3,11},{4,12},{5,13},{6,14},{7,15},{8,0},{9,1},... | collective-permute-start | bytes 49160 | tf_op jit(solution)/shard_map/ppermute | solution.py:304
  11.2 1.5 %collective-permute-start.4 = (bf16[16,512]{1,0:T(8,128)(2,1)S(1)}, bf16[16,512]{1,0:T(8,128)(2,1)S(1)}, u32[]{:S(2)}, u32[]{:S(2)}) collective-permute-start(bf16[16,512]{1,0:T(8,128)(2,1)S(1)} %collective-permute-done.3.own), channel_id=1, source_target_pairs={{0,8},{1,9},{2,10},{3,11},{4,12},{5,13},{6,14},{7,15},{8,0},{9,1},... | collective-permute-start | bytes 49160 | tf_op jit(solution)/shard_map/ppermute | solution.py:304

commit v8 on v7

--- a/solution.py
+++ b/solution.py
@@ -17,8 +17,8 @@
 EIGHTH = SAMPLES // 8
 LANES = 128
 GROUP = 8
-FAR = 6
-STEPS = (3, 1, 2)
+FAR = 4
+STEPS = (3, 2, 1)
 VMEM = pl.BlockSpec(memory_space=pltpu.VMEM)
 SMEM = pl.BlockSpec(memory_space=pltpu.SMEM)
 

time: 14.4 us -> 14.2 us (0.986)
  starting transfers between devices: 10.2 us -> 9.24 us
  waiting for transfers between devices: 0.91 us -> 1.7 us
    ppermute x8, starting transfers between devices: 10.2 us -> 9.24 us  [swap(): return lax.ppermute(block, ('row', 'col'), pairs)]
    ppermute x8, waiting for transfers between devices: 0.91 us -> 1.7 us  [swap(): return lax.ppermute(block, ('row', 'col'), pairs)]
  transfers between devices with their start and end apart: 8 -> 8, of which waited for: 2 -> 3; matrix products, arithmetic and copies ran while one was open for 0% -> 0% of each run, Pallas kernels for 4% -> 4%
where the time goes in v8:
time: 14.2 us; the launch traced here: 14.1 us
  starting transfers between devices  9.24 us (65%)
  Pallas kernels  3.08 us (22%)
  waiting for transfers between devices  1.7 us (12%)
    ppermute x8, starting transfers between devices, swap(): return lax.ppermute(block, ('row', 'col'), pairs)  9.24 us
    ppermute x8, waiting for transfers between devices, swap(): return lax.ppermute(block, ('row', 'col'), pairs)  1.7 us
    pallas_call x1, Pallas kernels, whiten(): pl.pallas_call(whiten_kernel, out_shape=pltpu.VMEM((count * SEG, 2 * BINS...  1.37 us
    pallas_call x1, Pallas kernels, correlate(): pl.pallas_call(functools.partial(correlate_kernel, count, len(ready), mas...  1.09 us
    pallas_call x1, Pallas kernels, stage(): pl.pallas_call(functools.partial(stage_kernel, row_masks), out_shape=pltp...  0.36 us
  transfers between devices with their start and end apart: 8, of which 3 were waited for; matrix products, arithmetic and copies ran while one was open for 0% of the time, Pallas kernels for 4%

profile of v8, /device:TPU:0, one launch (start us, length us, event | category | flops | bytes accessed | tf_op | source)
XLA Modules:
  0.0 14.1 jit_solution(16353497233381293558)
XLA Ops:
  0.0 1.4 %whiten.1.refs_0_.refs_5_ = bf16[16,512]{1,0:T(8,128)(2,1)S(1)} custom-call(s32[2,8]{1,0:T(2,128)} %offsets.1, s32[2]{0:T(128)} %band_lo.1, s32[2]{0:T(128)} %band_hi.1, s32[2]{0:T(128)} %live.1, f32[2,4096]{1,0:T(2,128)} %traces.1, f32[8,256]{1,0:T(8,128)} %constant.6.clone.waves, bf16[2,128,512]{2,1,0:T(8,128)(2,1)} %constant.7.clone.table), custom_call_target="tpu_custom_call" | custom-call | tf_op jit(solution)/shard_map/whiten/pallas_call | solution.py:132
  1.4 0.0 copy-start
  1.4 3.5 %collective-permute-start.3 = (bf16[16,512]{1,0:T(8,128)(2,1)S(1)}, bf16[16,512]{1,0:T(8,128)(2,1)S(1)}, u32[]{:S(2)}, u32[]{:S(2)}) collective-permute-start(bf16[16,512]{1,0:T(8,128)(2,1)S(1)} %whiten.1.refs_0_.refs_5_), channel_id=1, source_target_pairs={{0,12},{1,13},{2,14},{3,15},{4,8},{5,9},{6,10},{7,11},{8,4},{9,5},... | collective-permute-start | bytes 49160 | tf_op jit(solution)/shard_map/ppermute | solution.py:304
  4.9 0.7 %collective-permute-start = (bf16[16,512]{1,0:T(8,128)(2,1)S(1)}, bf16[16,512]{1,0:T(8,128)(2,1)S(1)}, u32[]{:S(2)}, u32[]{:S(2)}) collective-permute-start(bf16[16,512]{1,0:T(8,128)(2,1)S(1)} %whiten.1.refs_0_.refs_5_), channel_id=1, source_target_pairs={{0,8},{1,9},{2,10},{3,11},{4,12},{5,13},{6,14},{7,15},{8,0},{9,1},... | collective-permute-start | bytes 49160 | tf_op jit(solution)/shard_map/ppermute | solution.py:304
  5.6 1.1 %collective-permute-start.1 = (bf16[16,512]{1,0:T(8,128)(2,1)S(1)}, bf16[16,512]{1,0:T(8,128)(2,1)S(1)}, u32[]{:S(2)}, u32[]{:S(2)}) collective-permute-start(bf16[16,512]{1,0:T(8,128)(2,1)S(1)} %whiten.1.refs_0_.refs_5_), channel_id=1, source_target_pairs={{0,24},{1,25},{2,26},{3,27},{4,28},{5,29},{6,30},{7,31},{8,16},{9,... | collective-permute-start | bytes 49160 | tf_op jit(solution)/shard_map/ppermute | solution.py:304
  6.7 0.0 collective-permute-done.3.own
  6.7 0.0 collective-permute-done.refs_1_.other
  6.7 2.7 %collective-permute-start.5 = (bf16[32,512]{1,0:T(8,128)(2,1)S(1)}, bf16[32,512]{1,0:T(8,128)(2,1)S(1)}, u32[]{:S(2)}, u32[]{:S(2)}) collective-permute-start(bf16[32,512]{1,0:T(8,128)(2,1)S(1)} %join.1), channel_id=1, source_target_pairs={{0,11},{1,10},{2,9},{3,8},{4,15},{5,14},{6,13},{7,12},{8,3},{9,2},... | collective-permute-start | bytes 98312 | tf_op jit(solution)/shard_map/ppermute | solution.py:304
  9.4 0.2 %collective-permute-start.7 = (bf16[32,512]{1,0:T(8,128)(2,1)S(1)}, bf16[32,512]{1,0:T(8,128)(2,1)S(1)}, u32[]{:S(2)}, u32[]{:S(2)}) collective-permute-start(bf16[32,512]{1,0:T(8,128)(2,1)S(1)} %join.1), channel_id=1, source_target_pairs={{0,10},{1,11},{2,8},{3,9},{4,14},{5,15},{6,12},{7,13},{8,2},{9,3},... | collective-permute-start | bytes 98312 | tf_op jit(solution)/shard_map/ppermute | solution.py:304
  9.6 0.5 %collective-permute-start.6 = (bf16[32,512]{1,0:T(8,128)(2,1)S(1)}, bf16[32,512]{1,0:T(8,128)(2,1)S(1)}, u32[]{:S(2)}, u32[]{:S(2)}) collective-permute-start(bf16[32,512]{1,0:T(8,128)(2,1)S(1)} %join.1), channel_id=1, source_target_pairs={{0,9},{1,8},{2,11},{3,10},{4,13},{5,12},{6,15},{7,14},{8,1},{9,0},... | collective-permute-start | bytes 98312 | tf_op jit(solution)/shard_map/ppermute | solution.py:304
  10.1 0.0 collective-permute-done.1.refs_2_
  10.1 0.1 collective-permute-start.2
  10.2 0.5 %collective-permute-start.4 = (bf16[16,512]{1,0:T(8,128)(2,1)S(1)}, bf16[16,512]{1,0:T(8,128)(2,1)S(1)}, u32[]{:S(2)}, u32[]{:S(2)}) collective-permute-start(bf16[16,512]{1,0:T(8,128)(2,1)S(1)} %collective-permute-done.3.own), channel_id=1, source_target_pairs={{0,8},{1,9},{2,10},{3,11},{4,12},{5,13},{6,14},{7,15},{8,0},{9,1},... | collective-permute-start | bytes 49160 | tf_op jit(solution)/shard_map/ppermute | solution.py:304
  10.6 0.7 %collective-permute-done.2.refs_3_ = bf16[16,512]{1,0:T(8,128)(2,1)S(1)} collective-permute-done((bf16[16,512]{1,0:T(8,128)(2,1)S(1)}, bf16[16,512]{1,0:T(8,128)(2,1)S(1)}, u32[]{:S(2)}, u32[]{:S(2)}) %collective-permute-start.2) | collective-permute-done | bytes 16416 | tf_op jit(solution)/shard_map/ppermute | solution.py:304
  11.3 0.0 copy-done
  11.3 0.3 %prepare.1 = (f32[4,64,128]{2,1,0:T(8,128)S(1)}, bf16[2,1,4,2,512]{4,3,2,1,0:T(2,128)(2,1)S(1)}) custom-call(bf16[16,512]{1,0:T(8,128)(2,1)S(1)} %whiten.1.refs_0_.refs_5_, bf16[16,512]{1,0:T(8,128)(2,1)S(1)} %collective-permute-done.refs_1_.other, bf16[16,512]{1,0:T(8,128)(2,1)S(1)} %collective-permute-done.1.refs_2_, ...), custom_call_target="tpu_custom_call" | custom-call | tf_op jit(solution)/shard_map/prepare/pallas_call | solution.py:218
  11.6 0.0 collective-permute-done.4.refs_0_
  11.6 0.0 collective-permute-done.5.refs_1_
  11.6 0.4 %stage.1.refs_1_ = bf16[6,1,4,2,512]{4,3,2,1,0:T(2,128)(2,1)S(1)} custom-call(f32[4,64,128]{2,1,0:T(8,128)S(1)} %get-tuple-element.8.right.refs_2_, bf16[512,512]{1,0:T(8,128)(2,1)S(1)} %copy-done, bf16[16,512]{1,0:T(8,128)(2,1)S(1)} %collective-permute-done.4.refs_0_, bf16[32,512]{1,0:T(8,128)(2,1)S(1)} %collective-permute-done.5.refs_1_), custom_call_target="tpu_custom_call" | custom-call | tf_op jit(solution)/shard_map/stage/pallas_call | solution.py:243
  12.0 0.8 %collective-permute-done.7.refs_5_ = bf16[32,512]{1,0:T(8,128)(2,1)S(1)} collective-permute-done((bf16[32,512]{1,0:T(8,128)(2,1)S(1)}, bf16[32,512]{1,0:T(8,128)(2,1)S(1)}, u32[]{:S(2)}, u32[]{:S(2)}) %collective-permute-start.7) | collective-permute-done | bytes 32800 | tf_op jit(solution)/shard_map/ppermute | solution.py:304
  12.8 0.2 %collective-permute-done.6.refs_4_ = bf16[32,512]{1,0:T(8,128)(2,1)S(1)} collective-permute-done((bf16[32,512]{1,0:T(8,128)(2,1)S(1)}, bf16[32,512]{1,0:T(8,128)(2,1)S(1)}, u32[]{:S(2)}, u32[]{:S(2)}) %collective-permute-start.6) | collective-permute-done | bytes 32800 | tf_op jit(solution)/shard_map/ppermute | solution.py:304
  13.0 1.1 %correlate.1 = bf16[16,1,4,2,512]{4,3,2,1,0:T(2,128)(2,1)} custom-call(bf16[2,1,4,2,512]{4,3,2,1,0:T(2,128)(2,1)S(1)} %get-tuple-element.7.refs_0_, bf16[6,1,4,2,512]{4,3,2,1,0:T(2,128)(2,1)S(1)} %stage.1.refs_1_, f32[4,64,128]{2,1,0:T(8,128)S(1)} %get-tuple-element.8.right.refs_2_, bf16[512,512]{1,0:T(8,128)(2,1)S(1)} %copy-done, ...), custom_call_target="tpu_custom_call" | custom-call | tf_op jit(solution)/shard_map/correlate/pallas_call | solution.py:282
  (1 shorter events, 0.0 us)
Async XLA Ops:
  1.4 9.9 %copy-start = (bf16[512,512]{1,0:T(8,128)(2,1)S(1)}, bf16[512,512]{1,0:T(8,128)(2,1)}, u32[]{:S(2)}) copy-start(bf16[512,512]{1,0:T(8,128)(2,1)} %constant.8.clone.refs_4_.table.refs_3_) | copy-start | bytes 1572868
  1.4 5.3 %collective-permute-start.3 = (bf16[16,512]{1,0:T(8,128)(2,1)S(1)}, bf16[16,512]{1,0:T(8,128)(2,1)S(1)}, u32[]{:S(2)}, u32[]{:S(2)}) collective-permute-start(bf16[16,512]{1,0:T(8,128)(2,1)S(1)} %whiten.1.refs_0_.refs_5_), channel_id=1, source_target_pairs={{0,12},{1,13},{2,14},{3,15},{4,8},{5,9},{6,10},{7,11},{8,4},{9,5},... | collective-permute-start | bytes 49160 | tf_op jit(solution)/shard_map/ppermute | solution.py:304
  4.9 1.8 %collective-permute-start = (bf16[16,512]{1,0:T(8,128)(2,1)S(1)}, bf16[16,512]{1,0:T(8,128)(2,1)S(1)}, u32[]{:S(2)}, u32[]{:S(2)}) collective-permute-start(bf16[16,512]{1,0:T(8,128)(2,1)S(1)} %whiten.1.refs_0_.refs_5_), channel_id=1, source_target_pairs={{0,8},{1,9},{2,10},{3,11},{4,12},{5,13},{6,14},{7,15},{8,0},{9,1},... | collective-permute-start | bytes 49160 | tf_op jit(solution)/shard_map/ppermute | solution.py:304
  5.6 4.5 %collective-permute-start.1 = (bf16[16,512]{1,0:T(8,128)(2,1)S(1)}, bf16[16,512]{1,0:T(8,128)(2,1)S(1)}, u32[]{:S(2)}, u32[]{:S(2)}) collective-permute-start(bf16[16,512]{1,0:T(8,128)(2,1)S(1)} %whiten.1.refs_0_.refs_5_), channel_id=1, source_target_pairs={{0,24},{1,25},{2,26},{3,27},{4,28},{5,29},{6,30},{7,31},{8,16},{9,... | collective-permute-start | bytes 49160 | tf_op jit(solution)/shard_map/ppermute | solution.py:304
  6.7 4.9 %collective-permute-start.5 = (bf16[32,512]{1,0:T(8,128)(2,1)S(1)}, bf16[32,512]{1,0:T(8,128)(2,1)S(1)}, u32[]{:S(2)}, u32[]{:S(2)}) collective-permute-start(bf16[32,512]{1,0:T(8,128)(2,1)S(1)} %join.1), channel_id=1, source_target_pairs={{0,11},{1,10},{2,9},{3,8},{4,15},{5,14},{6,13},{7,12},{8,3},{9,2},... | collective-permute-start | bytes 98312 | tf_op jit(solution)/shard_map/ppermute | solution.py:304
  9.4 3.3 %collective-permute-start.7 = (bf16[32,512]{1,0:T(8,128)(2,1)S(1)}, bf16[32,512]{1,0:T(8,128)(2,1)S(1)}, u32[]{:S(2)}, u32[]{:S(2)}) collective-permute-start(bf16[32,512]{1,0:T(8,128)(2,1)S(1)} %join.1), channel_id=1, source_target_pairs={{0,10},{1,11},{2,8},{3,9},{4,14},{5,15},{6,12},{7,13},{8,2},{9,3},... | collective-permute-start | bytes 98312 | tf_op jit(solution)/shard_map/ppermute | solution.py:304
  9.6 3.3 %collective-permute-start.6 = (bf16[32,512]{1,0:T(8,128)(2,1)S(1)}, bf16[32,512]{1,0:T(8,128)(2,1)S(1)}, u32[]{:S(2)}, u32[]{:S(2)}) collective-permute-start(bf16[32,512]{1,0:T(8,128)(2,1)S(1)} %join.1), channel_id=1, source_target_pairs={{0,9},{1,8},{2,11},{3,10},{4,13},{5,12},{6,15},{7,14},{8,1},{9,0},... | collective-permute-start | bytes 98312 | tf_op jit(solution)/shard_map/ppermute | solution.py:304
  10.1 1.2 %collective-permute-start.2 = (bf16[16,512]{1,0:T(8,128)(2,1)S(1)}, bf16[16,512]{1,0:T(8,128)(2,1)S(1)}, u32[]{:S(2)}, u32[]{:S(2)}) collective-permute-start(bf16[16,512]{1,0:T(8,128)(2,1)S(1)} %collective-permute-done.1.refs_2_), channel_id=1, source_target_pairs={{0,8},{1,9},{2,10},{3,11},{4,12},{5,13},{6,14},{7,15},{8,0},{9,1},... | collective-permute-start | bytes 49160 | tf_op jit(solution)/shard_map/ppermute | solution.py:304
  10.2 1.4 %collective-permute-start.4 = (bf16[16,512]{1,0:T(8,128)(2,1)S(1)}, bf16[16,512]{1,0:T(8,128)(2,1)S(1)}, u32[]{:S(2)}, u32[]{:S(2)}) collective-permute-start(bf16[16,512]{1,0:T(8,128)(2,1)S(1)} %collective-permute-done.3.own), channel_id=1, source_target_pairs={{0,8},{1,9},{2,10},{3,11},{4,12},{5,13},{6,14},{7,15},{8,0},{9,1},... | collective-permute-start | bytes 49160 | tf_op jit(solution)/shard_map/ppermute | solution.py:304

commit v9 on v8

--- a/solution.py
+++ b/solution.py
@@ -231,26 +231,26 @@
     )(*(in_vmem(block) for block, _ in second), in_vmem(lags), *(in_vmem(block) for block, _ in first))
 
 
-def stage_kernel(row_masks, right, table, *refs):
+def stage_kernel(row_masks, right, table, after, *refs):
     *first_refs, ready, left, cross = refs
     cross_spectra(first_refs, left, right, cross, right.shape[1] // SEG)
     correlations(cross, table, ready, row_masks)
 
 
-def stage(count, row_masks, right, lags, first):
+def stage(count, row_masks, right, lags, after, first):
     n_row = len(row_masks)
     rows = sum(block.shape[0] for block in first)
     return pl.pallas_call(
         functools.partial(stage_kernel, row_masks),
         out_shape=pltpu.VMEM((rows // SEG, 1, n_row, count, LAGS), jnp.bfloat16),
-        in_specs=[VMEM] * (2 + len(first)),
+        in_specs=[VMEM] * (3 + len(first)),
         out_specs=VMEM,
         scratch_shapes=[
             pltpu.VMEM((rows, 2 * BINS), jnp.float32),
             pltpu.VMEM((rows // SEG * count * n_row, 2 * BINS), jnp.float32),
         ],
         name="stage",
-    )(*(in_vmem(block) for block in (right, lags, *first)))
+    )(*(in_vmem(block) for block in (right, lags, after, *first)))
 
 
 def correlate_kernel(count, n_ready, masks, bits, row_masks, *refs):
@@ -342,12 +342,10 @@
             bit *= 2
     lags = jnp.asarray(lag_table())
     right, *ready = prepare(count, row_masks, second, lags, [(own, pl.ds(0, held))])
-    ready += [stage(count, row_masks, right, lags, [other, near[0]])]
-    masks = [0, FAR]
-    for step in (STEPS[0], *STEPS[:0:-1]):
-        masks += [step ^ FAR, step]
-    last = near[:0:-1]
-    return correlate(count, n_row, n_col, masks, bits, row_masks, ready, right, lags, last)
+    for blocks in ([other, near[0]], [near[1]]):
+        ready += [stage(count, row_masks, right, lags, ready[-1], blocks)]
+    masks = [0, FAR] + [mask for step in STEPS for mask in (step ^ FAR, step)]
+    return correlate(count, n_row, n_col, masks, bits, row_masks, ready, right, lags, near[2:])
 
 
 def solution(mesh):

time: 14.2 us -> 14.2 us (level)
  waiting for transfers between devices: 1.7 us -> 1.5 us
    pallas_call x1 -> x2, Pallas kernels: 0.36 us -> 0.62 us  [stage(): pl.pallas_call(functools.partial(stage_kernel, row_masks), out_shape=pltp...]
    ppermute x8, waiting for transfers between devices: 1.7 us -> 1.5 us  [swap(): return lax.ppermute(block, ('row', 'col'), pairs)]
  transfers between devices with their start and end apart: 8 -> 8, of which waited for: 3 -> 2; matrix products, arithmetic and copies ran while one was open for 0% -> 0% of each run, Pallas kernels for 4% -> 6%
where the time goes in v9:
time: 14.2 us; the launch traced here: 14 us
  starting transfers between devices  9.24 us (65%)
  Pallas kernels  3.21 us (23%)
  waiting for transfers between devices  1.5 us (11%)
    ppermute x8, starting transfers between devices, swap(): return lax.ppermute(block, ('row', 'col'), pairs)  9.24 us
    ppermute x8, waiting for transfers between devices, swap(): return lax.ppermute(block, ('row', 'col'), pairs)  1.5 us
    pallas_call x1, Pallas kernels, whiten(): pl.pallas_call(whiten_kernel, out_shape=pltpu.VMEM((count * SEG, 2 * BINS...  1.37 us
    pallas_call x1, Pallas kernels, correlate(): pl.pallas_call(functools.partial(correlate_kernel, count, len(ready), mas...  0.96 us
    pallas_call x2, Pallas kernels, stage(): pl.pallas_call(functools.partial(stage_kernel, row_masks), out_shape=pltp...  0.62 us
  transfers between devices with their start and end apart: 8, of which 2 were waited for; matrix products, arithmetic and copies ran while one was open for 0% of the time, Pallas kernels for 6%

profile of v9, /device:TPU:0, one launch (start us, length us, event | category | flops | bytes accessed | tf_op | source)
XLA Modules:
  0.0 14.0 jit_solution(15171197800426950835)
XLA Ops:
  0.0 1.4 %whiten.1.refs_0_.refs_5_ = bf16[16,512]{1,0:T(8,128)(2,1)S(1)} custom-call(s32[2,8]{1,0:T(2,128)} %offsets.1, s32[2]{0:T(128)} %band_lo.1, s32[2]{0:T(128)} %band_hi.1, s32[2]{0:T(128)} %live.1, f32[2,4096]{1,0:T(2,128)} %traces.1, f32[8,256]{1,0:T(8,128)} %constant.6.clone.waves, bf16[2,128,512]{2,1,0:T(8,128)(2,1)} %constant.7.clone.table), custom_call_target="tpu_custom_call" | custom-call | tf_op jit(solution)/shard_map/whiten/pallas_call | solution.py:132
  1.4 0.0 copy-start
  1.4 3.5 %collective-permute-start.3 = (bf16[16,512]{1,0:T(8,128)(2,1)S(1)}, bf16[16,512]{1,0:T(8,128)(2,1)S(1)}, u32[]{:S(2)}, u32[]{:S(2)}) collective-permute-start(bf16[16,512]{1,0:T(8,128)(2,1)S(1)} %whiten.1.refs_0_.refs_5_), channel_id=1, source_target_pairs={{0,12},{1,13},{2,14},{3,15},{4,8},{5,9},{6,10},{7,11},{8,4},{9,5},... | collective-permute-start | bytes 49160 | tf_op jit(solution)/shard_map/ppermute | solution.py:304
  4.9 0.7 %collective-permute-start = (bf16[16,512]{1,0:T(8,128)(2,1)S(1)}, bf16[16,512]{1,0:T(8,128)(2,1)S(1)}, u32[]{:S(2)}, u32[]{:S(2)}) collective-permute-start(bf16[16,512]{1,0:T(8,128)(2,1)S(1)} %whiten.1.refs_0_.refs_5_), channel_id=1, source_target_pairs={{0,8},{1,9},{2,10},{3,11},{4,12},{5,13},{6,14},{7,15},{8,0},{9,1},... | collective-permute-start | bytes 49160 | tf_op jit(solution)/shard_map/ppermute | solution.py:304
  5.6 1.1 %collective-permute-start.1 = (bf16[16,512]{1,0:T(8,128)(2,1)S(1)}, bf16[16,512]{1,0:T(8,128)(2,1)S(1)}, u32[]{:S(2)}, u32[]{:S(2)}) collective-permute-start(bf16[16,512]{1,0:T(8,128)(2,1)S(1)} %whiten.1.refs_0_.refs_5_), channel_id=1, source_target_pairs={{0,24},{1,25},{2,26},{3,27},{4,28},{5,29},{6,30},{7,31},{8,16},{9,... | collective-permute-start | bytes 49160 | tf_op jit(solution)/shard_map/ppermute | solution.py:304
  6.7 0.0 collective-permute-done.3.own
  6.7 0.0 collective-permute-done.refs_1_.other
  6.7 2.7 %collective-permute-start.5 = (bf16[32,512]{1,0:T(8,128)(2,1)S(1)}, bf16[32,512]{1,0:T(8,128)(2,1)S(1)}, u32[]{:S(2)}, u32[]{:S(2)}) collective-permute-start(bf16[32,512]{1,0:T(8,128)(2,1)S(1)} %join.1), channel_id=1, source_target_pairs={{0,11},{1,10},{2,9},{3,8},{4,15},{5,14},{6,13},{7,12},{8,3},{9,2},... | collective-permute-start | bytes 98312 | tf_op jit(solution)/shard_map/ppermute | solution.py:304
  9.4 0.2 %collective-permute-start.6 = (bf16[32,512]{1,0:T(8,128)(2,1)S(1)}, bf16[32,512]{1,0:T(8,128)(2,1)S(1)}, u32[]{:S(2)}, u32[]{:S(2)}) collective-permute-start(bf16[32,512]{1,0:T(8,128)(2,1)S(1)} %join.1), channel_id=1, source_target_pairs={{0,10},{1,11},{2,8},{3,9},{4,14},{5,15},{6,12},{7,13},{8,2},{9,3},... | collective-permute-start | bytes 98312 | tf_op jit(solution)/shard_map/ppermute | solution.py:304
  9.6 0.5 %collective-permute-start.7 = (bf16[32,512]{1,0:T(8,128)(2,1)S(1)}, bf16[32,512]{1,0:T(8,128)(2,1)S(1)}, u32[]{:S(2)}, u32[]{:S(2)}) collective-permute-start(bf16[32,512]{1,0:T(8,128)(2,1)S(1)} %join.1), channel_id=1, source_target_pairs={{0,9},{1,8},{2,11},{3,10},{4,13},{5,12},{6,15},{7,14},{8,1},{9,0},... | collective-permute-start | bytes 98312 | tf_op jit(solution)/shard_map/ppermute | solution.py:304
  10.1 0.0 collective-permute-done.1.refs_2_
  10.1 0.1 collective-permute-start.2
  10.2 0.5 %collective-permute-start.4 = (bf16[16,512]{1,0:T(8,128)(2,1)S(1)}, bf16[16,512]{1,0:T(8,128)(2,1)S(1)}, u32[]{:S(2)}, u32[]{:S(2)}) collective-permute-start(bf16[16,512]{1,0:T(8,128)(2,1)S(1)} %collective-permute-done.3.own), channel_id=1, source_target_pairs={{0,8},{1,9},{2,10},{3,11},{4,12},{5,13},{6,14},{7,15},{8,0},{9,1},... | collective-permute-start | bytes 49160 | tf_op jit(solution)/shard_map/ppermute | solution.py:304
  10.6 0.7 %collective-permute-done.2.refs_3_ = bf16[16,512]{1,0:T(8,128)(2,1)S(1)} collective-permute-done((bf16[16,512]{1,0:T(8,128)(2,1)S(1)}, bf16[16,512]{1,0:T(8,128)(2,1)S(1)}, u32[]{:S(2)}, u32[]{:S(2)}) %collective-permute-start.2) | collective-permute-done | bytes 16416 | tf_op jit(solution)/shard_map/ppermute | solution.py:304
  11.3 0.0 copy-done
  11.3 0.3 %prepare.1 = (f32[4,64,128]{2,1,0:T(8,128)S(1)}, bf16[2,1,4,2,512]{4,3,2,1,0:T(2,128)(2,1)S(1)}) custom-call(bf16[16,512]{1,0:T(8,128)(2,1)S(1)} %whiten.1.refs_0_.refs_5_, bf16[16,512]{1,0:T(8,128)(2,1)S(1)} %collective-permute-done.refs_1_.other, bf16[16,512]{1,0:T(8,128)(2,1)S(1)} %collective-permute-done.1.refs_2_, ...), custom_call_target="tpu_custom_call" | custom-call | tf_op jit(solution)/shard_map/prepare/pallas_call | solution.py:218
  11.6 0.0 collective-permute-done.4.refs_0_
  11.6 0.0 collective-permute-done.5.refs_1_
  11.6 0.4 %stage.2.after.refs_1_ = bf16[6,1,4,2,512]{4,3,2,1,0:T(2,128)(2,1)S(1)} custom-call(f32[4,64,128]{2,1,0:T(8,128)S(1)} %get-tuple-element.8.right.refs_3_, bf16[512,512]{1,0:T(8,128)(2,1)S(1)} %copy-done, bf16[2,1,4,2,512]{4,3,2,1,0:T(2,128)(2,1)S(1)} %get-tuple-element.7.after.refs_0_, bf16[16,512]{1,0:T(8,128)(2,1)S(1)} %collective-permute-done.4.refs_0_, ...), custom_call_target="tpu_custom_call" | custom-call | tf_op jit(solution)/shard_map/stage/pallas_call | solution.py:243
  12.0 0.8 %collective-permute-done.6.refs_0_ = bf16[32,512]{1,0:T(8,128)(2,1)S(1)} collective-permute-done((bf16[32,512]{1,0:T(8,128)(2,1)S(1)}, bf16[32,512]{1,0:T(8,128)(2,1)S(1)}, u32[]{:S(2)}, u32[]{:S(2)}) %collective-permute-start.6) | collective-permute-done | bytes 32800 | tf_op jit(solution)/shard_map/ppermute | solution.py:304
  12.8 0.3 %stage.3.refs_2_ = bf16[4,1,4,2,512]{4,3,2,1,0:T(2,128)(2,1)S(1)} custom-call(f32[4,64,128]{2,1,0:T(8,128)S(1)} %get-tuple-element.8.right.refs_3_, bf16[512,512]{1,0:T(8,128)(2,1)S(1)} %copy-done, bf16[6,1,4,2,512]{4,3,2,1,0:T(2,128)(2,1)S(1)} %stage.2.after.refs_1_, bf16[32,512]{1,0:T(8,128)(2,1)S(1)} %collective-permute-done.6.refs_0_), custom_call_target="tpu_custom_call" | custom-call | tf_op jit(solution)/shard_map/stage/pallas_call | solution.py:243
  13.1 0.0 collective-permute-done.7.refs_5_
  13.1 1.0 %correlate.1 = bf16[16,1,4,2,512]{4,3,2,1,0:T(2,128)(2,1)} custom-call(bf16[2,1,4,2,512]{4,3,2,1,0:T(2,128)(2,1)S(1)} %get-tuple-element.7.after.refs_0_, bf16[6,1,4,2,512]{4,3,2,1,0:T(2,128)(2,1)S(1)} %stage.2.after.refs_1_, bf16[4,1,4,2,512]{4,3,2,1,0:T(2,128)(2,1)S(1)} %stage.3.refs_2_, f32[4,64,128]{2,1,0:T(8,128)S(1)} %get-tuple-element.8.right.refs_3_, ...), custom_call_target="tpu_custom_call" | custom-call | tf_op jit(solution)/shard_map/correlate/pallas_call | solution.py:282
  (1 shorter events, 0.0 us)
Async XLA Ops:
  1.4 9.9 %copy-start = (bf16[512,512]{1,0:T(8,128)(2,1)S(1)}, bf16[512,512]{1,0:T(8,128)(2,1)}, u32[]{:S(2)}) copy-start(bf16[512,512]{1,0:T(8,128)(2,1)} %constant.8.clone.refs_4_.table) | copy-start | bytes 1572868
  1.4 5.3 %collective-permute-start.3 = (bf16[16,512]{1,0:T(8,128)(2,1)S(1)}, bf16[16,512]{1,0:T(8,128)(2,1)S(1)}, u32[]{:S(2)}, u32[]{:S(2)}) collective-permute-start(bf16[16,512]{1,0:T(8,128)(2,1)S(1)} %whiten.1.refs_0_.refs_5_), channel_id=1, source_target_pairs={{0,12},{1,13},{2,14},{3,15},{4,8},{5,9},{6,10},{7,11},{8,4},{9,5},... | collective-permute-start | bytes 49160 | tf_op jit(solution)/shard_map/ppermute | solution.py:304
  4.9 1.8 %collective-permute-start = (bf16[16,512]{1,0:T(8,128)(2,1)S(1)}, bf16[16,512]{1,0:T(8,128)(2,1)S(1)}, u32[]{:S(2)}, u32[]{:S(2)}) collective-permute-start(bf16[16,512]{1,0:T(8,128)(2,1)S(1)} %whiten.1.refs_0_.refs_5_), channel_id=1, source_target_pairs={{0,8},{1,9},{2,10},{3,11},{4,12},{5,13},{6,14},{7,15},{8,0},{9,1},... | collective-permute-start | bytes 49160 | tf_op jit(solution)/shard_map/ppermute | solution.py:304
  5.6 4.5 %collective-permute-start.1 = (bf16[16,512]{1,0:T(8,128)(2,1)S(1)}, bf16[16,512]{1,0:T(8,128)(2,1)S(1)}, u32[]{:S(2)}, u32[]{:S(2)}) collective-permute-start(bf16[16,512]{1,0:T(8,128)(2,1)S(1)} %whiten.1.refs_0_.refs_5_), channel_id=1, source_target_pairs={{0,24},{1,25},{2,26},{3,27},{4,28},{5,29},{6,30},{7,31},{8,16},{9,... | collective-permute-start | bytes 49160 | tf_op jit(solution)/shard_map/ppermute | solution.py:304
  6.7 4.9 %collective-permute-start.5 = (bf16[32,512]{1,0:T(8,128)(2,1)S(1)}, bf16[32,512]{1,0:T(8,128)(2,1)S(1)}, u32[]{:S(2)}, u32[]{:S(2)}) collective-permute-start(bf16[32,512]{1,0:T(8,128)(2,1)S(1)} %join.1), channel_id=1, source_target_pairs={{0,11},{1,10},{2,9},{3,8},{4,15},{5,14},{6,13},{7,12},{8,3},{9,2},... | collective-permute-start | bytes 98312 | tf_op jit(solution)/shard_map/ppermute | solution.py:304
  9.4 3.3 %collective-permute-start.6 = (bf16[32,512]{1,0:T(8,128)(2,1)S(1)}, bf16[32,512]{1,0:T(8,128)(2,1)S(1)}, u32[]{:S(2)}, u32[]{:S(2)}) collective-permute-start(bf16[32,512]{1,0:T(8,128)(2,1)S(1)} %join.1), channel_id=1, source_target_pairs={{0,10},{1,11},{2,8},{3,9},{4,14},{5,15},{6,12},{7,13},{8,2},{9,3},... | collective-permute-start | bytes 98312 | tf_op jit(solution)/shard_map/ppermute | solution.py:304
  9.6 3.4 %collective-permute-start.7 = (bf16[32,512]{1,0:T(8,128)(2,1)S(1)}, bf16[32,512]{1,0:T(8,128)(2,1)S(1)}, u32[]{:S(2)}, u32[]{:S(2)}) collective-permute-start(bf16[32,512]{1,0:T(8,128)(2,1)S(1)} %join.1), channel_id=1, source_target_pairs={{0,9},{1,8},{2,11},{3,10},{4,13},{5,12},{6,15},{7,14},{8,1},{9,0},... | collective-permute-start | bytes 98312 | tf_op jit(solution)/shard_map/ppermute | solution.py:304
  10.1 1.2 %collective-permute-start.2 = (bf16[16,512]{1,0:T(8,128)(2,1)S(1)}, bf16[16,512]{1,0:T(8,128)(2,1)S(1)}, u32[]{:S(2)}, u32[]{:S(2)}) collective-permute-start(bf16[16,512]{1,0:T(8,128)(2,1)S(1)} %collective-permute-done.1.refs_2_), channel_id=1, source_target_pairs={{0,8},{1,9},{2,10},{3,11},{4,12},{5,13},{6,14},{7,15},{8,0},{9,1},... | collective-permute-start | bytes 49160 | tf_op jit(solution)/shard_map/ppermute | solution.py:304
  10.2 1.4 %collective-permute-start.4 = (bf16[16,512]{1,0:T(8,128)(2,1)S(1)}, bf16[16,512]{1,0:T(8,128)(2,1)S(1)}, u32[]{:S(2)}, u32[]{:S(2)}) collective-permute-start(bf16[16,512]{1,0:T(8,128)(2,1)S(1)} %collective-permute-done.3.own), channel_id=1, source_target_pairs={{0,8},{1,9},{2,10},{3,11},{4,12},{5,13},{6,14},{7,15},{8,0},{9,1},... | collective-permute-start | bytes 49160 | tf_op jit(solution)/shard_map/ppermute | solution.py:304

commit v10 on v9

--- a/solution.py
+++ b/solution.py
@@ -266,9 +266,9 @@
         for n, (block, col) in enumerate(zip(blocks, cols, strict=True))
     ]
     early = len(blocks) - last.shape[0] // count
+    cross_spectra(first_refs, left, right, cross, count * len(row_masks))
     for copy in copies[:early]:
         copy.start()
-    cross_spectra(first_refs, left, right, cross, count * len(row_masks))
     correlations(cross, table, last, row_masks)
     for copy in copies[early:]:
         copy.start()

time: 14.2 us -> 14.2 us (level)
  no operation moved by 1% of the time
where the time goes in v10:
time: 14.2 us; the launch traced here: 14 us
  starting transfers between devices  9.24 us (65%)
  Pallas kernels  3.21 us (23%)
  waiting for transfers between devices  1.5 us (11%)
    ppermute x8, starting transfers between devices, swap(): return lax.ppermute(block, ('row', 'col'), pairs)  9.24 us
    ppermute x8, waiting for transfers between devices, swap(): return lax.ppermute(block, ('row', 'col'), pairs)  1.5 us
    pallas_call x1, Pallas kernels, whiten(): pl.pallas_call(whiten_kernel, out_shape=pltpu.VMEM((count * SEG, 2 * BINS...  1.37 us
    pallas_call x1, Pallas kernels, correlate(): pl.pallas_call(functools.partial(correlate_kernel, count, len(ready), mas...  0.96 us
    pallas_call x2, Pallas kernels, stage(): pl.pallas_call(functools.partial(stage_kernel, row_masks), out_shape=pltp...  0.62 us
  transfers between devices with their start and end apart: 8, of which 2 were waited for; matrix products, arithmetic and copies ran while one was open for 0% of the time, Pallas kernels for 6%

profile of v10, /device:TPU:0, one launch (start us, length us, event | category | flops | bytes accessed | tf_op | source)
XLA Modules:
  0.0 14.0 jit_solution(15171197800426950835)
XLA Ops:
  0.0 1.4 %whiten.1.refs_0_.refs_5_ = bf16[16,512]{1,0:T(8,128)(2,1)S(1)} custom-call(s32[2,8]{1,0:T(2,128)} %offsets.1, s32[2]{0:T(128)} %band_lo.1, s32[2]{0:T(128)} %band_hi.1, s32[2]{0:T(128)} %live.1, f32[2,4096]{1,0:T(2,128)} %traces.1, f32[8,256]{1,0:T(8,128)} %constant.6.clone.waves, bf16[2,128,512]{2,1,0:T(8,128)(2,1)} %constant.7.clone.table), custom_call_target="tpu_custom_call" | custom-call | tf_op jit(solution)/shard_map/whiten/pallas_call | solution.py:132
  1.4 0.0 copy-start
  1.4 3.5 %collective-permute-start.3 = (bf16[16,512]{1,0:T(8,128)(2,1)S(1)}, bf16[16,512]{1,0:T(8,128)(2,1)S(1)}, u32[]{:S(2)}, u32[]{:S(2)}) collective-permute-start(bf16[16,512]{1,0:T(8,128)(2,1)S(1)} %whiten.1.refs_0_.refs_5_), channel_id=1, source_target_pairs={{0,12},{1,13},{2,14},{3,15},{4,8},{5,9},{6,10},{7,11},{8,4},{9,5},... | collective-permute-start | bytes 49160 | tf_op jit(solution)/shard_map/ppermute | solution.py:304
  4.9 0.7 %collective-permute-start = (bf16[16,512]{1,0:T(8,128)(2,1)S(1)}, bf16[16,512]{1,0:T(8,128)(2,1)S(1)}, u32[]{:S(2)}, u32[]{:S(2)}) collective-permute-start(bf16[16,512]{1,0:T(8,128)(2,1)S(1)} %whiten.1.refs_0_.refs_5_), channel_id=1, source_target_pairs={{0,8},{1,9},{2,10},{3,11},{4,12},{5,13},{6,14},{7,15},{8,0},{9,1},... | collective-permute-start | bytes 49160 | tf_op jit(solution)/shard_map/ppermute | solution.py:304
  5.6 1.1 %collective-permute-start.1 = (bf16[16,512]{1,0:T(8,128)(2,1)S(1)}, bf16[16,512]{1,0:T(8,128)(2,1)S(1)}, u32[]{:S(2)}, u32[]{:S(2)}) collective-permute-start(bf16[16,512]{1,0:T(8,128)(2,1)S(1)} %whiten.1.refs_0_.refs_5_), channel_id=1, source_target_pairs={{0,24},{1,25},{2,26},{3,27},{4,28},{5,29},{6,30},{7,31},{8,16},{9,... | collective-permute-start | bytes 49160 | tf_op jit(solution)/shard_map/ppermute | solution.py:304
  6.7 0.0 collective-permute-done.3.own
  6.7 0.0 collective-permute-done.refs_1_.other
  6.7 2.7 %collective-permute-start.5 = (bf16[32,512]{1,0:T(8,128)(2,1)S(1)}, bf16[32,512]{1,0:T(8,128)(2,1)S(1)}, u32[]{:S(2)}, u32[]{:S(2)}) collective-permute-start(bf16[32,512]{1,0:T(8,128)(2,1)S(1)} %join.1), channel_id=1, source_target_pairs={{0,11},{1,10},{2,9},{3,8},{4,15},{5,14},{6,13},{7,12},{8,3},{9,2},... | collective-permute-start | bytes 98312 | tf_op jit(solution)/shard_map/ppermute | solution.py:304
  9.4 0.2 %collective-permute-start.6 = (bf16[32,512]{1,0:T(8,128)(2,1)S(1)}, bf16[32,512]{1,0:T(8,128)(2,1)S(1)}, u32[]{:S(2)}, u32[]{:S(2)}) collective-permute-start(bf16[32,512]{1,0:T(8,128)(2,1)S(1)} %join.1), channel_id=1, source_target_pairs={{0,10},{1,11},{2,8},{3,9},{4,14},{5,15},{6,12},{7,13},{8,2},{9,3},... | collective-permute-start | bytes 98312 | tf_op jit(solution)/shard_map/ppermute | solution.py:304
  9.6 0.5 %collective-permute-start.7 = (bf16[32,512]{1,0:T(8,128)(2,1)S(1)}, bf16[32,512]{1,0:T(8,128)(2,1)S(1)}, u32[]{:S(2)}, u32[]{:S(2)}) collective-permute-start(bf16[32,512]{1,0:T(8,128)(2,1)S(1)} %join.1), channel_id=1, source_target_pairs={{0,9},{1,8},{2,11},{3,10},{4,13},{5,12},{6,15},{7,14},{8,1},{9,0},... | collective-permute-start | bytes 98312 | tf_op jit(solution)/shard_map/ppermute | solution.py:304
  10.1 0.0 collective-permute-done.1.refs_2_
  10.1 0.1 collective-permute-start.2
  10.2 0.5 %collective-permute-start.4 = (bf16[16,512]{1,0:T(8,128)(2,1)S(1)}, bf16[16,512]{1,0:T(8,128)(2,1)S(1)}, u32[]{:S(2)}, u32[]{:S(2)}) collective-permute-start(bf16[16,512]{1,0:T(8,128)(2,1)S(1)} %collective-permute-done.3.own), channel_id=1, source_target_pairs={{0,8},{1,9},{2,10},{3,11},{4,12},{5,13},{6,14},{7,15},{8,0},{9,1},... | collective-permute-start | bytes 49160 | tf_op jit(solution)/shard_map/ppermute | solution.py:304
  10.6 0.7 %collective-permute-done.2.refs_3_ = bf16[16,512]{1,0:T(8,128)(2,1)S(1)} collective-permute-done((bf16[16,512]{1,0:T(8,128)(2,1)S(1)}, bf16[16,512]{1,0:T(8,128)(2,1)S(1)}, u32[]{:S(2)}, u32[]{:S(2)}) %collective-permute-start.2) | collective-permute-done | bytes 16416 | tf_op jit(solution)/shard_map/ppermute | solution.py:304
  11.3 0.0 copy-done
  11.3 0.3 %prepare.1 = (f32[4,64,128]{2,1,0:T(8,128)S(1)}, bf16[2,1,4,2,512]{4,3,2,1,0:T(2,128)(2,1)S(1)}) custom-call(bf16[16,512]{1,0:T(8,128)(2,1)S(1)} %whiten.1.refs_0_.refs_5_, bf16[16,512]{1,0:T(8,128)(2,1)S(1)} %collective-permute-done.refs_1_.other, bf16[16,512]{1,0:T(8,128)(2,1)S(1)} %collective-permute-done.1.refs_2_, ...), custom_call_target="tpu_custom_call" | custom-call | tf_op jit(solution)/shard_map/prepare/pallas_call | solution.py:218
  11.6 0.0 collective-permute-done.4.refs_0_
  11.6 0.0 collective-permute-done.5.refs_1_
  11.6 0.4 %stage.2.after.refs_1_ = bf16[6,1,4,2,512]{4,3,2,1,0:T(2,128)(2,1)S(1)} custom-call(f32[4,64,128]{2,1,0:T(8,128)S(1)} %get-tuple-element.8.right.refs_3_, bf16[512,512]{1,0:T(8,128)(2,1)S(1)} %copy-done, bf16[2,1,4,2,512]{4,3,2,1,0:T(2,128)(2,1)S(1)} %get-tuple-element.7.after.refs_0_, bf16[16,512]{1,0:T(8,128)(2,1)S(1)} %collective-permute-done.4.refs_0_, ...), custom_call_target="tpu_custom_call" | custom-call | tf_op jit(solution)/shard_map/stage/pallas_call | solution.py:243
  12.0 0.8 %collective-permute-done.6.refs_0_ = bf16[32,512]{1,0:T(8,128)(2,1)S(1)} collective-permute-done((bf16[32,512]{1,0:T(8,128)(2,1)S(1)}, bf16[32,512]{1,0:T(8,128)(2,1)S(1)}, u32[]{:S(2)}, u32[]{:S(2)}) %collective-permute-start.6) | collective-permute-done | bytes 32800 | tf_op jit(solution)/shard_map/ppermute | solution.py:304
  12.8 0.3 %stage.3.refs_2_ = bf16[4,1,4,2,512]{4,3,2,1,0:T(2,128)(2,1)S(1)} custom-call(f32[4,64,128]{2,1,0:T(8,128)S(1)} %get-tuple-element.8.right.refs_3_, bf16[512,512]{1,0:T(8,128)(2,1)S(1)} %copy-done, bf16[6,1,4,2,512]{4,3,2,1,0:T(2,128)(2,1)S(1)} %stage.2.after.refs_1_, bf16[32,512]{1,0:T(8,128)(2,1)S(1)} %collective-permute-done.6.refs_0_), custom_call_target="tpu_custom_call" | custom-call | tf_op jit(solution)/shard_map/stage/pallas_call | solution.py:243
  13.1 0.0 collective-permute-done.7.refs_5_
  13.1 1.0 %correlate.1 = bf16[16,1,4,2,512]{4,3,2,1,0:T(2,128)(2,1)} custom-call(bf16[2,1,4,2,512]{4,3,2,1,0:T(2,128)(2,1)S(1)} %get-tuple-element.7.after.refs_0_, bf16[6,1,4,2,512]{4,3,2,1,0:T(2,128)(2,1)S(1)} %stage.2.after.refs_1_, bf16[4,1,4,2,512]{4,3,2,1,0:T(2,128)(2,1)S(1)} %stage.3.refs_2_, f32[4,64,128]{2,1,0:T(8,128)S(1)} %get-tuple-element.8.right.refs_3_, ...), custom_call_target="tpu_custom_call" | custom-call | tf_op jit(solution)/shard_map/correlate/pallas_call | solution.py:282
  (1 shorter events, 0.0 us)
Async XLA Ops:
  1.4 9.9 %copy-start = (bf16[512,512]{1,0:T(8,128)(2,1)S(1)}, bf16[512,512]{1,0:T(8,128)(2,1)}, u32[]{:S(2)}) copy-start(bf16[512,512]{1,0:T(8,128)(2,1)} %constant.8.clone.refs_4_.table) | copy-start | bytes 1572868
  1.4 5.3 %collective-permute-start.3 = (bf16[16,512]{1,0:T(8,128)(2,1)S(1)}, bf16[16,512]{1,0:T(8,128)(2,1)S(1)}, u32[]{:S(2)}, u32[]{:S(2)}) collective-permute-start(bf16[16,512]{1,0:T(8,128)(2,1)S(1)} %whiten.1.refs_0_.refs_5_), channel_id=1, source_target_pairs={{0,12},{1,13},{2,14},{3,15},{4,8},{5,9},{6,10},{7,11},{8,4},{9,5},... | collective-permute-start | bytes 49160 | tf_op jit(solution)/shard_map/ppermute | solution.py:304
  4.9 1.8 %collective-permute-start = (bf16[16,512]{1,0:T(8,128)(2,1)S(1)}, bf16[16,512]{1,0:T(8,128)(2,1)S(1)}, u32[]{:S(2)}, u32[]{:S(2)}) collective-permute-start(bf16[16,512]{1,0:T(8,128)(2,1)S(1)} %whiten.1.refs_0_.refs_5_), channel_id=1, source_target_pairs={{0,8},{1,9},{2,10},{3,11},{4,12},{5,13},{6,14},{7,15},{8,0},{9,1},... | collective-permute-start | bytes 49160 | tf_op jit(solution)/shard_map/ppermute | solution.py:304
  5.6 4.5 %collective-permute-start.1 = (bf16[16,512]{1,0:T(8,128)(2,1)S(1)}, bf16[16,512]{1,0:T(8,128)(2,1)S(1)}, u32[]{:S(2)}, u32[]{:S(2)}) collective-permute-start(bf16[16,512]{1,0:T(8,128)(2,1)S(1)} %whiten.1.refs_0_.refs_5_), channel_id=1, source_target_pairs={{0,24},{1,25},{2,26},{3,27},{4,28},{5,29},{6,30},{7,31},{8,16},{9,... | collective-permute-start | bytes 49160 | tf_op jit(solution)/shard_map/ppermute | solution.py:304
  6.7 4.9 %collective-permute-start.5 = (bf16[32,512]{1,0:T(8,128)(2,1)S(1)}, bf16[32,512]{1,0:T(8,128)(2,1)S(1)}, u32[]{:S(2)}, u32[]{:S(2)}) collective-permute-start(bf16[32,512]{1,0:T(8,128)(2,1)S(1)} %join.1), channel_id=1, source_target_pairs={{0,11},{1,10},{2,9},{3,8},{4,15},{5,14},{6,13},{7,12},{8,3},{9,2},... | collective-permute-start | bytes 98312 | tf_op jit(solution)/shard_map/ppermute | solution.py:304
  9.4 3.3 %collective-permute-start.6 = (bf16[32,512]{1,0:T(8,128)(2,1)S(1)}, bf16[32,512]{1,0:T(8,128)(2,1)S(1)}, u32[]{:S(2)}, u32[]{:S(2)}) collective-permute-start(bf16[32,512]{1,0:T(8,128)(2,1)S(1)} %join.1), channel_id=1, source_target_pairs={{0,10},{1,11},{2,8},{3,9},{4,14},{5,15},{6,12},{7,13},{8,2},{9,3},... | collective-permute-start | bytes 98312 | tf_op jit(solution)/shard_map/ppermute | solution.py:304
  9.6 3.4 %collective-permute-start.7 = (bf16[32,512]{1,0:T(8,128)(2,1)S(1)}, bf16[32,512]{1,0:T(8,128)(2,1)S(1)}, u32[]{:S(2)}, u32[]{:S(2)}) collective-permute-start(bf16[32,512]{1,0:T(8,128)(2,1)S(1)} %join.1), channel_id=1, source_target_pairs={{0,9},{1,8},{2,11},{3,10},{4,13},{5,12},{6,15},{7,14},{8,1},{9,0},... | collective-permute-start | bytes 98312 | tf_op jit(solution)/shard_map/ppermute | solution.py:304
  10.1 1.2 %collective-permute-start.2 = (bf16[16,512]{1,0:T(8,128)(2,1)S(1)}, bf16[16,512]{1,0:T(8,128)(2,1)S(1)}, u32[]{:S(2)}, u32[]{:S(2)}) collective-permute-start(bf16[16,512]{1,0:T(8,128)(2,1)S(1)} %collective-permute-done.1.refs_2_), channel_id=1, source_target_pairs={{0,8},{1,9},{2,10},{3,11},{4,12},{5,13},{6,14},{7,15},{8,0},{9,1},... | collective-permute-start | bytes 49160 | tf_op jit(solution)/shard_map/ppermute | solution.py:304
  10.2 1.4 %collective-permute-start.4 = (bf16[16,512]{1,0:T(8,128)(2,1)S(1)}, bf16[16,512]{1,0:T(8,128)(2,1)S(1)}, u32[]{:S(2)}, u32[]{:S(2)}) collective-permute-start(bf16[16,512]{1,0:T(8,128)(2,1)S(1)} %collective-permute-done.3.own), channel_id=1, source_target_pairs={{0,8},{1,9},{2,10},{3,11},{4,12},{5,13},{6,14},{7,15},{8,0},{9,1},... | collective-permute-start | bytes 49160 | tf_op jit(solution)/shard_map/ppermute | solution.py:304

commit v11 on v9

--- a/solution.py
+++ b/solution.py
@@ -145,7 +145,7 @@
         left[at : at + ref.shape[0], :] = ref[...].astype(jnp.float32)
         at += ref.shape[0]
 
-    @pl.loop(0, left.shape[0] // SEG, unroll=4)
+    @pl.loop(0, left.shape[0] // SEG, unroll=2)
     def _(i):
         there = pl.ds(pl.multiple_of(i * wide, wide), wide)
         segments = pl.ds(pl.multiple_of(i * SEG, SEG), SEG)

time: 14.2 us -> 14.2 us (level)
  no operation moved by 1% of the time
where the time goes in v11:
time: 14.2 us; the launch traced here: 14.1 us
  starting transfers between devices  9.24 us (65%)
  Pallas kernels  3.25 us (23%)
  waiting for transfers between devices  1.53 us (11%)
    ppermute x8, starting transfers between devices, swap(): return lax.ppermute(block, ('row', 'col'), pairs)  9.24 us
    ppermute x8, waiting for transfers between devices, swap(): return lax.ppermute(block, ('row', 'col'), pairs)  1.53 us
    pallas_call x1, Pallas kernels, whiten(): pl.pallas_call(whiten_kernel, out_shape=pltpu.VMEM((count * SEG, 2 * BINS...  1.37 us
    pallas_call x1, Pallas kernels, correlate(): pl.pallas_call(functools.partial(correlate_kernel, count, len(ready), mas...  0.99 us
    pallas_call x2, Pallas kernels, stage(): pl.pallas_call(functools.partial(stage_kernel, row_masks), out_shape=pltp...  0.65 us
  transfers between devices with their start and end apart: 8, of which 2 were waited for; matrix products, arithmetic and copies ran while one was open for 0% of the time, Pallas kernels for 6%

profile of v11, /device:TPU:0, one launch (start us, length us, event | category | flops | bytes accessed | tf_op | source)
XLA Modules:
  0.0 14.1 jit_solution(13788908992329735373)
XLA Ops:
  0.0 1.4 %whiten.1.refs_0_.refs_5_ = bf16[16,512]{1,0:T(8,128)(2,1)S(1)} custom-call(s32[2,8]{1,0:T(2,128)} %offsets.1, s32[2]{0:T(128)} %band_lo.1, s32[2]{0:T(128)} %band_hi.1, s32[2]{0:T(128)} %live.1, f32[2,4096]{1,0:T(2,128)} %traces.1, f32[8,256]{1,0:T(8,128)} %constant.6.clone.waves, bf16[2,128,512]{2,1,0:T(8,128)(2,1)} %constant.7.clone.table), custom_call_target="tpu_custom_call" | custom-call | tf_op jit(solution)/shard_map/whiten/pallas_call | solution.py:132
  1.4 0.0 copy-start
  1.4 3.5 %collective-permute-start.3 = (bf16[16,512]{1,0:T(8,128)(2,1)S(1)}, bf16[16,512]{1,0:T(8,128)(2,1)S(1)}, u32[]{:S(2)}, u32[]{:S(2)}) collective-permute-start(bf16[16,512]{1,0:T(8,128)(2,1)S(1)} %whiten.1.refs_0_.refs_5_), channel_id=1, source_target_pairs={{0,12},{1,13},{2,14},{3,15},{4,8},{5,9},{6,10},{7,11},{8,4},{9,5},... | collective-permute-start | bytes 49160 | tf_op jit(solution)/shard_map/ppermute | solution.py:304
  4.9 0.7 %collective-permute-start = (bf16[16,512]{1,0:T(8,128)(2,1)S(1)}, bf16[16,512]{1,0:T(8,128)(2,1)S(1)}, u32[]{:S(2)}, u32[]{:S(2)}) collective-permute-start(bf16[16,512]{1,0:T(8,128)(2,1)S(1)} %whiten.1.refs_0_.refs_5_), channel_id=1, source_target_pairs={{0,8},{1,9},{2,10},{3,11},{4,12},{5,13},{6,14},{7,15},{8,0},{9,1},... | collective-permute-start | bytes 49160 | tf_op jit(solution)/shard_map/ppermute | solution.py:304
  5.6 1.1 %collective-permute-start.1 = (bf16[16,512]{1,0:T(8,128)(2,1)S(1)}, bf16[16,512]{1,0:T(8,128)(2,1)S(1)}, u32[]{:S(2)}, u32[]{:S(2)}) collective-permute-start(bf16[16,512]{1,0:T(8,128)(2,1)S(1)} %whiten.1.refs_0_.refs_5_), channel_id=1, source_target_pairs={{0,24},{1,25},{2,26},{3,27},{4,28},{5,29},{6,30},{7,31},{8,16},{9,... | collective-permute-start | bytes 49160 | tf_op jit(solution)/shard_map/ppermute | solution.py:304
  6.7 0.0 collective-permute-done.3.own
  6.7 0.0 collective-permute-done.refs_1_.other
  6.7 2.7 %collective-permute-start.5 = (bf16[32,512]{1,0:T(8,128)(2,1)S(1)}, bf16[32,512]{1,0:T(8,128)(2,1)S(1)}, u32[]{:S(2)}, u32[]{:S(2)}) collective-permute-start(bf16[32,512]{1,0:T(8,128)(2,1)S(1)} %join.1), channel_id=1, source_target_pairs={{0,11},{1,10},{2,9},{3,8},{4,15},{5,14},{6,13},{7,12},{8,3},{9,2},... | collective-permute-start | bytes 98312 | tf_op jit(solution)/shard_map/ppermute | solution.py:304
  9.4 0.2 %collective-permute-start.6 = (bf16[32,512]{1,0:T(8,128)(2,1)S(1)}, bf16[32,512]{1,0:T(8,128)(2,1)S(1)}, u32[]{:S(2)}, u32[]{:S(2)}) collective-permute-start(bf16[32,512]{1,0:T(8,128)(2,1)S(1)} %join.1), channel_id=1, source_target_pairs={{0,10},{1,11},{2,8},{3,9},{4,14},{5,15},{6,12},{7,13},{8,2},{9,3},... | collective-permute-start | bytes 98312 | tf_op jit(solution)/shard_map/ppermute | solution.py:304
  9.6 0.5 %collective-permute-start.7 = (bf16[32,512]{1,0:T(8,128)(2,1)S(1)}, bf16[32,512]{1,0:T(8,128)(2,1)S(1)}, u32[]{:S(2)}, u32[]{:S(2)}) collective-permute-start(bf16[32,512]{1,0:T(8,128)(2,1)S(1)} %join.1), channel_id=1, source_target_pairs={{0,9},{1,8},{2,11},{3,10},{4,13},{5,12},{6,15},{7,14},{8,1},{9,0},... | collective-permute-start | bytes 98312 | tf_op jit(solution)/shard_map/ppermute | solution.py:304
  10.1 0.0 collective-permute-done.1.refs_2_
  10.1 0.1 collective-permute-start.2
  10.2 0.5 %collective-permute-start.4 = (bf16[16,512]{1,0:T(8,128)(2,1)S(1)}, bf16[16,512]{1,0:T(8,128)(2,1)S(1)}, u32[]{:S(2)}, u32[]{:S(2)}) collective-permute-start(bf16[16,512]{1,0:T(8,128)(2,1)S(1)} %collective-permute-done.3.own), channel_id=1, source_target_pairs={{0,8},{1,9},{2,10},{3,11},{4,12},{5,13},{6,14},{7,15},{8,0},{9,1},... | collective-permute-start | bytes 49160 | tf_op jit(solution)/shard_map/ppermute | solution.py:304
  10.6 0.7 %collective-permute-done.2.refs_3_ = bf16[16,512]{1,0:T(8,128)(2,1)S(1)} collective-permute-done((bf16[16,512]{1,0:T(8,128)(2,1)S(1)}, bf16[16,512]{1,0:T(8,128)(2,1)S(1)}, u32[]{:S(2)}, u32[]{:S(2)}) %collective-permute-start.2) | collective-permute-done | bytes 16416 | tf_op jit(solution)/shard_map/ppermute | solution.py:304
  11.3 0.0 copy-done
  11.3 0.2 %prepare.1 = (f32[4,64,128]{2,1,0:T(8,128)S(1)}, bf16[2,1,4,2,512]{4,3,2,1,0:T(2,128)(2,1)S(1)}) custom-call(bf16[16,512]{1,0:T(8,128)(2,1)S(1)} %whiten.1.refs_0_.refs_5_, bf16[16,512]{1,0:T(8,128)(2,1)S(1)} %collective-permute-done.refs_1_.other, bf16[16,512]{1,0:T(8,128)(2,1)S(1)} %collective-permute-done.1.refs_2_, ...), custom_call_target="tpu_custom_call" | custom-call | tf_op jit(solution)/shard_map/prepare/pallas_call | solution.py:218
  11.6 0.0 collective-permute-done.4.refs_0_
  11.6 0.0 collective-permute-done.5.refs_1_
  11.6 0.4 %stage.2.after.refs_1_ = bf16[6,1,4,2,512]{4,3,2,1,0:T(2,128)(2,1)S(1)} custom-call(f32[4,64,128]{2,1,0:T(8,128)S(1)} %get-tuple-element.8.right.refs_3_, bf16[512,512]{1,0:T(8,128)(2,1)S(1)} %copy-done, bf16[2,1,4,2,512]{4,3,2,1,0:T(2,128)(2,1)S(1)} %get-tuple-element.7.after.refs_0_, bf16[16,512]{1,0:T(8,128)(2,1)S(1)} %collective-permute-done.4.refs_0_, ...), custom_call_target="tpu_custom_call" | custom-call | tf_op jit(solution)/shard_map/stage/pallas_call | solution.py:243
  11.9 0.8 %collective-permute-done.6.refs_0_ = bf16[32,512]{1,0:T(8,128)(2,1)S(1)} collective-permute-done((bf16[32,512]{1,0:T(8,128)(2,1)S(1)}, bf16[32,512]{1,0:T(8,128)(2,1)S(1)}, u32[]{:S(2)}, u32[]{:S(2)}) %collective-permute-start.6) | collective-permute-done | bytes 32800 | tf_op jit(solution)/shard_map/ppermute | solution.py:304
  12.8 0.3 %stage.3.refs_2_ = bf16[4,1,4,2,512]{4,3,2,1,0:T(2,128)(2,1)S(1)} custom-call(f32[4,64,128]{2,1,0:T(8,128)S(1)} %get-tuple-element.8.right.refs_3_, bf16[512,512]{1,0:T(8,128)(2,1)S(1)} %copy-done, bf16[6,1,4,2,512]{4,3,2,1,0:T(2,128)(2,1)S(1)} %stage.2.after.refs_1_, bf16[32,512]{1,0:T(8,128)(2,1)S(1)} %collective-permute-done.6.refs_0_), custom_call_target="tpu_custom_call" | custom-call | tf_op jit(solution)/shard_map/stage/pallas_call | solution.py:243
  13.1 0.0 collective-permute-done.7.refs_5_
  13.1 1.0 %correlate.1 = bf16[16,1,4,2,512]{4,3,2,1,0:T(2,128)(2,1)} custom-call(bf16[2,1,4,2,512]{4,3,2,1,0:T(2,128)(2,1)S(1)} %get-tuple-element.7.after.refs_0_, bf16[6,1,4,2,512]{4,3,2,1,0:T(2,128)(2,1)S(1)} %stage.2.after.refs_1_, bf16[4,1,4,2,512]{4,3,2,1,0:T(2,128)(2,1)S(1)} %stage.3.refs_2_, f32[4,64,128]{2,1,0:T(8,128)S(1)} %get-tuple-element.8.right.refs_3_, ...), custom_call_target="tpu_custom_call" | custom-call | tf_op jit(solution)/shard_map/correlate/pallas_call | solution.py:282
  (1 shorter events, 0.0 us)
Async XLA Ops:
  1.4 9.9 %copy-start = (bf16[512,512]{1,0:T(8,128)(2,1)S(1)}, bf16[512,512]{1,0:T(8,128)(2,1)}, u32[]{:S(2)}) copy-start(bf16[512,512]{1,0:T(8,128)(2,1)} %constant.8.clone.refs_4_.table) | copy-start | bytes 1572868
  1.4 5.3 %collective-permute-start.3 = (bf16[16,512]{1,0:T(8,128)(2,1)S(1)}, bf16[16,512]{1,0:T(8,128)(2,1)S(1)}, u32[]{:S(2)}, u32[]{:S(2)}) collective-permute-start(bf16[16,512]{1,0:T(8,128)(2,1)S(1)} %whiten.1.refs_0_.refs_5_), channel_id=1, source_target_pairs={{0,12},{1,13},{2,14},{3,15},{4,8},{5,9},{6,10},{7,11},{8,4},{9,5},... | collective-permute-start | bytes 49160 | tf_op jit(solution)/shard_map/ppermute | solution.py:304
  4.9 1.8 %collective-permute-start = (bf16[16,512]{1,0:T(8,128)(2,1)S(1)}, bf16[16,512]{1,0:T(8,128)(2,1)S(1)}, u32[]{:S(2)}, u32[]{:S(2)}) collective-permute-start(bf16[16,512]{1,0:T(8,128)(2,1)S(1)} %whiten.1.refs_0_.refs_5_), channel_id=1, source_target_pairs={{0,8},{1,9},{2,10},{3,11},{4,12},{5,13},{6,14},{7,15},{8,0},{9,1},... | collective-permute-start | bytes 49160 | tf_op jit(solution)/shard_map/ppermute | solution.py:304
  5.6 4.5 %collective-permute-start.1 = (bf16[16,512]{1,0:T(8,128)(2,1)S(1)}, bf16[16,512]{1,0:T(8,128)(2,1)S(1)}, u32[]{:S(2)}, u32[]{:S(2)}) collective-permute-start(bf16[16,512]{1,0:T(8,128)(2,1)S(1)} %whiten.1.refs_0_.refs_5_), channel_id=1, source_target_pairs={{0,24},{1,25},{2,26},{3,27},{4,28},{5,29},{6,30},{7,31},{8,16},{9,... | collective-permute-start | bytes 49160 | tf_op jit(solution)/shard_map/ppermute | solution.py:304
  6.7 4.8 %collective-permute-start.5 = (bf16[32,512]{1,0:T(8,128)(2,1)S(1)}, bf16[32,512]{1,0:T(8,128)(2,1)S(1)}, u32[]{:S(2)}, u32[]{:S(2)}) collective-permute-start(bf16[32,512]{1,0:T(8,128)(2,1)S(1)} %join.1), channel_id=1, source_target_pairs={{0,11},{1,10},{2,9},{3,8},{4,15},{5,14},{6,13},{7,12},{8,3},{9,2},... | collective-permute-start | bytes 98312 | tf_op jit(solution)/shard_map/ppermute | solution.py:304
  9.4 3.3 %collective-permute-start.6 = (bf16[32,512]{1,0:T(8,128)(2,1)S(1)}, bf16[32,512]{1,0:T(8,128)(2,1)S(1)}, u32[]{:S(2)}, u32[]{:S(2)}) collective-permute-start(bf16[32,512]{1,0:T(8,128)(2,1)S(1)} %join.1), channel_id=1, source_target_pairs={{0,10},{1,11},{2,8},{3,9},{4,14},{5,15},{6,12},{7,13},{8,2},{9,3},... | collective-permute-start | bytes 98312 | tf_op jit(solution)/shard_map/ppermute | solution.py:304
  9.6 3.4 %collective-permute-start.7 = (bf16[32,512]{1,0:T(8,128)(2,1)S(1)}, bf16[32,512]{1,0:T(8,128)(2,1)S(1)}, u32[]{:S(2)}, u32[]{:S(2)}) collective-permute-start(bf16[32,512]{1,0:T(8,128)(2,1)S(1)} %join.1), channel_id=1, source_target_pairs={{0,9},{1,8},{2,11},{3,10},{4,13},{5,12},{6,15},{7,14},{8,1},{9,0},... | collective-permute-start | bytes 98312 | tf_op jit(solution)/shard_map/ppermute | solution.py:304
  10.1 1.2 %collective-permute-start.2 = (bf16[16,512]{1,0:T(8,128)(2,1)S(1)}, bf16[16,512]{1,0:T(8,128)(2,1)S(1)}, u32[]{:S(2)}, u32[]{:S(2)}) collective-permute-start(bf16[16,512]{1,0:T(8,128)(2,1)S(1)} %collective-permute-done.1.refs_2_), channel_id=1, source_target_pairs={{0,8},{1,9},{2,10},{3,11},{4,12},{5,13},{6,14},{7,15},{8,0},{9,1},... | collective-permute-start | bytes 49160 | tf_op jit(solution)/shard_map/ppermute | solution.py:304
  10.2 1.4 %collective-permute-start.4 = (bf16[16,512]{1,0:T(8,128)(2,1)S(1)}, bf16[16,512]{1,0:T(8,128)(2,1)S(1)}, u32[]{:S(2)}, u32[]{:S(2)}) collective-permute-start(bf16[16,512]{1,0:T(8,128)(2,1)S(1)} %collective-permute-done.3.own), channel_id=1, source_target_pairs={{0,8},{1,9},{2,10},{3,11},{4,12},{5,13},{6,14},{7,15},{8,0},{9,1},... | collective-permute-start | bytes 49160 | tf_op jit(solution)/shard_map/ppermute | solution.py:304
